TPU v7x, 32 devices: a whole 2x2x4 slice. The times are simulated.
32 devices in a mesh: groups: 2 (over y), dp: 8 (over z, x), fsdp: 2 (over core).
Axes of the slice: x: 2, y: 2, z: 4, core: 2. Of those that a mesh axis runs over, the one named last changes fastest.
Arguments:
- layer_input: bfloat16 [4096, 8192], P(('groups', 'dp'), 'fsdp'), parts along dimension 0, may hold values from -6 to 6
- w_value: bfloat16 [8192, 128], P('fsdp', 'dp'), may hold values from -0.0625 to 0.0625
- queries: bfloat16 [4096, 1024], P(('groups', 'dp'), 'fsdp'), parts along dimension 0, may hold values from -16 to 16
- keys: bfloat16 [4096, 128], P(('groups', 'dp')), parts along dimension 0, may hold values from -16 to 16
- grad_out: bfloat16 [4096, 1024], P(('groups', 'dp'), 'fsdp'), parts along dimension 0, may hold values from -6 to 6
- doc_lengths: int32 [8], P('groups'), parts along dimension 0, may hold values from 1 to 768, 2048 in all
- prefix_spans: int32 [8], P('groups'), parts along dimension 0, may hold values from 1 to 768
Outputs:
- grad_input: bfloat16 [4096, 8192], P(('groups', 'dp'), 'fsdp'), parts along dimension 0
- grad_queries: bfloat16 [4096, 1024], P(('groups', 'dp'), 'fsdp'), parts along dimension 0
- grad_keys: bfloat16 [4096, 128], P(('groups', 'dp')), parts along dimension 0
- grad_weight: float32 [16384, 128], P(('groups', 'fsdp'), 'dp'), parts along dimension 0
There are 2 independent parts, one for each index of `groups`. A program takes and returns all parts, laid end to end along the dimension named above; an argument that names none is the same for every part. Nothing has to cross between parts.
Inputs may be any that keep to these rules, and one draw needn't show every extreme that they name: `doc_lengths`: the lengths sum to 2048 and one of them equals 768.
All inputs are finite; a program needn't handle non-finite values.
Results may differ from a plain program's by a relative error of at most 0.0065.
Values may be sent and summed in bfloat16 or wider, within the bound.
No kernel may reach another device: no remote copies, remote signals or barrier semaphores. Data moves between devices by JAX's collectives and lax.ppermute only.
A program may use at most 128 MiB of HBM per device.

v0:
```python
import math

import jax
import jax.numpy as jnp
from jax import lax
from jax.experimental import pallas as pl
from jax.experimental.pallas import tpu as pltpu
from jax.sharding import PartitionSpec as P

SPAN = 3
NEGATIVE = -1e30
CHUNK = 256
ROWS = 128
BOTH = ("dp", "fsdp")
F32 = jnp.float32
BF16 = jnp.bfloat16
VMEM = pl.BlockSpec(memory_space=pltpu.VMEM)
SMEM = pl.BlockSpec(memory_space=pltpu.SMEM)


def core_swap(value):
    return lax.ppermute(value, "fsdp", [(0, 1), (1, 0)])


def dp_swap(value, mask):
    count = lax.axis_size("dp")
    return lax.ppermute(value, "dp", [(i, i ^ mask) for i in range(count)])


def fan_out(value, distance):
    count = lax.axis_size("dp")
    pairs = [(2 * i, 2 * (i + distance)) for i in range(count - distance)]
    pairs += [(2 * i + 1, 2 * (i - distance) + 1) for i in range(distance, count)]
    return lax.ppermute(value, BOTH, pairs)


def after(value, *others):
    return lax.optimization_barrier((value, *others))[0]


def chunk_range(first, window_first, docs_ref):
    last = first + ROWS - 1
    zero = jnp.int32(0)
    count = docs_ref.shape[0] // 2
    position = first + lax.broadcasted_iota(jnp.int32, (ROWS, 128), 0)
    low, high = jnp.zeros((ROWS, 128), jnp.int32), jnp.zeros((ROWS, 128), jnp.int32)

    def step(doc, carry):
        start, least, most, low, high = carry
        length = docs_ref[doc]
        end = start + length
        bound = start + jnp.minimum(docs_ref[count + doc], length)
        least = jnp.where((start <= first) & (first < end), start, least)
        most = jnp.where((start <= last) & (last < end), jnp.maximum(last + 1, bound), most)
        inside = (position >= start) & (position < end)
        low = jnp.where(inside, start, low)
        high = jnp.where(inside, jnp.maximum(position + 1, bound), high)
        return (end, least, most, low, high)

    carry = (zero, zero, zero, low, high)
    if count <= 8:
        for doc in range(count):
            carry = step(doc, carry)
    else:
        carry = lax.fori_loop(0, count, step, carry)
    _, least, most, low, high = carry
    chunk_low = lax.div(least - window_first, CHUNK)
    chunk_high = lax.div(most - window_first + CHUNK - 1, CHUNK)
    return chunk_low, chunk_high, low, high


def at_block(index, rows):
    return pl.ds(pl.multiple_of(index * rows, rows), rows)


def place_window(core, window_ref, own, mine, other):
    rows = own.shape[0]
    window_ref[SPAN * rows : (SPAN + 1) * rows, :] = own
    side = 2 * core - 1
    for k in range(1, SPAN + 1):
        window_ref[at_block(SPAN + side * k, rows), :] = mine[k - 1]
        window_ref[at_block(SPAN - side * k, rows), :] = other[k - 1]


def give_out(core, total_ref, own_ref, mine_ref, give_ref, factor):
    rows = own_ref.shape[0]
    own_ref[...] = total_ref[SPAN * rows : (SPAN + 1) * rows, :] * factor
    side = 1 - 2 * core
    for k in range(1, SPAN + 1):
        mine_ref[k - 1] = total_ref[at_block(SPAN + side * k, rows), :] * factor
        give_ref[k - 1] = (total_ref[at_block(SPAN - side * k, rows), :] * factor).astype(BF16)


def stack_heads(value, head):
    rows, wide = value.shape
    split = value.reshape(rows // ROWS, ROWS, wide // head, head)
    return split.transpose(0, 2, 1, 3).reshape(rows // ROWS, -1, head)


def nt_dot(a, b):
    return lax.dot_general(a, b, (((1,), (1,)), ((), ())), preferred_element_type=F32)


def tn_dot(a, b):
    return lax.dot_general(a, b, (((0,), (0,)), ((), ())), preferred_element_type=F32)


def weights_kernel(
    docs_ref, queries_ref, grads_ref, key_ref, r1, r2, r3, s1, s2, s3,
    range_ref, probs_ref, scaled_ref, inverse_ref, window_ref, own_ref, mine_ref, give_ref,
    score_ref, peak_ref, sum_ref, total_ref,
):
    rows = key_ref.shape[0]
    heads = peak_ref.shape[0]
    me, core = lax.axis_index("dp"), lax.axis_index("fsdp")
    window_first = (me - SPAN) * rows
    lane = lax.broadcasted_iota(jnp.int32, (ROWS, 128), 1)
    place_window(
        core, window_ref, key_ref[...], (r1[...], r2[...], r3[...]), (s1[...], s2[...], s3[...])
    )
    total_ref[...] = jnp.zeros_like(total_ref)
    power = math.log2(math.e) / math.sqrt(128.0)
    for part in range(rows // ROWS):
        chunk_low, chunk_high, low, high = chunk_range(
            me * rows + part * ROWS, window_first, docs_ref
        )
        range_ref[2 * part] = chunk_low
        range_ref[2 * part + 1] = chunk_high
        low = low - lane - window_first
        high = high - lane - window_first
        peak_ref[...] = jnp.full_like(peak_ref, NEGATIVE)
        sum_ref[...] = jnp.zeros_like(sum_ref)

        def score_step(chunk, _):
            keys = window_ref[pl.ds(pl.multiple_of(chunk * CHUNK, CHUNK), CHUNK), :]
            scores = nt_dot(queries_ref[part], keys).reshape(heads, ROWS, CHUNK)
            peak = peak_ref[...]
            for half in range(CHUNK // 128):
                base = chunk * CHUNK + half * 128
                seen = (low <= base) & (base < high)
                masked = jnp.where(seen[None], scores[:, :, half * 128 : (half + 1) * 128], NEGATIVE)
                score_ref[chunk, :, :, half * 128 : (half + 1) * 128] = masked
                peak = jnp.maximum(peak, masked)
            peak_ref[...] = peak
            return 0

        lax.fori_loop(chunk_low, chunk_high, score_step, 0)
        peak = jnp.max(peak_ref[...], axis=2, keepdims=True)
        peak_ref[...] = jnp.broadcast_to(peak, peak_ref.shape)

        def exp_step(chunk, _):
            total = sum_ref[...]
            peak = peak_ref[...]
            for half in range(CHUNK // 128):
                cut = slice(half * 128, (half + 1) * 128)
                probs = jnp.exp2((score_ref[chunk, :, :, cut] - peak) * power)
                total = total + probs
                probs_ref[part, chunk, :, cut] = probs.reshape(heads * ROWS, 128).astype(BF16)
            sum_ref[...] = total
            return 0

        lax.fori_loop(chunk_low, chunk_high, exp_step, 0)
        inverse = 1.0 / jnp.sum(sum_ref[...], axis=2, keepdims=True)
        inverse_ref[part] = jnp.broadcast_to(inverse, sum_ref.shape).reshape(heads * ROWS, 128)
        scaled_ref[part] = (
            (grads_ref[part].astype(F32).reshape(heads, ROWS, 128) * inverse)
            .reshape(heads * ROWS, 128)
            .astype(BF16)
        )

        def value_step(chunk, _):
            at = pl.ds(pl.multiple_of(chunk * CHUNK, CHUNK), CHUNK)
            total_ref[at, :] += tn_dot(probs_ref[part, chunk], scaled_ref[part])
            return 0

        lax.fori_loop(chunk_low, chunk_high, value_step, 0)
    give_out(core, total_ref, own_ref, mine_ref, give_ref, 1.0)


def scores_kernel(
    range_ref, queries_ref, scaled_ref, inverse_ref, probs_ref, keys_ref, value_ref,
    r1, r2, r3, s1, s2, s3,
    grad_q_ref, own_ref, mine_ref, give_ref,
    values_ref, product_ref, delta_ref, query_ref, total_ref,
):
    rows = value_ref.shape[0]
    heads = grad_q_ref.shape[1] // 128
    core = lax.axis_index("fsdp")
    place_window(core, values_ref, value_ref[...], (r1[0], r2[0], r3[0]), (s1[0], s2[0], s3[0]))
    total_ref[...] = jnp.zeros_like(total_ref)
    scaling = 1.0 / math.sqrt(128.0)
    for part in range(rows // ROWS):
        chunk_low, chunk_high = range_ref[2 * part], range_ref[2 * part + 1]
        delta_ref[...] = jnp.zeros_like(delta_ref)
        query_ref[...] = jnp.zeros_like(query_ref)

        def delta_step(chunk, _):
            at = pl.ds(pl.multiple_of(chunk * CHUNK, CHUNK), CHUNK)
            product = nt_dot(scaled_ref[part], values_ref[at, :])
            product_ref[chunk] = product
            terms = product * probs_ref[part, chunk].astype(F32)
            delta = delta_ref[...]
            for half in range(CHUNK // 128):
                delta = delta + terms[:, half * 128 : (half + 1) * 128]
            delta_ref[...] = delta
            return 0

        lax.fori_loop(chunk_low, chunk_high, delta_step, 0)
        delta = jnp.sum(delta_ref[...], axis=1, keepdims=True)
        delta_ref[...] = delta * inverse_ref[part]

        def grad_step(chunk, _):
            at = pl.ds(pl.multiple_of(chunk * CHUNK, CHUNK), CHUNK)
            probs = probs_ref[part, chunk].astype(F32)
            delta = delta_ref[...]
            product = product_ref[chunk]
            grad = jnp.concatenate(
                [
                    (probs[:, cut] * (product[:, cut] - delta)).astype(BF16)
                    for cut in (slice(i, i + 128) for i in range(0, CHUNK, 128))
                ],
                axis=1,
            )
            query_ref[...] += jnp.dot(grad, keys_ref[at, :], preferred_element_type=F32)
            total_ref[at, :] += tn_dot(grad, queries_ref[part])
            return 0

        lax.fori_loop(chunk_low, chunk_high, grad_step, 0)
        for h in range(heads):
            grad_q_ref[part * ROWS : (part + 1) * ROWS, h * 128 : (h + 1) * 128] = (
                query_ref[h * ROWS : (h + 1) * ROWS, :] * scaling
            ).astype(BF16)
    give_out(core, total_ref, own_ref, mine_ref, give_ref, scaling)


def pack_kernel(half_ref, other_ref, mine_ref, got_ref, value_ref, *outs):
    value = (half_ref[...] + other_ref[...]).astype(BF16)
    value_ref[...] = value
    for k, out in enumerate(outs):
        out[0] = value
        out[1] = (mine_ref[k] + got_ref[k].astype(F32)).astype(BF16)


def sum_blocks(own, other, mine, others):
    total = own + other
    for a, b in zip(mine, others):
        total = total + (a.astype(F32) + b.astype(F32))
    return total


def value_kernel(x_ref, z0, z1, z2, z3, c0, c1, c2, c3, part_ref, weight_ref):
    me = lax.axis_index("dp")
    width = z0.shape[0]
    for k, (near, cross) in enumerate(((z0, c0), (z1, c1), (z2, c2), (z3, c3))):
        owner = me ^ (2 * k)
        weight_ref[pl.ds(pl.multiple_of(owner * width, width), width), :] = near[...]
        there = owner ^ 1
        weight_ref[pl.ds(pl.multiple_of(there * width, width), width), :] = cross[...]
    part_ref[...] = nt_dot(x_ref[...], weight_ref[...])


def weight_grad_kernel(x_ref, a_ref, b_ref, r1, r2, r3, s1, s2, s3, grad_ref, *outs):
    me = lax.axis_index("dp")
    grad = sum_blocks(
        a_ref[...], b_ref[...], (r1[1], r2[1], r3[1]), (s1[1], s2[1], s3[1])
    ).astype(BF16)
    grad_ref[...] = grad
    depth = x_ref.shape[1]
    width = outs[0].shape[0]
    step = 512
    scratch = outs[8]
    for at in range(0, depth, step):
        scratch[:, at : at + step] = tn_dot(grad, x_ref[:, at : at + step])
    for k in range(4):
        owner = me ^ (2 * k)
        outs[k][...] = scratch[pl.ds(pl.multiple_of(owner * width, width), width), :]
        there = owner ^ 1
        rows = scratch[pl.ds(pl.multiple_of(there * width, width), width), :]
        outs[4 + k][...] = rows.astype(BF16)


def call(kernel, outs, scratch, limit_mib, smem, *args):
    return pl.pallas_call(
        kernel,
        in_specs=[SMEM] * smem + [VMEM] * (len(args) - smem),
        out_specs=[SMEM if len(shape) == 1 else VMEM for shape, _ in outs],
        out_shape=[jax.ShapeDtypeStruct(shape, kind) for shape, kind in outs],
        scratch_shapes=scratch,
        compiler_params=pltpu.CompilerParams(vmem_limit_bytes=limit_mib << 20),
        cost_estimate=pl.CostEstimate(flops=1 << 30, bytes_accessed=4 << 20, transcendentals=0),
    )(*args)


def body(layer_input, w_value, queries, keys, grad_out, doc_lengths, prefix_spans):
    rows, depth = layer_input.shape
    head = keys.shape[1]
    heads = queries.shape[1] // head
    dp = lax.axis_size("dp")
    window = (2 * SPAN + 1) * rows
    chunks = window // CHUNK
    parts = rows // ROWS
    stack = heads * ROWS
    weight = w_value.T
    width = weight.shape[0]
    direct = dp == 8
    distances = range(1, SPAN + 1)

    mine = [fan_out(keys, k) for k in distances]
    other = [core_swap(block) for block in mine]
    if direct:
        weight = after(weight, mine[0])
        z3, z2, z1 = (dp_swap(weight, 2 * k) for k in (3, 2, 1))
        cross0 = dp_swap(weight, 1)

    query_stack = stack_heads(queries, head)
    grad_stack = stack_heads(grad_out, head)

    ranges, probs, scaled, inverse, key_window, own_v, mine_v, give_v = call(
        weights_kernel,
        [
            ((2 * parts,), jnp.int32),
            ((parts, chunks, stack, CHUNK), BF16),
            ((parts, stack, head), BF16),
            ((parts, stack, 128), F32),
            ((window, head), BF16),
            ((rows, head), F32),
            ((SPAN, rows, head), F32),
            ((SPAN, rows, head), BF16),
        ],
        [
            pltpu.VMEM((chunks, heads, ROWS, CHUNK), F32),
            pltpu.VMEM((heads, ROWS, 128), F32),
            pltpu.VMEM((heads, ROWS, 128), F32),
            pltpu.VMEM((window, head), F32),
        ],
        20, 1,
        jnp.concatenate([doc_lengths, prefix_spans]), query_stack, grad_stack, keys, *mine, *other,
    )
    got_v = core_swap(give_v)
    other_v = core_swap(own_v)

    if direct:
        cross = [cross0] + [dp_swap(block, 1) for block in (z1, z2, z3)]
        value_part, full_weight = call(
            value_kernel,
            [((rows, head), F32), ((head, depth), BF16)],
            [], 12, 0,
            layer_input, weight, z1, z2, z3, *cross,
        )
    else:
        full_weight = lax.all_gather(weight, "dp", axis=0, tiled=True)
        value_part = nt_dot(layer_input, full_weight)
    value, *packs = call(
        pack_kernel,
        [((rows, head), BF16)] + [((2, rows, head), BF16)] * SPAN,
        [], 8, 0,
        value_part, core_swap(value_part), mine_v, got_v,
    )
    mine = [fan_out(pack, k) for pack, k in zip(packs, distances)]
    other = [core_swap(block) for block in mine]

    if direct:
        grad_value, *blocks = call(
            weight_grad_kernel,
            [((rows, head), BF16)] + [((width, depth), F32)] * 4 + [((width, depth), BF16)] * 4,
            [pltpu.VMEM((head, depth), F32)], 16, 0,
            layer_input, own_v, other_v, *mine, *other,
        )
        keep, send = blocks[:4], blocks[4:]
        total = keep[0]
        for k in (3, 2, 1):
            pair = (keep[k] + dp_swap(send[k], 1).astype(F32)).astype(BF16)
            total = total + dp_swap(pair, 2 * k).astype(F32)
        total = total + dp_swap(send[0], 1).astype(F32)
        grad_weight = total.T
    else:
        grad_value = sum_blocks(
            own_v, other_v, [block[1] for block in mine], [block[1] for block in other]
        ).astype(BF16)
        grad_weight = lax.psum_scatter(
            tn_dot(grad_value, layer_input), "dp", scatter_dimension=0, tiled=True
        ).T
    grad_queries, own_k, mine_k, give_k = call(
        scores_kernel,
        [
            ((rows, heads * head), BF16),
            ((rows, head), F32),
            ((SPAN, rows, head), F32),
            ((SPAN, rows, head), BF16),
        ],
        [
            pltpu.VMEM((window, head), BF16),
            pltpu.VMEM((chunks, stack, CHUNK), F32),
            pltpu.VMEM((stack, 128), F32),
            pltpu.VMEM((stack, head), F32),
            pltpu.VMEM((window, head), F32),
        ],
        20, 1,
        after(ranges, grad_value), query_stack, scaled, inverse, probs, key_window, value, *mine, *other,
    )
    got_k = core_swap(give_k)
    mine = [
        fan_out((mine_k[k - 1] + got_k[k - 1].astype(F32)).astype(BF16), k) for k in distances
    ]
    other = [core_swap(block) for block in mine]
    grad_input = jnp.dot(
        grad_value, full_weight, preferred_element_type=F32
    ).astype(BF16)
    grad_keys = sum_blocks(own_k, core_swap(own_k), mine, other).astype(BF16)
    return (grad_input, grad_queries, grad_keys, grad_weight)


def solution(mesh):
    in_specs = (
        P(("groups", "dp"), "fsdp"),
        P("fsdp", "dp"),
        P(("groups", "dp"), "fsdp"),
        P(("groups", "dp"), None),
        P(("groups", "dp"), "fsdp"),
        P("groups"),
        P("groups"),
    )
    out_specs = (
        P(("groups", "dp"), "fsdp"),
        P(("groups", "dp"), "fsdp"),
        P(("groups", "dp"), None),
        P(("groups", "fsdp"), "dp"),
    )
    return jax.shard_map(body, mesh=mesh, in_specs=in_specs, out_specs=out_specs, check_vma=False)
```

profile of v0, /device:TPU:0, one launch (start us, length us, event | category | flops | bytes accessed | tf_op | source)
XLA Modules:
  0.0 84.8 jit_solution(7560543896137598286)
XLA Ops:
  0.6 5.0 %collective-permute-start = (bf16[256,128]{1,0:T(8,128)(2,1)}, bf16[256,128]{1,0:T(8,128)(2,1)S(1)}, u32[]{:S(2)}, u32[]{:S(2)}) collective-permute-start(bf16[256,128]{1,0:T(8,128)(2,1)} %key_ref.1), channel_id=1, source_target_pairs={{0,2},{2,4},{4,6},{6,8},{8,10},{10,12},{12,14},{3,1},{5,3},{7,5},{... | collective-permute-start | bytes 196616 | tf_op jit(solution)/shard_map/ppermute | solution.py:34
  5.6 3.5 %collective-permute-start.1 = (bf16[256,128]{1,0:T(8,128)(2,1)}, bf16[256,128]{1,0:T(8,128)(2,1)S(1)}, u32[]{:S(2)}, u32[]{:S(2)}) collective-permute-start(bf16[256,128]{1,0:T(8,128)(2,1)} %key_ref.1), channel_id=1, source_target_pairs={{0,4},{2,6},{4,8},{6,10},{8,12},{10,14},{5,1},{7,3},{9,5},{11,7},{... | collective-permute-start | bytes 196616 | tf_op jit(solution)/shard_map/ppermute | solution.py:34
  9.1 4.5 %collective-permute-start.2 = (bf16[256,128]{1,0:T(8,128)(2,1)}, bf16[256,128]{1,0:T(8,128)(2,1)S(1)}, u32[]{:S(2)}, u32[]{:S(2)}) collective-permute-start(bf16[256,128]{1,0:T(8,128)(2,1)} %key_ref.1), channel_id=1, source_target_pairs={{0,6},{2,8},{4,10},{6,12},{8,14},{7,1},{9,3},{11,5},{13,7},{15,9},... | collective-permute-start | bytes 196616 | tf_op jit(solution)/shard_map/ppermute | solution.py:34
  13.8 4.3 %collective-permute-start.9 = (bf16[16,4096]{1,0:T(8,128)(2,1)}, bf16[16,4096]{1,0:T(8,128)(2,1)S(1)}, u32[]{:S(2)}, u32[]{:S(2)}) collective-permute-start(bf16[16,4096]{1,0:T(8,128)(2,1)} %bitcast.22), channel_id=1, source_target_pairs={{0,12},{2,14},{4,8},{6,10},{8,4},{10,6},{12,0},{14,2},{1,13},{3,15... | collective-permute-start | bytes 393224 | tf_op jit(solution)/shard_map/ppermute | solution.py:27
  18.6 0.7 collective-permute-done.3.s1
  19.3 1.5 %collective-permute-start.10 = (bf16[16,4096]{1,0:T(8,128)(2,1)}, bf16[16,4096]{1,0:T(8,128)(2,1)S(1)}, u32[]{:S(2)}, u32[]{:S(2)}) collective-permute-start(bf16[16,4096]{1,0:T(8,128)(2,1)} %bitcast.23), channel_id=1, source_target_pairs={{0,2},{2,0},{4,6},{6,4},{8,10},{10,8},{12,14},{14,12},{1,3},{3,1},... | collective-permute-start | bytes 393224 | tf_op jit(solution)/shard_map/ppermute | solution.py:27
  21.4 2.8 %collective-permute-done.8.z2 = bf16[16,4096]{1,0:T(8,128)(2,1)S(1)} collective-permute-done((bf16[16,4096]{1,0:T(8,128)(2,1)}, bf16[16,4096]{1,0:T(8,128)(2,1)S(1)}, u32[]{:S(2)}, u32[]{:S(2)}) %collective-permute-start.8) | collective-permute-done | bytes 131104 | tf_op jit(solution)/shard_map/ppermute | solution.py:27
  24.2 1.7 %collective-permute-start.12 = (bf16[16,4096]{1,0:T(8,128)(2,1)S(1)}, bf16[16,4096]{1,0:T(8,128)(2,1)S(1)}, u32[]{:S(2)}, u32[]{:S(2)}) collective-permute-start(bf16[16,4096]{1,0:T(8,128)(2,1)S(1)} %collective-permute-done.8.z2), channel_id=1, source_target_pairs={{0,2},{2,0},{4,6},{6,4},{8,10},{10,8},{12,14},{14,12},{1,3},{3,1},... | collective-permute-start | bytes 393224 | tf_op jit(solution)/shard_map/ppermute | solution.py:27
  26.3 0.7 pad_add_fusion.docs_ref
  27.0 1.0 %reshape.29 = bf16[2,128,4,128]{3,2,1,0:T(4,128)(2,1)S(1)} reshape(bf16[256,512]{1,0:T(8,128)(2,1)} %param.9) | data formatting | bytes 524288 | tf_op jit(solution)/shard_map/reshape | solution.py:96
  28.1 1.0 %reshape.31 = bf16[2,128,4,128]{3,2,1,0:T(4,128)(2,1)S(1)} reshape(bf16[256,512]{1,0:T(8,128)(2,1)} %param.11) | data formatting | bytes 524288 | tf_op jit(solution)/shard_map/reshape | solution.py:96
  29.2 3.3 %shard_map.102 = (s32[4]{0:T(128)S(1)}, bf16[2,7,512,256]{3,2,1,0:T(8,128)(2,1)S(1)}, bf16[2,512,128]{2,1,0:T(8,128)(2,1)S(1)}, f32[2,512,128]{2,1,0:T(8,128)S(1...) custom-call(s32[8]{0:T(128)S(1)} %pad_add_fusion.docs_ref, ...), custom_call_target="tpu_custom_call" | custom-call | flops 1073741824 | bytes 4194304 | tf_op jit(solution)/shard_map/pallas_call | solution.py:283
  32.6 0.9 %collective-permute-done.13.c3 = bf16[16,4096]{1,0:T(8,128)(2,1)S(1)} collective-permute-done((bf16[16,4096]{1,0:T(8,128)(2,1)S(1)}, bf16[16,4096]{1,0:T(8,128)(2,1)S(1)}, u32[]{:S(2)}, u32[]{:S(2)}) %collective-permute-start.13) | collective-permute-done | bytes 131104 | tf_op jit(solution)/shard_map/ppermute | solution.py:27
  33.5 0.8 shard_map.103
  34.4 1.3 %collective-permute-done.14.other_ref = f32[256,128]{1,0:T(8,128)S(1)} collective-permute-done((f32[256,128]{1,0:T(8,128)S(1)}, f32[256,128]{1,0:T(8,128)S(1)}, u32[]{:S(2)}, u32[]{:S(2)}) %collective-permute-start.14) | collective-permute-done | bytes 131104 | tf_op jit(solution)/shard_map/ppermute | solution.py:22
  35.8 5.9 %collective-permute-start.16 = (bf16[2,256,128]{2,1,0:T(8,128)(2,1)S(1)}, bf16[2,256,128]{2,1,0:T(8,128)(2,1)S(1)}, u32[]{:S(2)}, u32[]{:S(2)}) collective-permute-start(bf16[2,256,128]{2,1,0:T(8,128)(2,1)S(1)} %get-tuple-element.38), channel_id=1, source_target_pairs={{0,2},{2,4},{4,6},{6,8},{8,10},{10,12},{12,14},{3,1},{5,3},{7,5},{... | collective-permute-start | bytes 393224 | tf_op jit(solution)/shard_map/ppermute | solution.py:34
  41.7 2.3 %collective-permute-start.17 = (bf16[2,256,128]{2,1,0:T(8,128)(2,1)S(1)}, bf16[2,256,128]{2,1,0:T(8,128)(2,1)S(1)}, u32[]{:S(2)}, u32[]{:S(2)}) collective-permute-start(bf16[2,256,128]{2,1,0:T(8,128)(2,1)S(1)} %get-tuple-element.39), channel_id=1, source_target_pairs={{0,4},{2,6},{4,8},{6,10},{8,12},{10,14},{5,1},{7,3},{9,5},{11,7},{... | collective-permute-start | bytes 393224 | tf_op jit(solution)/shard_map/ppermute | solution.py:34
  44.0 3.3 %collective-permute-start.18 = (bf16[2,256,128]{2,1,0:T(8,128)(2,1)S(1)}, bf16[2,256,128]{2,1,0:T(8,128)(2,1)S(1)}, u32[]{:S(2)}, u32[]{:S(2)}) collective-permute-start(bf16[2,256,128]{2,1,0:T(8,128)(2,1)S(1)} %get-tuple-element.40), channel_id=1, source_target_pairs={{0,6},{2,8},{4,10},{6,12},{8,14},{7,1},{9,3},{11,5},{13,7},{15,9},... | collective-permute-start | bytes 393224 | tf_op jit(solution)/shard_map/ppermute | solution.py:34
  48.0 2.2 %collective-permute-done.18.r3 = bf16[2,256,128]{2,1,0:T(8,128)(2,1)S(1)} collective-permute-done((bf16[2,256,128]{2,1,0:T(8,128)(2,1)S(1)}, bf16[2,256,128]{2,1,0:T(8,128)(2,1)S(1)}, u32[]{:S(2)}, u32[]{:S(2)}) %collective-permute-start.18) | collective-permute-done | bytes 131104 | tf_op jit(solution)/shard_map/ppermute | solution.py:34
  50.3 1.3 %collective-permute-done.21.s3 = bf16[2,256,128]{2,1,0:T(8,128)(2,1)S(1)} collective-permute-done((bf16[2,256,128]{2,1,0:T(8,128)(2,1)S(1)}, bf16[2,256,128]{2,1,0:T(8,128)(2,1)S(1)}, u32[]{:S(2)}, u32[]{:S(2)}) %collective-permute-start.21) | collective-permute-done | bytes 131104 | tf_op jit(solution)/shard_map/ppermute | solution.py:22
  51.6 0.6 shard_map.105
  52.2 2.6 %collective-permute-start.30 = (bf16[16,4096]{1,0:T(8,128)(2,1)S(1)}, bf16[16,4096]{1,0:T(8,128)(2,1)S(1)}, u32[]{:S(2)}, u32[]{:S(2)}) collective-permute-start(bf16[16,4096]{1,0:T(8,128)(2,1)S(1)} %get-tuple-element.56), channel_id=1, source_target_pairs={{0,2},{2,0},{4,6},{6,4},{8,10},{10,8},{12,14},{14,12},{1,3},{3,1},... | collective-permute-start | bytes 393224 | tf_op jit(solution)/shard_map/ppermute | solution.py:27
  54.9 1.9 %collective-permute-start.34 = (bf16[16,4096]{1,0:T(8,128)(2,1)S(1)}, bf16[16,4096]{1,0:T(8,128)(2,1)S(1)}, u32[]{:S(2)}, u32[]{:S(2)}) collective-permute-start(bf16[16,4096]{1,0:T(8,128)(2,1)S(1)} %get-tuple-element.60), channel_id=1, source_target_pairs={{0,2},{2,0},{4,6},{6,4},{8,10},{10,8},{12,14},{14,12},{1,3},{3,1},... | collective-permute-start | bytes 393224 | tf_op jit(solution)/shard_map/ppermute | solution.py:27
  57.0 2.9 %shard_map.106 = (bf16[256,512]{1,0:T(8,128)(2,1)}, f32[256,128]{1,0:T(8,128)S(1)}, f32[3,256,128]{2,1,0:T(8,128)S(1)}, bf16[3,256,128]{2,1,0:T(8,128)(2,1)S(1)}) custom-call(s32[4]{0:T(128)S(1)} %get-tuple-element.44.range_ref, bf16[2,512,128]{2,1,0:T(8,128)(2,1)S(1)} %bitcast.18, bf16[2,512,128]{2,1,0:T(8,128)(2,1)S(1)} %get-tuple-element.45.scaled_ref, ...), custom_call_target="tpu_custom_call" | custom-call | flops 1073741824 | bytes 4194304 | tf_op jit(solution)/shard_map/pallas_call | solution.py:283
  59.9 4.5 %collective-permute-start.31 = (bf16[16,4096]{1,0:T(8,128)(2,1)S(1)}, bf16[16,4096]{1,0:T(8,128)(2,1)S(1)}, u32[]{:S(2)}, u32[]{:S(2)}) collective-permute-start(bf16[16,4096]{1,0:T(8,128)(2,1)S(1)} %add_convert_fusion.2), channel_id=1, source_target_pairs={{0,12},{2,14},{4,8},{6,10},{8,4},{10,6},{12,0},{14,2},{1,13},{3,15... | collective-permute-start | bytes 393224 | tf_op jit(solution)/shard_map/ppermute | solution.py:27
  64.5 2.1 %collective-permute-start.33 = (bf16[16,4096]{1,0:T(8,128)(2,1)S(1)}, bf16[16,4096]{1,0:T(8,128)(2,1)S(1)}, u32[]{:S(2)}, u32[]{:S(2)}) collective-permute-start(bf16[16,4096]{1,0:T(8,128)(2,1)S(1)} %add_convert_fusion.1), channel_id=1, source_target_pairs={{0,8},{2,10},{4,12},{6,14},{8,0},{10,2},{12,4},{14,6},{1,9},{3,11}... | collective-permute-start | bytes 393224 | tf_op jit(solution)/shard_map/ppermute | solution.py:27
  67.0 4.4 %collective-permute-start.24 = (bf16[256,128]{1,0:T(8,128)(2,1)S(1)}, bf16[256,128]{1,0:T(8,128)(2,1)S(1)}, u32[]{:S(2)}, u32[]{:S(2)}) collective-permute-start(bf16[256,128]{1,0:T(8,128)(2,1)S(1)} %get-tuple-element.62), channel_id=1, source_target_pairs={{0,2},{2,4},{4,6},{6,8},{8,10},{10,12},{12,14},{3,1},{5,3},{7,5},{... | collective-permute-start | bytes 196616 | tf_op jit(solution)/shard_map/ppermute | solution.py:34
  71.4 3.1 %collective-permute-start.26 = (bf16[256,128]{1,0:T(8,128)(2,1)S(1)}, bf16[256,128]{1,0:T(8,128)(2,1)S(1)}, u32[]{:S(2)}, u32[]{:S(2)}) collective-permute-start(bf16[256,128]{1,0:T(8,128)(2,1)S(1)} %get-tuple-element.64), channel_id=1, source_target_pairs={{0,4},{2,6},{4,8},{6,10},{8,12},{10,14},{5,1},{7,3},{9,5},{11,7},{... | collective-permute-start | bytes 196616 | tf_op jit(solution)/shard_map/ppermute | solution.py:34
  74.5 5.6 %collective-permute-start.28 = (bf16[256,128]{1,0:T(8,128)(2,1)S(1)}, bf16[256,128]{1,0:T(8,128)(2,1)S(1)}, u32[]{:S(2)}, u32[]{:S(2)}) collective-permute-start(bf16[256,128]{1,0:T(8,128)(2,1)S(1)} %get-tuple-element.63), channel_id=1, source_target_pairs={{0,6},{2,8},{4,10},{6,12},{8,14},{7,1},{9,3},{11,5},{13,7},{15,9},... | collective-permute-start | bytes 196616 | tf_op jit(solution)/shard_map/ppermute | solution.py:34
  80.1 2.0 %convolution_convert_fusion = bf16[256,4096]{1,0:T(8,128)(2,1)} fusion(bf16[256,128]{1,0:T(8,128)(2,1)S(1)} %get-tuple-element.41, bf16[128,4096]{1,0:T(8,128)(2,1)S(1)} %get-tuple-element.42), kind=kOutput, calls=%fused_computation | convolution fusion | flops 269484032 | bytes 3211264 | tf_op jit(solution)/shard_map/dot_general | solution.py:406
  83.2 0.8 add_bitcast_fusion
  84.1 0.7 add_convert_fusion.3
  (65 shorter events, 4.4 us)
Async XLA Ops:
  0.6 13.0 %collective-permute-start = (bf16[256,128]{1,0:T(8,128)(2,1)}, bf16[256,128]{1,0:T(8,128)(2,1)S(1)}, u32[]{:S(2)}, u32[]{:S(2)}) collective-permute-start(bf16[256,128]{1,0:T(8,128)(2,1)} %key_ref.1), channel_id=1, source_target_pairs={{0,2},{2,4},{4,6},{6,8},{8,10},{10,12},{12,14},{3,1},{5,3},{7,5},{... | collective-permute-start | bytes 196616 | tf_op jit(solution)/shard_map/ppermute | solution.py:34
  5.6 12.4 %collective-permute-start.1 = (bf16[256,128]{1,0:T(8,128)(2,1)}, bf16[256,128]{1,0:T(8,128)(2,1)S(1)}, u32[]{:S(2)}, u32[]{:S(2)}) collective-permute-start(bf16[256,128]{1,0:T(8,128)(2,1)} %key_ref.1), channel_id=1, source_target_pairs={{0,4},{2,6},{4,8},{6,10},{8,12},{10,14},{5,1},{7,3},{9,5},{11,7},{... | collective-permute-start | bytes 196616 | tf_op jit(solution)/shard_map/ppermute | solution.py:34
  9.1 8.9 %collective-permute-start.2 = (bf16[256,128]{1,0:T(8,128)(2,1)}, bf16[256,128]{1,0:T(8,128)(2,1)S(1)}, u32[]{:S(2)}, u32[]{:S(2)}) collective-permute-start(bf16[256,128]{1,0:T(8,128)(2,1)} %key_ref.1), channel_id=1, source_target_pairs={{0,6},{2,8},{4,10},{6,12},{8,14},{7,1},{9,3},{11,5},{13,7},{15,9},... | collective-permute-start | bytes 196616 | tf_op jit(solution)/shard_map/ppermute | solution.py:34
  13.6 7.2 %collective-permute-start.7 = (bf16[16,4096]{1,0:T(8,128)(2,1)}, bf16[16,4096]{1,0:T(8,128)(2,1)S(1)}, u32[]{:S(2)}, u32[]{:S(2)}) collective-permute-start(bf16[16,4096]{1,0:T(8,128)(2,1)} %bitcast.20), channel_id=1, source_target_pairs={{0,4},{2,6},{4,0},{6,2},{8,12},{10,14},{12,8},{14,10},{1,5},{3,7},... | collective-permute-start | bytes 393224 | tf_op jit(solution)/shard_map/ppermute | solution.py:27
  13.7 10.5 %collective-permute-start.8 = (bf16[16,4096]{1,0:T(8,128)(2,1)}, bf16[16,4096]{1,0:T(8,128)(2,1)S(1)}, u32[]{:S(2)}, u32[]{:S(2)}) collective-permute-start(bf16[16,4096]{1,0:T(8,128)(2,1)} %bitcast.21), channel_id=1, source_target_pairs={{0,8},{2,10},{4,12},{6,14},{8,0},{10,2},{12,4},{14,6},{1,9},{3,11}... | collective-permute-start | bytes 393224 | tf_op jit(solution)/shard_map/ppermute | solution.py:27
  13.8 12.1 %collective-permute-start.9 = (bf16[16,4096]{1,0:T(8,128)(2,1)}, bf16[16,4096]{1,0:T(8,128)(2,1)S(1)}, u32[]{:S(2)}, u32[]{:S(2)}) collective-permute-start(bf16[16,4096]{1,0:T(8,128)(2,1)} %bitcast.22), channel_id=1, source_target_pairs={{0,12},{2,14},{4,8},{6,10},{8,4},{10,6},{12,0},{14,2},{1,13},{3,15... | collective-permute-start | bytes 393224 | tf_op jit(solution)/shard_map/ppermute | solution.py:27
  18.1 2.7 %collective-permute-start.4 = (bf16[256,128]{1,0:T(8,128)(2,1)S(1)}, bf16[256,128]{1,0:T(8,128)(2,1)S(1)}, u32[]{:S(2)}, u32[]{:S(2)}) collective-permute-start(bf16[256,128]{1,0:T(8,128)(2,1)S(1)} %collective-permute-done.1.r2), channel_id=1, source_target_pairs={{0,1},{1,0},{2,3},{3,2},{4,5},{5,4},{6,7},{7,6},{8,9},{9,8},{10,11... | collective-permute-start | bytes 196616 | tf_op jit(solution)/shard_map/ppermute | solution.py:22
  19.3 13.2 %collective-permute-start.10 = (bf16[16,4096]{1,0:T(8,128)(2,1)}, bf16[16,4096]{1,0:T(8,128)(2,1)S(1)}, u32[]{:S(2)}, u32[]{:S(2)}) collective-permute-start(bf16[16,4096]{1,0:T(8,128)(2,1)} %bitcast.23), channel_id=1, source_target_pairs={{0,2},{2,0},{4,6},{6,4},{8,10},{10,8},{12,14},{14,12},{1,3},{3,1},... | collective-permute-start | bytes 393224 | tf_op jit(solution)/shard_map/ppermute | solution.py:27
  20.8 8.3 %collective-permute-start.5 = (bf16[256,128]{1,0:T(8,128)(2,1)S(1)}, bf16[256,128]{1,0:T(8,128)(2,1)S(1)}, u32[]{:S(2)}, u32[]{:S(2)}) collective-permute-start(bf16[256,128]{1,0:T(8,128)(2,1)S(1)} %collective-permute-done.2.r3), channel_id=1, source_target_pairs={{0,1},{1,0},{2,3},{3,2},{4,5},{5,4},{6,7},{7,6},{8,9},{9,8},{10,11... | collective-permute-start | bytes 196616 | tf_op jit(solution)/shard_map/ppermute | solution.py:22
  20.8 11.7 %collective-permute-start.11 = (bf16[16,4096]{1,0:T(8,128)(2,1)S(1)}, bf16[16,4096]{1,0:T(8,128)(2,1)S(1)}, u32[]{:S(2)}, u32[]{:S(2)}) collective-permute-start(bf16[16,4096]{1,0:T(8,128)(2,1)S(1)} %collective-permute-done.7.z1), channel_id=1, source_target_pairs={{0,2},{2,0},{4,6},{6,4},{8,10},{10,8},{12,14},{14,12},{1,3},{3,1},... | collective-permute-start | bytes 393224 | tf_op jit(solution)/shard_map/ppermute | solution.py:27
  24.2 8.3 %collective-permute-start.12 = (bf16[16,4096]{1,0:T(8,128)(2,1)S(1)}, bf16[16,4096]{1,0:T(8,128)(2,1)S(1)}, u32[]{:S(2)}, u32[]{:S(2)}) collective-permute-start(bf16[16,4096]{1,0:T(8,128)(2,1)S(1)} %collective-permute-done.8.z2), channel_id=1, source_target_pairs={{0,2},{2,0},{4,6},{6,4},{8,10},{10,8},{12,14},{14,12},{1,3},{3,1},... | collective-permute-start | bytes 393224 | tf_op jit(solution)/shard_map/ppermute | solution.py:27
  25.9 7.6 %collective-permute-start.13 = (bf16[16,4096]{1,0:T(8,128)(2,1)S(1)}, bf16[16,4096]{1,0:T(8,128)(2,1)S(1)}, u32[]{:S(2)}, u32[]{:S(2)}) collective-permute-start(bf16[16,4096]{1,0:T(8,128)(2,1)S(1)} %collective-permute-done.9.z3), channel_id=1, source_target_pairs={{0,2},{2,0},{4,6},{6,4},{8,10},{10,8},{12,14},{14,12},{1,3},{3,1},... | collective-permute-start | bytes 393224 | tf_op jit(solution)/shard_map/ppermute | solution.py:27
  32.5 1.9 %collective-permute-start.15 = (bf16[3,256,128]{2,1,0:T(8,128)(2,1)S(1)}, bf16[3,256,128]{2,1,0:T(8,128)(2,1)S(1)}, u32[]{:S(2)}, u32[]{:S(2)}) collective-permute-start(bf16[3,256,128]{2,1,0:T(8,128)(2,1)S(1)} %get-tuple-element.37), channel_id=1, source_target_pairs={{0,1},{1,0},{2,3},{3,2},{4,5},{5,4},{6,7},{7,6},{8,9},{9,8},{10,11... | collective-permute-start | bytes 589832 | tf_op jit(solution)/shard_map/ppermute | solution.py:22
  35.8 11.6 %collective-permute-start.16 = (bf16[2,256,128]{2,1,0:T(8,128)(2,1)S(1)}, bf16[2,256,128]{2,1,0:T(8,128)(2,1)S(1)}, u32[]{:S(2)}, u32[]{:S(2)}) collective-permute-start(bf16[2,256,128]{2,1,0:T(8,128)(2,1)S(1)} %get-tuple-element.38), channel_id=1, source_target_pairs={{0,2},{2,4},{4,6},{6,8},{8,10},{10,12},{12,14},{3,1},{5,3},{7,5},{... | collective-permute-start | bytes 393224 | tf_op jit(solution)/shard_map/ppermute | solution.py:34
  41.7 6.2 %collective-permute-start.17 = (bf16[2,256,128]{2,1,0:T(8,128)(2,1)S(1)}, bf16[2,256,128]{2,1,0:T(8,128)(2,1)S(1)}, u32[]{:S(2)}, u32[]{:S(2)}) collective-permute-start(bf16[2,256,128]{2,1,0:T(8,128)(2,1)S(1)} %get-tuple-element.39), channel_id=1, source_target_pairs={{0,4},{2,6},{4,8},{6,10},{8,12},{10,14},{5,1},{7,3},{9,5},{11,7},{... | collective-permute-start | bytes 393224 | tf_op jit(solution)/shard_map/ppermute | solution.py:34
  44.0 6.2 %collective-permute-start.18 = (bf16[2,256,128]{2,1,0:T(8,128)(2,1)S(1)}, bf16[2,256,128]{2,1,0:T(8,128)(2,1)S(1)}, u32[]{:S(2)}, u32[]{:S(2)}) collective-permute-start(bf16[2,256,128]{2,1,0:T(8,128)(2,1)S(1)} %get-tuple-element.40), channel_id=1, source_target_pairs={{0,6},{2,8},{4,10},{6,12},{8,14},{7,1},{9,3},{11,5},{13,7},{15,9},... | collective-permute-start | bytes 393224 | tf_op jit(solution)/shard_map/ppermute | solution.py:34
  47.3 2.9 %collective-permute-start.6 = (f32[256,128]{1,0:T(8,128)S(1)}, f32[256,128]{1,0:T(8,128)S(1)}, u32[]{:S(2)}, u32[]{:S(2)}) collective-permute-start(f32[256,128]{1,0:T(8,128)S(1)} %get-tuple-element.33.a_ref), channel_id=1, source_target_pairs={{0,1},{1,0},{2,3},{3,2},{4,5},{5,4},{6,7},{7,6},{8,9},{9,8},{10,11... | collective-permute-start | bytes 393224 | tf_op jit(solution)/shard_map/ppermute | solution.py:22
  47.4 2.8 %collective-permute-start.19 = (bf16[2,256,128]{2,1,0:T(8,128)(2,1)S(1)}, bf16[2,256,128]{2,1,0:T(8,128)(2,1)S(1)}, u32[]{:S(2)}, u32[]{:S(2)}) collective-permute-start(bf16[2,256,128]{2,1,0:T(8,128)(2,1)S(1)} %collective-permute-done.16.r1), channel_id=1, source_target_pairs={{0,1},{1,0},{2,3},{3,2},{4,5},{5,4},{6,7},{7,6},{8,9},{9,8},{10,11... | collective-permute-start | bytes 393224 | tf_op jit(solution)/shard_map/ppermute | solution.py:22
  47.9 2.3 %collective-permute-start.20 = (bf16[2,256,128]{2,1,0:T(8,128)(2,1)S(1)}, bf16[2,256,128]{2,1,0:T(8,128)(2,1)S(1)}, u32[]{:S(2)}, u32[]{:S(2)}) collective-permute-start(bf16[2,256,128]{2,1,0:T(8,128)(2,1)S(1)} %collective-permute-done.17.r2), channel_id=1, source_target_pairs={{0,1},{1,0},{2,3},{3,2},{4,5},{5,4},{6,7},{7,6},{8,9},{9,8},{10,11... | collective-permute-start | bytes 393224 | tf_op jit(solution)/shard_map/ppermute | solution.py:22
  52.2 7.7 %collective-permute-start.30 = (bf16[16,4096]{1,0:T(8,128)(2,1)S(1)}, bf16[16,4096]{1,0:T(8,128)(2,1)S(1)}, u32[]{:S(2)}, u32[]{:S(2)}) collective-permute-start(bf16[16,4096]{1,0:T(8,128)(2,1)S(1)} %get-tuple-element.56), channel_id=1, source_target_pairs={{0,2},{2,0},{4,6},{6,4},{8,10},{10,8},{12,14},{14,12},{1,3},{3,1},... | collective-permute-start | bytes 393224 | tf_op jit(solution)/shard_map/ppermute | solution.py:27
  54.9 9.6 %collective-permute-start.32 = (bf16[16,4096]{1,0:T(8,128)(2,1)S(1)}, bf16[16,4096]{1,0:T(8,128)(2,1)S(1)}, u32[]{:S(2)}, u32[]{:S(2)}) collective-permute-start(bf16[16,4096]{1,0:T(8,128)(2,1)S(1)} %get-tuple-element.58), channel_id=1, source_target_pairs={{0,2},{2,0},{4,6},{6,4},{8,10},{10,8},{12,14},{14,12},{1,3},{3,1},... | collective-permute-start | bytes 393224 | tf_op jit(solution)/shard_map/ppermute | solution.py:27
  54.9 11.7 %collective-permute-start.34 = (bf16[16,4096]{1,0:T(8,128)(2,1)S(1)}, bf16[16,4096]{1,0:T(8,128)(2,1)S(1)}, u32[]{:S(2)}, u32[]{:S(2)}) collective-permute-start(bf16[16,4096]{1,0:T(8,128)(2,1)S(1)} %get-tuple-element.60), channel_id=1, source_target_pairs={{0,2},{2,0},{4,6},{6,4},{8,10},{10,8},{12,14},{14,12},{1,3},{3,1},... | collective-permute-start | bytes 393224 | tf_op jit(solution)/shard_map/ppermute | solution.py:27
  56.9 14.5 %collective-permute-start.36 = (bf16[16,4096]{1,0:T(8,128)(2,1)S(1)}, bf16[16,4096]{1,0:T(8,128)(2,1)S(1)}, u32[]{:S(2)}, u32[]{:S(2)}) collective-permute-start(bf16[16,4096]{1,0:T(8,128)(2,1)S(1)} %get-tuple-element.61), channel_id=1, source_target_pairs={{0,2},{2,0},{4,6},{6,4},{8,10},{10,8},{12,14},{14,12},{1,3},{3,1},... | collective-permute-start | bytes 393224 | tf_op jit(solution)/shard_map/ppermute | solution.py:27
  59.9 7.1 %collective-permute-start.23 = (bf16[3,256,128]{2,1,0:T(8,128)(2,1)S(1)}, bf16[3,256,128]{2,1,0:T(8,128)(2,1)S(1)}, u32[]{:S(2)}, u32[]{:S(2)}) collective-permute-start(bf16[3,256,128]{2,1,0:T(8,128)(2,1)S(1)} %get-tuple-element.53), channel_id=1, source_target_pairs={{0,1},{1,0},{2,3},{3,2},{4,5},{5,4},{6,7},{7,6},{8,9},{9,8},{10,11... | collective-permute-start | bytes 589832 | tf_op jit(solution)/shard_map/ppermute | solution.py:22
  59.9 14.6 %collective-permute-start.31 = (bf16[16,4096]{1,0:T(8,128)(2,1)S(1)}, bf16[16,4096]{1,0:T(8,128)(2,1)S(1)}, u32[]{:S(2)}, u32[]{:S(2)}) collective-permute-start(bf16[16,4096]{1,0:T(8,128)(2,1)S(1)} %add_convert_fusion.2), channel_id=1, source_target_pairs={{0,12},{2,14},{4,8},{6,10},{8,4},{10,6},{12,0},{14,2},{1,13},{3,15... | collective-permute-start | bytes 393224 | tf_op jit(solution)/shard_map/ppermute | solution.py:27
  64.5 17.6 %collective-permute-start.33 = (bf16[16,4096]{1,0:T(8,128)(2,1)S(1)}, bf16[16,4096]{1,0:T(8,128)(2,1)S(1)}, u32[]{:S(2)}, u32[]{:S(2)}) collective-permute-start(bf16[16,4096]{1,0:T(8,128)(2,1)S(1)} %add_convert_fusion.1), channel_id=1, source_target_pairs={{0,8},{2,10},{4,12},{6,14},{8,0},{10,2},{12,4},{14,6},{1,9},{3,11}... | collective-permute-start | bytes 393224 | tf_op jit(solution)/shard_map/ppermute | solution.py:27
  66.7 16.5 %collective-permute-start.35 = (bf16[16,4096]{1,0:T(8,128)(2,1)S(1)}, bf16[16,4096]{1,0:T(8,128)(2,1)S(1)}, u32[]{:S(2)}, u32[]{:S(2)}) collective-permute-start(bf16[16,4096]{1,0:T(8,128)(2,1)S(1)} %add_convert_fusion), channel_id=1, source_target_pairs={{0,4},{2,6},{4,0},{6,2},{8,12},{10,14},{12,8},{14,10},{1,5},{3,7},... | collective-permute-start | bytes 393224 | tf_op jit(solution)/shard_map/ppermute | solution.py:27
  67.0 15.1 %collective-permute-start.24 = (bf16[256,128]{1,0:T(8,128)(2,1)S(1)}, bf16[256,128]{1,0:T(8,128)(2,1)S(1)}, u32[]{:S(2)}, u32[]{:S(2)}) collective-permute-start(bf16[256,128]{1,0:T(8,128)(2,1)S(1)} %get-tuple-element.62), channel_id=1, source_target_pairs={{0,2},{2,4},{4,6},{6,8},{8,10},{10,12},{12,14},{3,1},{5,3},{7,5},{... | collective-permute-start | bytes 196616 | tf_op jit(solution)/shard_map/ppermute | solution.py:34
  71.4 11.2 %collective-permute-start.26 = (bf16[256,128]{1,0:T(8,128)(2,1)S(1)}, bf16[256,128]{1,0:T(8,128)(2,1)S(1)}, u32[]{:S(2)}, u32[]{:S(2)}) collective-permute-start(bf16[256,128]{1,0:T(8,128)(2,1)S(1)} %get-tuple-element.64), channel_id=1, source_target_pairs={{0,4},{2,6},{4,8},{6,10},{8,12},{10,14},{5,1},{7,3},{9,5},{11,7},{... | collective-permute-start | bytes 196616 | tf_op jit(solution)/shard_map/ppermute | solution.py:34
  74.5 8.2 %collective-permute-start.28 = (bf16[256,128]{1,0:T(8,128)(2,1)S(1)}, bf16[256,128]{1,0:T(8,128)(2,1)S(1)}, u32[]{:S(2)}, u32[]{:S(2)}) collective-permute-start(bf16[256,128]{1,0:T(8,128)(2,1)S(1)} %get-tuple-element.63), channel_id=1, source_target_pairs={{0,6},{2,8},{4,10},{6,12},{8,14},{7,1},{9,3},{11,5},{13,7},{15,9},... | collective-permute-start | bytes 196616 | tf_op jit(solution)/shard_map/ppermute | solution.py:34
  82.1 1.8 %collective-permute-start.22 = (f32[256,128]{1,0:T(8,128)S(1)}, f32[256,128]{1,0:T(8,128)S(1)}, u32[]{:S(2)}, u32[]{:S(2)}) collective-permute-start(f32[256,128]{1,0:T(8,128)S(1)} %get-tuple-element.51), channel_id=1, source_target_pairs={{0,1},{1,0},{2,3},{3,2},{4,5},{5,4},{6,7},{7,6},{8,9},{9,8},{10,11... | collective-permute-start | bytes 393224 | tf_op jit(solution)/shard_map/ppermute | solution.py:22
  82.1 1.8 %collective-permute-start.25 = (bf16[256,128]{1,0:T(8,128)(2,1)S(1)}, bf16[256,128]{1,0:T(8,128)(2,1)S(1)}, u32[]{:S(2)}, u32[]{:S(2)}) collective-permute-start(bf16[256,128]{1,0:T(8,128)(2,1)S(1)} %collective-permute-done.24), channel_id=1, source_target_pairs={{0,1},{1,0},{2,3},{3,2},{4,5},{5,4},{6,7},{7,6},{8,9},{9,8},{10,11... | collective-permute-start | bytes 196616 | tf_op jit(solution)/shard_map/ppermute | solution.py:22
  (8 other events, 44.0 us)
where the time goes:
time: 86.3 us; the launch traced here: 84.8 us
  starting transfers between devices  60.1 us (70%)
  waiting for transfers between devices  9.55 us (11%)
  Pallas kernels  7.67 us (9%)
  other arithmetic  2.37 us (3%)
  local copies, waits for them, and re-layouts  2.12 us (2%)
  matrix products  2.02 us (2%)
  between operations  0.95 us (1%)
    ppermute x9, starting transfers between devices, fan_out(): return lax.ppermute(value, BOTH, pairs)  37.5 us
    ppermute x14, starting transfers between devices, dp_swap(): return lax.ppermute(value, 'dp', [(i, i ^ mask) for i in range(count)])  20.3 us
    pallas_call x5, Pallas kernels, call(): pl.pallas_call(kernel, in_specs=[SMEM] * smem + [VMEM] * (len(args) - sme...  7.67 us
    ppermute x14, waiting for transfers between devices, dp_swap(): return lax.ppermute(value, 'dp', [(i, i ^ mask) for i in range(count)])  3.78 us
    ppermute x14, waiting for transfers between devices, core_swap(): return lax.ppermute(value, 'fsdp', [(0, 1), (1, 0)])  3.52 us
    ppermute x14, starting transfers between devices, core_swap(): return lax.ppermute(value, 'fsdp', [(0, 1), (1, 0)])  2.32 us
    ppermute x9, waiting for transfers between devices, fan_out(): return lax.ppermute(value, BOTH, pairs)  2.26 us
    reshape x4, local copies, waits for them, and re-layouts, stack_heads(): split = value.reshape(rows // ROWS, ROWS, wide // head, head)  2.1 us
  transfers between devices with their start and end apart: 37, of which 7 were waited for; matrix products, arithmetic and copies ran while one was open for 7% of the time, Pallas kernels for 8%

commit v1 on v0

--- a/solution.py
+++ b/solution.py
@@ -27,11 +27,22 @@
     return lax.ppermute(value, "dp", [(i, i ^ mask) for i in range(count)])
 
 
-def fan_out(value, distance):
+def reach(step, core, odd):
+    turn = 1 - 2 * odd
+    return ((-3 * turn, turn - 2), (-2, turn + 2), (2, turn))[step][core]
+
+
+def offset(step, core, odd, sign):
+    turn = 1 - 2 * odd
+    near = ((0, -2), (-2, 2), (2, 0))[step]
+    first = -3 * turn if step == 0 else sign * near[0]
+    return jnp.where(core == 0, first, sign * near[1] + turn)
+
+
+def fan_out(value, step):
     count = lax.axis_size("dp")
-    pairs = [(2 * i, 2 * (i + distance)) for i in range(count - distance)]
-    pairs += [(2 * i + 1, 2 * (i - distance) + 1) for i in range(distance, count)]
-    return lax.ppermute(value, BOTH, pairs)
+    pairs = [(2 * i + c, 2 * (i + reach(step, c, i % 2)) + c) for i in range(count) for c in (0, 1)]
+    return lax.ppermute(value, BOTH, [(i, j) for i, j in pairs if 0 <= j < 2 * count])
 
 
 def after(value, *others):
@@ -42,8 +53,8 @@
     last = first + ROWS - 1
     zero = jnp.int32(0)
     count = docs_ref.shape[0] // 2
-    position = first + lax.broadcasted_iota(jnp.int32, (ROWS, 128), 0)
-    low, high = jnp.zeros((ROWS, 128), jnp.int32), jnp.zeros((ROWS, 128), jnp.int32)
+    position = first + lax.broadcasted_iota(jnp.int32, (1, ROWS), 1)
+    low, high = jnp.zeros((1, ROWS), jnp.int32), jnp.zeros((1, ROWS), jnp.int32)
 
     def step(doc, carry):
         start, least, most, low, high = carry
@@ -75,20 +86,21 @@
 
 def place_window(core, window_ref, own, mine, other):
     rows = own.shape[0]
+    odd = lax.rem(lax.axis_index("dp"), 2)
     window_ref[SPAN * rows : (SPAN + 1) * rows, :] = own
-    side = 2 * core - 1
-    for k in range(1, SPAN + 1):
-        window_ref[at_block(SPAN + side * k, rows), :] = mine[k - 1]
-        window_ref[at_block(SPAN - side * k, rows), :] = other[k - 1]
+    for k in range(SPAN):
+        window_ref[at_block(SPAN + offset(k, core, odd, -1), rows), :] = mine[k]
+        window_ref[at_block(SPAN + offset(k, 1 - core, odd, -1), rows), :] = other[k]
 
 
 def give_out(core, total_ref, own_ref, mine_ref, give_ref, factor):
     rows = own_ref.shape[0]
+    odd = lax.rem(lax.axis_index("dp"), 2)
     own_ref[...] = total_ref[SPAN * rows : (SPAN + 1) * rows, :] * factor
-    side = 1 - 2 * core
-    for k in range(1, SPAN + 1):
-        mine_ref[k - 1] = total_ref[at_block(SPAN + side * k, rows), :] * factor
-        give_ref[k - 1] = (total_ref[at_block(SPAN - side * k, rows), :] * factor).astype(BF16)
+    for k in range(SPAN):
+        mine_ref[k] = total_ref[at_block(SPAN + offset(k, core, odd, 1), rows), :] * factor
+        there = total_ref[at_block(SPAN + offset(k, 1 - core, odd, 1), rows), :] * factor
+        give_ref[k] = there.astype(BF16)
 
 
 def stack_heads(value, head):
@@ -105,72 +117,66 @@
     return lax.dot_general(a, b, (((0,), (0,)), ((), ())), preferred_element_type=F32)
 
 
+def fold(total, value, reduce):
+    rows, lanes = value.shape
+    return reduce(jnp.concatenate([total[None], value.reshape(rows // 8, 8, lanes)]), axis=0)
+
+
 def weights_kernel(
     docs_ref, queries_ref, grads_ref, key_ref, r1, r2, r3, s1, s2, s3,
-    range_ref, probs_ref, scaled_ref, inverse_ref, window_ref, own_ref, mine_ref, give_ref,
+    range_ref, probs_ref, window_ref, own_ref, mine_ref, give_ref,
     score_ref, peak_ref, sum_ref, total_ref,
 ):
     rows = key_ref.shape[0]
-    heads = peak_ref.shape[0]
+    stack = queries_ref.shape[1]
     me, core = lax.axis_index("dp"), lax.axis_index("fsdp")
     window_first = (me - SPAN) * rows
-    lane = lax.broadcasted_iota(jnp.int32, (ROWS, 128), 1)
     place_window(
         core, window_ref, key_ref[...], (r1[...], r2[...], r3[...]), (s1[...], s2[...], s3[...])
     )
     total_ref[...] = jnp.zeros_like(total_ref)
     power = math.log2(math.e) / math.sqrt(128.0)
+    index = lax.broadcasted_iota(jnp.int32, (CHUNK, ROWS), 0)
     for part in range(rows // ROWS):
         chunk_low, chunk_high, low, high = chunk_range(
             me * rows + part * ROWS, window_first, docs_ref
         )
         range_ref[2 * part] = chunk_low
         range_ref[2 * part + 1] = chunk_high
-        low = low - lane - window_first
-        high = high - lane - window_first
+        low = low - window_first
+        high = high - window_first
         peak_ref[...] = jnp.full_like(peak_ref, NEGATIVE)
         sum_ref[...] = jnp.zeros_like(sum_ref)
 
         def score_step(chunk, _):
-            keys = window_ref[pl.ds(pl.multiple_of(chunk * CHUNK, CHUNK), CHUNK), :]
-            scores = nt_dot(queries_ref[part], keys).reshape(heads, ROWS, CHUNK)
-            peak = peak_ref[...]
-            for half in range(CHUNK // 128):
-                base = chunk * CHUNK + half * 128
-                seen = (low <= base) & (base < high)
-                masked = jnp.where(seen[None], scores[:, :, half * 128 : (half + 1) * 128], NEGATIVE)
-                score_ref[chunk, :, :, half * 128 : (half + 1) * 128] = masked
-                peak = jnp.maximum(peak, masked)
-            peak_ref[...] = peak
+            keys = window_ref[at_block(chunk, CHUNK), :]
+            scores = nt_dot(keys, queries_ref[part])
+            place = index + chunk * CHUNK
+            seen = (place >= low) & (place < high)
+            for h in range(0, stack, ROWS):
+                masked = jnp.where(seen, scores[:, h : h + ROWS], NEGATIVE)
+                score_ref[chunk, :, h : h + ROWS] = masked
+                peak_ref[:, h : h + ROWS] = fold(peak_ref[:, h : h + ROWS], masked, jnp.max)
             return 0
 
         lax.fori_loop(chunk_low, chunk_high, score_step, 0)
-        peak = jnp.max(peak_ref[...], axis=2, keepdims=True)
-        peak_ref[...] = jnp.broadcast_to(peak, peak_ref.shape)
+        peak = jnp.max(peak_ref[...], axis=0, keepdims=True)
 
         def exp_step(chunk, _):
-            total = sum_ref[...]
-            peak = peak_ref[...]
-            for half in range(CHUNK // 128):
-                cut = slice(half * 128, (half + 1) * 128)
-                probs = jnp.exp2((score_ref[chunk, :, :, cut] - peak) * power)
-                total = total + probs
-                probs_ref[part, chunk, :, cut] = probs.reshape(heads * ROWS, 128).astype(BF16)
-            sum_ref[...] = total
+            probs = jnp.exp2((score_ref[chunk] - peak) * power)
+            score_ref[chunk] = probs
+            sum_ref[...] = fold(sum_ref[...], probs, jnp.sum)
             return 0
 
         lax.fori_loop(chunk_low, chunk_high, exp_step, 0)
-        inverse = 1.0 / jnp.sum(sum_ref[...], axis=2, keepdims=True)
-        inverse_ref[part] = jnp.broadcast_to(inverse, sum_ref.shape).reshape(heads * ROWS, 128)
-        scaled_ref[part] = (
-            (grads_ref[part].astype(F32).reshape(heads, ROWS, 128) * inverse)
-            .reshape(heads * ROWS, 128)
-            .astype(BF16)
-        )
+        inverse = 1.0 / jnp.sum(sum_ref[...], axis=0, keepdims=True)
 
         def value_step(chunk, _):
-            at = pl.ds(pl.multiple_of(chunk * CHUNK, CHUNK), CHUNK)
-            total_ref[at, :] += tn_dot(probs_ref[part, chunk], scaled_ref[part])
+            probs = (score_ref[chunk] * inverse).astype(BF16)
+            probs_ref[part, chunk] = probs
+            total_ref[at_block(chunk, CHUNK), :] += jnp.dot(
+                probs, grads_ref[part], preferred_element_type=F32
+            )
             return 0
 
         lax.fori_loop(chunk_low, chunk_high, value_step, 0)
@@ -178,13 +184,13 @@
 
 
 def scores_kernel(
-    range_ref, queries_ref, scaled_ref, inverse_ref, probs_ref, keys_ref, value_ref,
+    range_ref, queries_ref, grads_ref, probs_ref, keys_ref, value_ref,
     r1, r2, r3, s1, s2, s3,
     grad_q_ref, own_ref, mine_ref, give_ref,
     values_ref, product_ref, delta_ref, query_ref, total_ref,
 ):
     rows = value_ref.shape[0]
-    heads = grad_q_ref.shape[1] // 128
+    stack = queries_ref.shape[1]
     core = lax.axis_index("fsdp")
     place_window(core, values_ref, value_ref[...], (r1[0], r2[0], r3[0]), (s1[0], s2[0], s3[0]))
     total_ref[...] = jnp.zeros_like(total_ref)
@@ -195,41 +201,27 @@
         query_ref[...] = jnp.zeros_like(query_ref)
 
         def delta_step(chunk, _):
-            at = pl.ds(pl.multiple_of(chunk * CHUNK, CHUNK), CHUNK)
-            product = nt_dot(scaled_ref[part], values_ref[at, :])
+            product = nt_dot(values_ref[at_block(chunk, CHUNK), :], grads_ref[part])
             product_ref[chunk] = product
             terms = product * probs_ref[part, chunk].astype(F32)
-            delta = delta_ref[...]
-            for half in range(CHUNK // 128):
-                delta = delta + terms[:, half * 128 : (half + 1) * 128]
-            delta_ref[...] = delta
+            delta_ref[...] = fold(delta_ref[...], terms, jnp.sum)
             return 0
 
         lax.fori_loop(chunk_low, chunk_high, delta_step, 0)
-        delta = jnp.sum(delta_ref[...], axis=1, keepdims=True)
-        delta_ref[...] = delta * inverse_ref[part]
+        delta = jnp.sum(delta_ref[...], axis=0, keepdims=True)
 
         def grad_step(chunk, _):
-            at = pl.ds(pl.multiple_of(chunk * CHUNK, CHUNK), CHUNK)
-            probs = probs_ref[part, chunk].astype(F32)
-            delta = delta_ref[...]
-            product = product_ref[chunk]
-            grad = jnp.concatenate(
-                [
-                    (probs[:, cut] * (product[:, cut] - delta)).astype(BF16)
-                    for cut in (slice(i, i + 128) for i in range(0, CHUNK, 128))
-                ],
-                axis=1,
+            at = at_block(chunk, CHUNK)
+            grad = (probs_ref[part, chunk].astype(F32) * (product_ref[chunk] - delta)).astype(BF16)
+            total_ref[at, :] += jnp.dot(grad, queries_ref[part], preferred_element_type=F32)
+            query_ref[...] += tn_dot(keys_ref[at, :], grad)
+            return 0
+
+        lax.fori_loop(chunk_low, chunk_high, grad_step, 0)
+        for h in range(0, stack, ROWS):
+            grad_q_ref[part * ROWS : (part + 1) * ROWS, h : h + ROWS] = (
+                (query_ref[:, h : h + ROWS] * scaling).T.astype(BF16)
             )
-            query_ref[...] += jnp.dot(grad, keys_ref[at, :], preferred_element_type=F32)
-            total_ref[at, :] += tn_dot(grad, queries_ref[part])
-            return 0
-
-        lax.fori_loop(chunk_low, chunk_high, grad_step, 0)
-        for h in range(heads):
-            grad_q_ref[part * ROWS : (part + 1) * ROWS, h * 128 : (h + 1) * 128] = (
-                query_ref[h * ROWS : (h + 1) * ROWS, :] * scaling
-            ).astype(BF16)
     give_out(core, total_ref, own_ref, mine_ref, give_ref, scaling)
 
 
@@ -303,38 +295,36 @@
     weight = w_value.T
     width = weight.shape[0]
     direct = dp == 8
-    distances = range(1, SPAN + 1)
-
-    mine = [fan_out(keys, k) for k in distances]
-    other = [core_swap(block) for block in mine]
+    steps = range(SPAN)
+
+    docs = jnp.concatenate([doc_lengths, prefix_spans])
+    query_stack = stack_heads(queries, head)
+    grad_stack = stack_heads(grad_out, head)
+    mine = [fan_out(keys, k) for k in steps]
+    other = [core_swap(after(block, docs, query_stack, grad_stack)) for block in mine]
     if direct:
         weight = after(weight, mine[0])
         z3, z2, z1 = (dp_swap(weight, 2 * k) for k in (3, 2, 1))
         cross0 = dp_swap(weight, 1)
 
-    query_stack = stack_heads(queries, head)
-    grad_stack = stack_heads(grad_out, head)
-
-    ranges, probs, scaled, inverse, key_window, own_v, mine_v, give_v = call(
+    ranges, probs, key_window, own_v, mine_v, give_v = call(
         weights_kernel,
         [
             ((2 * parts,), jnp.int32),
-            ((parts, chunks, stack, CHUNK), BF16),
-            ((parts, stack, head), BF16),
-            ((parts, stack, 128), F32),
+            ((parts, chunks, CHUNK, stack), BF16),
             ((window, head), BF16),
             ((rows, head), F32),
             ((SPAN, rows, head), F32),
             ((SPAN, rows, head), BF16),
         ],
         [
-            pltpu.VMEM((chunks, heads, ROWS, CHUNK), F32),
-            pltpu.VMEM((heads, ROWS, 128), F32),
-            pltpu.VMEM((heads, ROWS, 128), F32),
+            pltpu.VMEM((chunks, CHUNK, stack), F32),
+            pltpu.VMEM((8, stack), F32),
+            pltpu.VMEM((8, stack), F32),
             pltpu.VMEM((window, head), F32),
         ],
         20, 1,
-        jnp.concatenate([doc_lengths, prefix_spans]), query_stack, grad_stack, keys, *mine, *other,
+        docs, query_stack, grad_stack, keys, *mine, *other,
     )
     got_v = core_swap(give_v)
     other_v = core_swap(own_v)
@@ -356,7 +346,7 @@
         [], 8, 0,
         value_part, core_swap(value_part), mine_v, got_v,
     )
-    mine = [fan_out(pack, k) for pack, k in zip(packs, distances)]
+    mine = [fan_out(pack, k) for pack, k in zip(packs, steps)]
     other = [core_swap(block) for block in mine]
 
     if direct:
@@ -390,17 +380,17 @@
         ],
         [
             pltpu.VMEM((window, head), BF16),
-            pltpu.VMEM((chunks, stack, CHUNK), F32),
-            pltpu.VMEM((stack, 128), F32),
-            pltpu.VMEM((stack, head), F32),
+            pltpu.VMEM((chunks, CHUNK, stack), F32),
+            pltpu.VMEM((8, stack), F32),
+            pltpu.VMEM((head, stack), F32),
             pltpu.VMEM((window, head), F32),
         ],
         20, 1,
-        after(ranges, grad_value), query_stack, scaled, inverse, probs, key_window, value, *mine, *other,
+        after(ranges, grad_value), query_stack, grad_stack, probs, key_window, value, *mine, *other,
     )
     got_k = core_swap(give_k)
     mine = [
-        fan_out((mine_k[k - 1] + got_k[k - 1].astype(F32)).astype(BF16), k) for k in distances
+        fan_out((mine_k[k] + got_k[k].astype(F32)).astype(BF16), k) for k in steps
     ]
     other = [core_swap(block) for block in mine]
     grad_input = jnp.dot(

time: 86.3 us -> 80.6 us (0.934)
  starting transfers between devices: 60.1 us -> 53.3 us
    ppermute x9, starting transfers between devices: 37.5 us -> 22.7 us  [fan_out(): lax.ppermute(value, BOTH, [(i, j) for i, j in pairs if 0 <= j < 2 * count])]
    ppermute x14, starting transfers between devices: 2.32 us -> 7.4 us  [core_swap(): return lax.ppermute(value, 'fsdp', [(0, 1), (1, 0)])]
    ppermute x14, waiting for transfers between devices: 3.78 us -> 6.98 us  [dp_swap(): return lax.ppermute(value, 'dp', [(i, i ^ mask) for i in range(count)])]
    ppermute x14, starting transfers between devices: 20.3 us -> 23.1 us  [dp_swap(): return lax.ppermute(value, 'dp', [(i, i ^ mask) for i in range(count)])]
    ppermute x9, waiting for transfers between devices: 2.26 us -> 0.02 us  [fan_out(): lax.ppermute(value, BOTH, [(i, j) for i, j in pairs if 0 <= j < 2 * count])]
  transfers between devices with their start and end apart: 37 -> 37, of which waited for: 7 -> 8; matrix products, arithmetic and copies ran while one was open for 7% -> 7% of each run, Pallas kernels for 8% -> 10%
where the time goes in v1:
time: 80.6 us; the launch traced here: 79.4 us
  starting transfers between devices  53.3 us (66%)
  waiting for transfers between devices  10.2 us (13%)
  Pallas kernels  8.52 us (11%)
  other arithmetic  2.37 us (3%)
  local copies, waits for them, and re-layouts  2.12 us (3%)
  matrix products  2.02 us (3%)
  between operations  0.93 us (1%)
    ppermute x14, starting transfers between devices, dp_swap(): return lax.ppermute(value, 'dp', [(i, i ^ mask) for i in range(count)])  23.1 us
    ppermute x9, starting transfers between devices, fan_out(): lax.ppermute(value, BOTH, [(i, j) for i, j in pairs if 0 <= j < 2 * count])  22.7 us
    pallas_call x5, Pallas kernels, call(): pl.pallas_call(kernel, in_specs=[SMEM] * smem + [VMEM] * (len(args) - sme...  8.52 us
    ppermute x14, starting transfers between devices, core_swap(): return lax.ppermute(value, 'fsdp', [(0, 1), (1, 0)])  7.4 us
    ppermute x14, waiting for transfers between devices, dp_swap(): return lax.ppermute(value, 'dp', [(i, i ^ mask) for i in range(count)])  6.98 us
    ppermute x14, waiting for transfers between devices, core_swap(): return lax.ppermute(value, 'fsdp', [(0, 1), (1, 0)])  3.17 us
    reshape x4, local copies, waits for them, and re-layouts, stack_heads(): split = value.reshape(rows // ROWS, ROWS, wide // head, head)  2.1 us
    dot_general x1, matrix products, body(): jnp.dot(grad_value, full_weight, preferred_element_type=F32).astype(BF16)  2.02 us
  transfers between devices with their start and end apart: 37, of which 8 were waited for; matrix products, arithmetic and copies ran while one was open for 7% of the time, Pallas kernels for 10%

profile of v1, /device:TPU:0, one launch (start us, length us, event | category | flops | bytes accessed | tf_op | source)
XLA Modules:
  0.0 79.4 jit_solution(8111996709827259184)
XLA Ops:
  0.7 0.8 %collective-permute-start = (bf16[256,128]{1,0:T(8,128)(2,1)}, bf16[256,128]{1,0:T(8,128)(2,1)S(1)}, u32[]{:S(2)}, u32[]{:S(2)}) collective-permute-start(bf16[256,128]{1,0:T(8,128)(2,1)} %key_ref.1), channel_id=1, source_target_pairs={{2,8},{5,3},{6,12},{7,1},{8,2},{9,7},{11,5},{12,6},{13,11},{15,9},... | collective-permute-start | bytes 196616 | tf_op jit(solution)/shard_map/ppermute | solution.py:45
  1.5 1.3 %collective-permute-start.1 = (bf16[256,128]{1,0:T(8,128)(2,1)}, bf16[256,128]{1,0:T(8,128)(2,1)S(1)}, u32[]{:S(2)}, u32[]{:S(2)}) collective-permute-start(bf16[256,128]{1,0:T(8,128)(2,1)} %key_ref.1), channel_id=1, source_target_pairs={{1,7},{3,5},{4,0},{5,11},{6,2},{7,9},{8,4},{9,15},{10,6},{11,13},{... | collective-permute-start | bytes 196616 | tf_op jit(solution)/shard_map/ppermute | solution.py:45
  2.8 5.6 %collective-permute-start.2 = (bf16[256,128]{1,0:T(8,128)(2,1)}, bf16[256,128]{1,0:T(8,128)(2,1)S(1)}, u32[]{:S(2)}, u32[]{:S(2)}) collective-permute-start(bf16[256,128]{1,0:T(8,128)(2,1)} %key_ref.1), channel_id=1, source_target_pairs={{0,4},{1,3},{2,6},{3,1},{4,8},{5,7},{6,10},{7,5},{8,12},{9,11},{10... | collective-permute-start | bytes 196616 | tf_op jit(solution)/shard_map/ppermute | solution.py:45
  8.3 4.1 %collective-permute-start.7 = (bf16[16,4096]{1,0:T(8,128)(2,1)}, bf16[16,4096]{1,0:T(8,128)(2,1)S(1)}, u32[]{:S(2)}, u32[]{:S(2)}) collective-permute-start(bf16[16,4096]{1,0:T(8,128)(2,1)} %bitcast.21), channel_id=1, source_target_pairs={{0,4},{2,6},{4,0},{6,2},{8,12},{10,14},{12,8},{14,10},{1,5},{3,7},... | collective-permute-start | bytes 393224 | tf_op jit(solution)/shard_map/ppermute | solution.py:27
  12.5 3.1 %collective-permute-start.8 = (bf16[16,4096]{1,0:T(8,128)(2,1)}, bf16[16,4096]{1,0:T(8,128)(2,1)S(1)}, u32[]{:S(2)}, u32[]{:S(2)}) collective-permute-start(bf16[16,4096]{1,0:T(8,128)(2,1)} %bitcast.22), channel_id=1, source_target_pairs={{0,8},{2,10},{4,12},{6,14},{8,0},{10,2},{12,4},{14,6},{1,9},{3,11}... | collective-permute-start | bytes 393224 | tf_op jit(solution)/shard_map/ppermute | solution.py:27
  15.6 0.7 pad_add_fusion.docs_ref
  16.4 1.0 %reshape.29 = bf16[2,128,4,128]{3,2,1,0:T(4,128)(2,1)S(1)} reshape(bf16[256,512]{1,0:T(8,128)(2,1)} %param.9) | data formatting | bytes 524288 | tf_op jit(solution)/shard_map/reshape | solution.py:108
  17.4 1.0 %reshape.31 = bf16[2,128,4,128]{3,2,1,0:T(4,128)(2,1)S(1)} reshape(bf16[256,512]{1,0:T(8,128)(2,1)} %param.11) | data formatting | bytes 524288 | tf_op jit(solution)/shard_map/reshape | solution.py:108
  19.1 0.7 collective-permute-done.3.s1
  20.0 2.9 %collective-permute-start.10 = (bf16[16,4096]{1,0:T(8,128)(2,1)S(1)}, bf16[16,4096]{1,0:T(8,128)(2,1)S(1)}, u32[]{:S(2)}, u32[]{:S(2)}) collective-permute-start(bf16[16,4096]{1,0:T(8,128)(2,1)S(1)} %bitcast.24), channel_id=1, source_target_pairs={{0,2},{2,0},{4,6},{6,4},{8,10},{10,8},{12,14},{14,12},{1,3},{3,1},... | collective-permute-start | bytes 393224 | tf_op jit(solution)/shard_map/ppermute | solution.py:27
  23.0 2.9 %collective-permute-done.8.z2 = bf16[16,4096]{1,0:T(8,128)(2,1)S(1)} collective-permute-done((bf16[16,4096]{1,0:T(8,128)(2,1)}, bf16[16,4096]{1,0:T(8,128)(2,1)S(1)}, u32[]{:S(2)}, u32[]{:S(2)}) %collective-permute-start.8) | collective-permute-done | bytes 131104 | tf_op jit(solution)/shard_map/ppermute | solution.py:27
  25.9 1.0 %collective-permute-start.12 = (bf16[16,4096]{1,0:T(8,128)(2,1)S(1)}, bf16[16,4096]{1,0:T(8,128)(2,1)S(1)}, u32[]{:S(2)}, u32[]{:S(2)}) collective-permute-start(bf16[16,4096]{1,0:T(8,128)(2,1)S(1)} %collective-permute-done.8.z2), channel_id=1, source_target_pairs={{0,2},{2,0},{4,6},{6,4},{8,10},{10,8},{12,14},{14,12},{1,3},{3,1},... | collective-permute-start | bytes 393224 | tf_op jit(solution)/shard_map/ppermute | solution.py:27
  26.8 1.1 %collective-permute-start.13 = (bf16[16,4096]{1,0:T(8,128)(2,1)S(1)}, bf16[16,4096]{1,0:T(8,128)(2,1)S(1)}, u32[]{:S(2)}, u32[]{:S(2)}) collective-permute-start(bf16[16,4096]{1,0:T(8,128)(2,1)S(1)} %collective-permute-done.9.z3), channel_id=1, source_target_pairs={{0,2},{2,0},{4,6},{6,4},{8,10},{10,8},{12,14},{14,12},{1,3},{3,1},... | collective-permute-start | bytes 393224 | tf_op jit(solution)/shard_map/ppermute | solution.py:27
  27.9 3.5 %shard_map.102 = (s32[4]{0:T(128)S(1)}, bf16[2,7,256,512]{3,2,1,0:T(8,128)(2,1)S(1)}, bf16[1792,128]{1,0:T(8,128)(2,1)S(1)}, f32[256,128]{1,0:T(8,128)S(1)}, f32...) custom-call(s32[8]{0:T(128)S(1)} %pad_add_fusion.docs_ref, bf16[2,512,128]{2,1,0:T(8,128)(2,1)S(1)} %bitcast.17, ...), custom_call_target="tpu_custom_call" | custom-call | flops 1073741824 | bytes 4194304 | tf_op jit(solution)/shard_map/pallas_call | solution.py:275
  31.5 1.4 %collective-permute-done.12.c2 = bf16[16,4096]{1,0:T(8,128)(2,1)S(1)} collective-permute-done((bf16[16,4096]{1,0:T(8,128)(2,1)S(1)}, bf16[16,4096]{1,0:T(8,128)(2,1)S(1)}, u32[]{:S(2)}, u32[]{:S(2)}) %collective-permute-start.12) | collective-permute-done | bytes 131104 | tf_op jit(solution)/shard_map/ppermute | solution.py:27
  32.9 2.5 %collective-permute-done.13.c3 = bf16[16,4096]{1,0:T(8,128)(2,1)S(1)} collective-permute-done((bf16[16,4096]{1,0:T(8,128)(2,1)S(1)}, bf16[16,4096]{1,0:T(8,128)(2,1)S(1)}, u32[]{:S(2)}, u32[]{:S(2)}) %collective-permute-start.13) | collective-permute-done | bytes 131104 | tf_op jit(solution)/shard_map/ppermute | solution.py:27
  35.3 0.8 %shard_map.103 = (f32[256,128]{1,0:T(8,128)S(1)}, bf16[128,4096]{1,0:T(8,128)(2,1)S(1)}) custom-call(bf16[256,4096]{1,0:T(8,128)(2,1)S(1)} %copy-done, bf16[16,4096]{1,0:T(8,128)(2,1)S(1)} %bitcast.25, bf16[16,4096]{1,0:T(8,128)(2,1)S(1)} %collective-permute-done.7.z1, bf16[16,4096]{1,0:T(8,128)(2,1)S(1)} %collective-permute-done.8.z2, ...), custom_call_target="tpu_custom_call" | custom-call | flops 1073741824 | bytes 4194304 | tf_op jit(solution)/shard_map/pallas_call | solution.py:275
  36.2 1.3 %collective-permute-done.14.other_ref = f32[256,128]{1,0:T(8,128)S(1)} collective-permute-done((f32[256,128]{1,0:T(8,128)S(1)}, f32[256,128]{1,0:T(8,128)S(1)}, u32[]{:S(2)}, u32[]{:S(2)}) %collective-permute-start.14) | collective-permute-done | bytes 131104 | tf_op jit(solution)/shard_map/ppermute | solution.py:22
  38.3 1.3 %collective-permute-start.17 = (bf16[2,256,128]{2,1,0:T(8,128)(2,1)S(1)}, bf16[2,256,128]{2,1,0:T(8,128)(2,1)S(1)}, u32[]{:S(2)}, u32[]{:S(2)}) collective-permute-start(bf16[2,256,128]{2,1,0:T(8,128)(2,1)S(1)} %get-tuple-element.43), channel_id=1, source_target_pairs={{1,7},{3,5},{4,0},{5,11},{6,2},{7,9},{8,4},{9,15},{10,6},{11,13},{... | collective-permute-start | bytes 393224 | tf_op jit(solution)/shard_map/ppermute | solution.py:45
  39.6 4.6 %collective-permute-start.18 = (bf16[2,256,128]{2,1,0:T(8,128)(2,1)S(1)}, bf16[2,256,128]{2,1,0:T(8,128)(2,1)S(1)}, u32[]{:S(2)}, u32[]{:S(2)}) collective-permute-start(bf16[2,256,128]{2,1,0:T(8,128)(2,1)S(1)} %get-tuple-element.44), channel_id=1, source_target_pairs={{0,4},{1,3},{2,6},{3,1},{4,8},{5,7},{6,10},{7,5},{8,12},{9,11},{10... | collective-permute-start | bytes 393224 | tf_op jit(solution)/shard_map/ppermute | solution.py:45
  44.2 3.3 %collective-permute-start.6 = (f32[256,128]{1,0:T(8,128)S(1)}, f32[256,128]{1,0:T(8,128)S(1)}, u32[]{:S(2)}, u32[]{:S(2)}) collective-permute-start(f32[256,128]{1,0:T(8,128)S(1)} %get-tuple-element.37.a_ref), channel_id=1, source_target_pairs={{0,1},{1,0},{2,3},{3,2},{4,5},{5,4},{6,7},{7,6},{8,9},{9,8},{10,11... | collective-permute-start | bytes 393224 | tf_op jit(solution)/shard_map/ppermute | solution.py:22
  47.9 1.8 %collective-permute-start.21 = (bf16[2,256,128]{2,1,0:T(8,128)(2,1)S(1)}, bf16[2,256,128]{2,1,0:T(8,128)(2,1)S(1)}, u32[]{:S(2)}, u32[]{:S(2)}) collective-permute-start(bf16[2,256,128]{2,1,0:T(8,128)(2,1)S(1)} %collective-permute-done.18.r3), channel_id=1, source_target_pairs={{0,1},{1,0},{2,3},{3,2},{4,5},{5,4},{6,7},{7,6},{8,9},{9,8},{10,11... | collective-permute-start | bytes 393224 | tf_op jit(solution)/shard_map/ppermute | solution.py:22
  49.7 1.0 %collective-permute-done.21.s3 = bf16[2,256,128]{2,1,0:T(8,128)(2,1)S(1)} collective-permute-done((bf16[2,256,128]{2,1,0:T(8,128)(2,1)S(1)}, bf16[2,256,128]{2,1,0:T(8,128)(2,1)S(1)}, u32[]{:S(2)}, u32[]{:S(2)}) %collective-permute-start.21) | collective-permute-done | bytes 131104 | tf_op jit(solution)/shard_map/ppermute | solution.py:22
  51.3 1.8 %collective-permute-start.30 = (bf16[16,4096]{1,0:T(8,128)(2,1)S(1)}, bf16[16,4096]{1,0:T(8,128)(2,1)S(1)}, u32[]{:S(2)}, u32[]{:S(2)}) collective-permute-start(bf16[16,4096]{1,0:T(8,128)(2,1)S(1)} %get-tuple-element.58), channel_id=1, source_target_pairs={{0,2},{2,0},{4,6},{6,4},{8,10},{10,8},{12,14},{14,12},{1,3},{3,1},... | collective-permute-start | bytes 393224 | tf_op jit(solution)/shard_map/ppermute | solution.py:27
  53.4 1.7 %collective-permute-start.34 = (bf16[16,4096]{1,0:T(8,128)(2,1)S(1)}, bf16[16,4096]{1,0:T(8,128)(2,1)S(1)}, u32[]{:S(2)}, u32[]{:S(2)}) collective-permute-start(bf16[16,4096]{1,0:T(8,128)(2,1)S(1)} %get-tuple-element.62), channel_id=1, source_target_pairs={{0,2},{2,0},{4,6},{6,4},{8,10},{10,8},{12,14},{14,12},{1,3},{3,1},... | collective-permute-start | bytes 393224 | tf_op jit(solution)/shard_map/ppermute | solution.py:27
  55.5 3.6 %shard_map.106 = (bf16[256,512]{1,0:T(8,128)(2,1)}, f32[256,128]{1,0:T(8,128)S(1)}, f32[3,256,128]{2,1,0:T(8,128)S(1)}, bf16[3,256,128]{2,1,0:T(8,128)(2,1)S(1)}) custom-call(s32[4]{0:T(128)S(1)} %get-tuple-element.48.range_ref, bf16[2,512,128]{2,1,0:T(8,128)(2,1)S(1)} %bitcast.18, bf16[2,512,128]{2,1,0:T(8,128)(2,1)S(1)} %bitcast.20, ...), custom_call_target="tpu_custom_call" | custom-call | flops 1073741824 | bytes 4194304 | tf_op jit(solution)/shard_map/pallas_call | solution.py:275
  59.1 4.6 %collective-permute-start.31 = (bf16[16,4096]{1,0:T(8,128)(2,1)S(1)}, bf16[16,4096]{1,0:T(8,128)(2,1)S(1)}, u32[]{:S(2)}, u32[]{:S(2)}) collective-permute-start(bf16[16,4096]{1,0:T(8,128)(2,1)S(1)} %add_convert_fusion.2), channel_id=1, source_target_pairs={{0,12},{2,14},{4,8},{6,10},{8,4},{10,6},{12,0},{14,2},{1,13},{3,15... | collective-permute-start | bytes 393224 | tf_op jit(solution)/shard_map/ppermute | solution.py:27
  63.8 2.0 %collective-permute-start.35 = (bf16[16,4096]{1,0:T(8,128)(2,1)S(1)}, bf16[16,4096]{1,0:T(8,128)(2,1)S(1)}, u32[]{:S(2)}, u32[]{:S(2)}) collective-permute-start(bf16[16,4096]{1,0:T(8,128)(2,1)S(1)} %add_convert_fusion), channel_id=1, source_target_pairs={{0,4},{2,6},{4,0},{6,2},{8,12},{10,14},{12,8},{14,10},{1,5},{3,7},... | collective-permute-start | bytes 393224 | tf_op jit(solution)/shard_map/ppermute | solution.py:27
  66.6 1.3 %collective-permute-start.26 = (bf16[256,128]{1,0:T(8,128)(2,1)S(1)}, bf16[256,128]{1,0:T(8,128)(2,1)S(1)}, u32[]{:S(2)}, u32[]{:S(2)}) collective-permute-start(bf16[256,128]{1,0:T(8,128)(2,1)S(1)} %get-tuple-element.66), channel_id=1, source_target_pairs={{1,7},{3,5},{4,0},{5,11},{6,2},{7,9},{8,4},{9,15},{10,6},{11,13},{... | collective-permute-start | bytes 196616 | tf_op jit(solution)/shard_map/ppermute | solution.py:45
  68.1 6.6 %collective-permute-start.28 = (bf16[256,128]{1,0:T(8,128)(2,1)S(1)}, bf16[256,128]{1,0:T(8,128)(2,1)S(1)}, u32[]{:S(2)}, u32[]{:S(2)}) collective-permute-start(bf16[256,128]{1,0:T(8,128)(2,1)S(1)} %get-tuple-element.65), channel_id=1, source_target_pairs={{0,4},{1,3},{2,6},{3,1},{4,8},{5,7},{6,10},{7,5},{8,12},{9,11},{10... | collective-permute-start | bytes 196616 | tf_op jit(solution)/shard_map/ppermute | solution.py:45
  74.7 2.0 %convolution_convert_fusion = bf16[256,4096]{1,0:T(8,128)(2,1)} fusion(bf16[256,128]{1,0:T(8,128)(2,1)S(1)} %get-tuple-element.45, bf16[128,4096]{1,0:T(8,128)(2,1)S(1)} %get-tuple-element.46), kind=kOutput, calls=%fused_computation | convolution fusion | flops 269484032 | bytes 3211264 | tf_op jit(solution)/shard_map/dot_general | solution.py:396
  77.8 0.8 add_bitcast_fusion
  (65 shorter events, 6.5 us)
Async XLA Ops:
  0.7 7.7 %collective-permute-start = (bf16[256,128]{1,0:T(8,128)(2,1)}, bf16[256,128]{1,0:T(8,128)(2,1)S(1)}, u32[]{:S(2)}, u32[]{:S(2)}) collective-permute-start(bf16[256,128]{1,0:T(8,128)(2,1)} %key_ref.1), channel_id=1, source_target_pairs={{2,8},{5,3},{6,12},{7,1},{8,2},{9,7},{11,5},{12,6},{13,11},{15,9},... | collective-permute-start | bytes 196616 | tf_op jit(solution)/shard_map/ppermute | solution.py:45
  1.5 17.0 %collective-permute-start.1 = (bf16[256,128]{1,0:T(8,128)(2,1)}, bf16[256,128]{1,0:T(8,128)(2,1)S(1)}, u32[]{:S(2)}, u32[]{:S(2)}) collective-permute-start(bf16[256,128]{1,0:T(8,128)(2,1)} %key_ref.1), channel_id=1, source_target_pairs={{1,7},{3,5},{4,0},{5,11},{6,2},{7,9},{8,4},{9,15},{10,6},{11,13},{... | collective-permute-start | bytes 196616 | tf_op jit(solution)/shard_map/ppermute | solution.py:45
  2.8 15.8 %collective-permute-start.2 = (bf16[256,128]{1,0:T(8,128)(2,1)}, bf16[256,128]{1,0:T(8,128)(2,1)S(1)}, u32[]{:S(2)}, u32[]{:S(2)}) collective-permute-start(bf16[256,128]{1,0:T(8,128)(2,1)} %key_ref.1), channel_id=1, source_target_pairs={{0,4},{1,3},{2,6},{3,1},{4,8},{5,7},{6,10},{7,5},{8,12},{9,11},{10... | collective-permute-start | bytes 196616 | tf_op jit(solution)/shard_map/ppermute | solution.py:45
  8.3 14.6 %collective-permute-start.7 = (bf16[16,4096]{1,0:T(8,128)(2,1)}, bf16[16,4096]{1,0:T(8,128)(2,1)S(1)}, u32[]{:S(2)}, u32[]{:S(2)}) collective-permute-start(bf16[16,4096]{1,0:T(8,128)(2,1)} %bitcast.21), channel_id=1, source_target_pairs={{0,4},{2,6},{4,0},{6,2},{8,12},{10,14},{12,8},{14,10},{1,5},{3,7},... | collective-permute-start | bytes 393224 | tf_op jit(solution)/shard_map/ppermute | solution.py:27
  12.5 13.4 %collective-permute-start.8 = (bf16[16,4096]{1,0:T(8,128)(2,1)}, bf16[16,4096]{1,0:T(8,128)(2,1)S(1)}, u32[]{:S(2)}, u32[]{:S(2)}) collective-permute-start(bf16[16,4096]{1,0:T(8,128)(2,1)} %bitcast.22), channel_id=1, source_target_pairs={{0,8},{2,10},{4,12},{6,14},{8,0},{10,2},{12,4},{14,6},{1,9},{3,11}... | collective-permute-start | bytes 393224 | tf_op jit(solution)/shard_map/ppermute | solution.py:27
  15.6 11.2 %collective-permute-start.9 = (bf16[16,4096]{1,0:T(8,128)(2,1)}, bf16[16,4096]{1,0:T(8,128)(2,1)S(1)}, u32[]{:S(2)}, u32[]{:S(2)}) collective-permute-start(bf16[16,4096]{1,0:T(8,128)(2,1)} %bitcast.23), channel_id=1, source_target_pairs={{0,12},{2,14},{4,8},{6,10},{8,4},{10,6},{12,0},{14,2},{1,13},{3,15... | collective-permute-start | bytes 393224 | tf_op jit(solution)/shard_map/ppermute | solution.py:27
  19.8 8.1 %collective-permute-start.5 = (bf16[256,128]{1,0:T(8,128)(2,1)S(1)}, bf16[256,128]{1,0:T(8,128)(2,1)S(1)}, u32[]{:S(2)}, u32[]{:S(2)}) collective-permute-start(bf16[256,128]{1,0:T(8,128)(2,1)S(1)} %collective-permute-done.2.r3), channel_id=1, source_target_pairs={{0,1},{1,0},{2,3},{3,2},{4,5},{5,4},{6,7},{7,6},{8,9},{9,8},{10,11... | collective-permute-start | bytes 196616 | tf_op jit(solution)/shard_map/ppermute | solution.py:22
  20.0 11.4 %collective-permute-start.10 = (bf16[16,4096]{1,0:T(8,128)(2,1)S(1)}, bf16[16,4096]{1,0:T(8,128)(2,1)S(1)}, u32[]{:S(2)}, u32[]{:S(2)}) collective-permute-start(bf16[16,4096]{1,0:T(8,128)(2,1)S(1)} %bitcast.24), channel_id=1, source_target_pairs={{0,2},{2,0},{4,6},{6,4},{8,10},{10,8},{12,14},{14,12},{1,3},{3,1},... | collective-permute-start | bytes 393224 | tf_op jit(solution)/shard_map/ppermute | solution.py:27
  22.9 8.5 %collective-permute-start.11 = (bf16[16,4096]{1,0:T(8,128)(2,1)S(1)}, bf16[16,4096]{1,0:T(8,128)(2,1)S(1)}, u32[]{:S(2)}, u32[]{:S(2)}) collective-permute-start(bf16[16,4096]{1,0:T(8,128)(2,1)S(1)} %collective-permute-done.7.z1), channel_id=1, source_target_pairs={{0,2},{2,0},{4,6},{6,4},{8,10},{10,8},{12,14},{14,12},{1,3},{3,1},... | collective-permute-start | bytes 393224 | tf_op jit(solution)/shard_map/ppermute | solution.py:27
  25.9 7.0 %collective-permute-start.12 = (bf16[16,4096]{1,0:T(8,128)(2,1)S(1)}, bf16[16,4096]{1,0:T(8,128)(2,1)S(1)}, u32[]{:S(2)}, u32[]{:S(2)}) collective-permute-start(bf16[16,4096]{1,0:T(8,128)(2,1)S(1)} %collective-permute-done.8.z2), channel_id=1, source_target_pairs={{0,2},{2,0},{4,6},{6,4},{8,10},{10,8},{12,14},{14,12},{1,3},{3,1},... | collective-permute-start | bytes 393224 | tf_op jit(solution)/shard_map/ppermute | solution.py:27
  26.8 8.5 %collective-permute-start.13 = (bf16[16,4096]{1,0:T(8,128)(2,1)S(1)}, bf16[16,4096]{1,0:T(8,128)(2,1)S(1)}, u32[]{:S(2)}, u32[]{:S(2)}) collective-permute-start(bf16[16,4096]{1,0:T(8,128)(2,1)S(1)} %collective-permute-done.9.z3), channel_id=1, source_target_pairs={{0,2},{2,0},{4,6},{6,4},{8,10},{10,8},{12,14},{14,12},{1,3},{3,1},... | collective-permute-start | bytes 393224 | tf_op jit(solution)/shard_map/ppermute | solution.py:27
  31.4 4.9 %collective-permute-start.15 = (bf16[3,256,128]{2,1,0:T(8,128)(2,1)S(1)}, bf16[3,256,128]{2,1,0:T(8,128)(2,1)S(1)}, u32[]{:S(2)}, u32[]{:S(2)}) collective-permute-start(bf16[3,256,128]{2,1,0:T(8,128)(2,1)S(1)} %get-tuple-element.41), channel_id=1, source_target_pairs={{0,1},{1,0},{2,3},{3,2},{4,5},{5,4},{6,7},{7,6},{8,9},{9,8},{10,11... | collective-permute-start | bytes 589832 | tf_op jit(solution)/shard_map/ppermute | solution.py:22
  37.6 9.8 %collective-permute-start.16 = (bf16[2,256,128]{2,1,0:T(8,128)(2,1)S(1)}, bf16[2,256,128]{2,1,0:T(8,128)(2,1)S(1)}, u32[]{:S(2)}, u32[]{:S(2)}) collective-permute-start(bf16[2,256,128]{2,1,0:T(8,128)(2,1)S(1)} %get-tuple-element.42), channel_id=1, source_target_pairs={{2,8},{5,3},{6,12},{7,1},{8,2},{9,7},{11,5},{12,6},{13,11},{15,9},... | collective-permute-start | bytes 393224 | tf_op jit(solution)/shard_map/ppermute | solution.py:45
  38.3 9.2 %collective-permute-start.17 = (bf16[2,256,128]{2,1,0:T(8,128)(2,1)S(1)}, bf16[2,256,128]{2,1,0:T(8,128)(2,1)S(1)}, u32[]{:S(2)}, u32[]{:S(2)}) collective-permute-start(bf16[2,256,128]{2,1,0:T(8,128)(2,1)S(1)} %get-tuple-element.43), channel_id=1, source_target_pairs={{1,7},{3,5},{4,0},{5,11},{6,2},{7,9},{8,4},{9,15},{10,6},{11,13},{... | collective-permute-start | bytes 393224 | tf_op jit(solution)/shard_map/ppermute | solution.py:45
  39.6 8.3 %collective-permute-start.18 = (bf16[2,256,128]{2,1,0:T(8,128)(2,1)S(1)}, bf16[2,256,128]{2,1,0:T(8,128)(2,1)S(1)}, u32[]{:S(2)}, u32[]{:S(2)}) collective-permute-start(bf16[2,256,128]{2,1,0:T(8,128)(2,1)S(1)} %get-tuple-element.44), channel_id=1, source_target_pairs={{0,4},{1,3},{2,6},{3,1},{4,8},{5,7},{6,10},{7,5},{8,12},{9,11},{10... | collective-permute-start | bytes 393224 | tf_op jit(solution)/shard_map/ppermute | solution.py:45
  44.2 5.5 %collective-permute-start.6 = (f32[256,128]{1,0:T(8,128)S(1)}, f32[256,128]{1,0:T(8,128)S(1)}, u32[]{:S(2)}, u32[]{:S(2)}) collective-permute-start(f32[256,128]{1,0:T(8,128)S(1)} %get-tuple-element.37.a_ref), channel_id=1, source_target_pairs={{0,1},{1,0},{2,3},{3,2},{4,5},{5,4},{6,7},{7,6},{8,9},{9,8},{10,11... | collective-permute-start | bytes 393224 | tf_op jit(solution)/shard_map/ppermute | solution.py:22
  47.4 2.3 %collective-permute-start.19 = (bf16[2,256,128]{2,1,0:T(8,128)(2,1)S(1)}, bf16[2,256,128]{2,1,0:T(8,128)(2,1)S(1)}, u32[]{:S(2)}, u32[]{:S(2)}) collective-permute-start(bf16[2,256,128]{2,1,0:T(8,128)(2,1)S(1)} %collective-permute-done.16.r1), channel_id=1, source_target_pairs={{0,1},{1,0},{2,3},{3,2},{4,5},{5,4},{6,7},{7,6},{8,9},{9,8},{10,11... | collective-permute-start | bytes 393224 | tf_op jit(solution)/shard_map/ppermute | solution.py:22
  47.5 2.2 %collective-permute-start.20 = (bf16[2,256,128]{2,1,0:T(8,128)(2,1)S(1)}, bf16[2,256,128]{2,1,0:T(8,128)(2,1)S(1)}, u32[]{:S(2)}, u32[]{:S(2)}) collective-permute-start(bf16[2,256,128]{2,1,0:T(8,128)(2,1)S(1)} %collective-permute-done.17.r2), channel_id=1, source_target_pairs={{0,1},{1,0},{2,3},{3,2},{4,5},{5,4},{6,7},{7,6},{8,9},{9,8},{10,11... | collective-permute-start | bytes 393224 | tf_op jit(solution)/shard_map/ppermute | solution.py:22
  47.9 2.7 %collective-permute-start.21 = (bf16[2,256,128]{2,1,0:T(8,128)(2,1)S(1)}, bf16[2,256,128]{2,1,0:T(8,128)(2,1)S(1)}, u32[]{:S(2)}, u32[]{:S(2)}) collective-permute-start(bf16[2,256,128]{2,1,0:T(8,128)(2,1)S(1)} %collective-permute-done.18.r3), channel_id=1, source_target_pairs={{0,1},{1,0},{2,3},{3,2},{4,5},{5,4},{6,7},{7,6},{8,9},{9,8},{10,11... | collective-permute-start | bytes 393224 | tf_op jit(solution)/shard_map/ppermute | solution.py:22
  51.3 7.7 %collective-permute-start.30 = (bf16[16,4096]{1,0:T(8,128)(2,1)S(1)}, bf16[16,4096]{1,0:T(8,128)(2,1)S(1)}, u32[]{:S(2)}, u32[]{:S(2)}) collective-permute-start(bf16[16,4096]{1,0:T(8,128)(2,1)S(1)} %get-tuple-element.58), channel_id=1, source_target_pairs={{0,2},{2,0},{4,6},{6,4},{8,10},{10,8},{12,14},{14,12},{1,3},{3,1},... | collective-permute-start | bytes 393224 | tf_op jit(solution)/shard_map/ppermute | solution.py:27
  53.1 10.5 %collective-permute-start.32 = (bf16[16,4096]{1,0:T(8,128)(2,1)S(1)}, bf16[16,4096]{1,0:T(8,128)(2,1)S(1)}, u32[]{:S(2)}, u32[]{:S(2)}) collective-permute-start(bf16[16,4096]{1,0:T(8,128)(2,1)S(1)} %get-tuple-element.60), channel_id=1, source_target_pairs={{0,2},{2,0},{4,6},{6,4},{8,10},{10,8},{12,14},{14,12},{1,3},{3,1},... | collective-permute-start | bytes 393224 | tf_op jit(solution)/shard_map/ppermute | solution.py:27
  53.4 10.3 %collective-permute-start.34 = (bf16[16,4096]{1,0:T(8,128)(2,1)S(1)}, bf16[16,4096]{1,0:T(8,128)(2,1)S(1)}, u32[]{:S(2)}, u32[]{:S(2)}) collective-permute-start(bf16[16,4096]{1,0:T(8,128)(2,1)S(1)} %get-tuple-element.62), channel_id=1, source_target_pairs={{0,2},{2,0},{4,6},{6,4},{8,10},{10,8},{12,14},{14,12},{1,3},{3,1},... | collective-permute-start | bytes 393224 | tf_op jit(solution)/shard_map/ppermute | solution.py:27
  55.2 11.4 %collective-permute-start.36 = (bf16[16,4096]{1,0:T(8,128)(2,1)S(1)}, bf16[16,4096]{1,0:T(8,128)(2,1)S(1)}, u32[]{:S(2)}, u32[]{:S(2)}) collective-permute-start(bf16[16,4096]{1,0:T(8,128)(2,1)S(1)} %get-tuple-element.63), channel_id=1, source_target_pairs={{0,2},{2,0},{4,6},{6,4},{8,10},{10,8},{12,14},{14,12},{1,3},{3,1},... | collective-permute-start | bytes 393224 | tf_op jit(solution)/shard_map/ppermute | solution.py:27
  59.0 6.8 %collective-permute-start.23 = (bf16[3,256,128]{2,1,0:T(8,128)(2,1)S(1)}, bf16[3,256,128]{2,1,0:T(8,128)(2,1)S(1)}, u32[]{:S(2)}, u32[]{:S(2)}) collective-permute-start(bf16[3,256,128]{2,1,0:T(8,128)(2,1)S(1)} %get-tuple-element.55), channel_id=1, source_target_pairs={{0,1},{1,0},{2,3},{3,2},{4,5},{5,4},{6,7},{7,6},{8,9},{9,8},{10,11... | collective-permute-start | bytes 589832 | tf_op jit(solution)/shard_map/ppermute | solution.py:22
  59.1 9.0 %collective-permute-start.31 = (bf16[16,4096]{1,0:T(8,128)(2,1)S(1)}, bf16[16,4096]{1,0:T(8,128)(2,1)S(1)}, u32[]{:S(2)}, u32[]{:S(2)}) collective-permute-start(bf16[16,4096]{1,0:T(8,128)(2,1)S(1)} %add_convert_fusion.2), channel_id=1, source_target_pairs={{0,12},{2,14},{4,8},{6,10},{8,4},{10,6},{12,0},{14,2},{1,13},{3,15... | collective-permute-start | bytes 393224 | tf_op jit(solution)/shard_map/ppermute | solution.py:27
  63.7 13.1 %collective-permute-start.33 = (bf16[16,4096]{1,0:T(8,128)(2,1)S(1)}, bf16[16,4096]{1,0:T(8,128)(2,1)S(1)}, u32[]{:S(2)}, u32[]{:S(2)}) collective-permute-start(bf16[16,4096]{1,0:T(8,128)(2,1)S(1)} %add_convert_fusion.1), channel_id=1, source_target_pairs={{0,8},{2,10},{4,12},{6,14},{8,0},{10,2},{12,4},{14,6},{1,9},{3,11}... | collective-permute-start | bytes 393224 | tf_op jit(solution)/shard_map/ppermute | solution.py:27
  63.8 14.0 %collective-permute-start.35 = (bf16[16,4096]{1,0:T(8,128)(2,1)S(1)}, bf16[16,4096]{1,0:T(8,128)(2,1)S(1)}, u32[]{:S(2)}, u32[]{:S(2)}) collective-permute-start(bf16[16,4096]{1,0:T(8,128)(2,1)S(1)} %add_convert_fusion), channel_id=1, source_target_pairs={{0,4},{2,6},{4,0},{6,2},{8,12},{10,14},{12,8},{14,10},{1,5},{3,7},... | collective-permute-start | bytes 393224 | tf_op jit(solution)/shard_map/ppermute | solution.py:27
  65.9 10.8 %collective-permute-start.24 = (bf16[256,128]{1,0:T(8,128)(2,1)S(1)}, bf16[256,128]{1,0:T(8,128)(2,1)S(1)}, u32[]{:S(2)}, u32[]{:S(2)}) collective-permute-start(bf16[256,128]{1,0:T(8,128)(2,1)S(1)} %get-tuple-element.64), channel_id=1, source_target_pairs={{2,8},{5,3},{6,12},{7,1},{8,2},{9,7},{11,5},{12,6},{13,11},{15,9},... | collective-permute-start | bytes 196616 | tf_op jit(solution)/shard_map/ppermute | solution.py:45
  66.6 10.7 %collective-permute-start.26 = (bf16[256,128]{1,0:T(8,128)(2,1)S(1)}, bf16[256,128]{1,0:T(8,128)(2,1)S(1)}, u32[]{:S(2)}, u32[]{:S(2)}) collective-permute-start(bf16[256,128]{1,0:T(8,128)(2,1)S(1)} %get-tuple-element.66), channel_id=1, source_target_pairs={{1,7},{3,5},{4,0},{5,11},{6,2},{7,9},{8,4},{9,15},{10,6},{11,13},{... | collective-permute-start | bytes 196616 | tf_op jit(solution)/shard_map/ppermute | solution.py:45
  68.1 9.2 %collective-permute-start.28 = (bf16[256,128]{1,0:T(8,128)(2,1)S(1)}, bf16[256,128]{1,0:T(8,128)(2,1)S(1)}, u32[]{:S(2)}, u32[]{:S(2)}) collective-permute-start(bf16[256,128]{1,0:T(8,128)(2,1)S(1)} %get-tuple-element.65), channel_id=1, source_target_pairs={{0,4},{1,3},{2,6},{3,1},{4,8},{5,7},{6,10},{7,5},{8,12},{9,11},{10... | collective-permute-start | bytes 196616 | tf_op jit(solution)/shard_map/ppermute | solution.py:45
  76.8 1.8 %collective-permute-start.22 = (f32[256,128]{1,0:T(8,128)S(1)}, f32[256,128]{1,0:T(8,128)S(1)}, u32[]{:S(2)}, u32[]{:S(2)}) collective-permute-start(f32[256,128]{1,0:T(8,128)S(1)} %get-tuple-element.53), channel_id=1, source_target_pairs={{0,1},{1,0},{2,3},{3,2},{4,5},{5,4},{6,7},{7,6},{8,9},{9,8},{10,11... | collective-permute-start | bytes 393224 | tf_op jit(solution)/shard_map/ppermute | solution.py:22
  76.8 1.8 %collective-permute-start.25 = (bf16[256,128]{1,0:T(8,128)(2,1)S(1)}, bf16[256,128]{1,0:T(8,128)(2,1)S(1)}, u32[]{:S(2)}, u32[]{:S(2)}) collective-permute-start(bf16[256,128]{1,0:T(8,128)(2,1)S(1)} %collective-permute-done.24), channel_id=1, source_target_pairs={{0,1},{1,0},{2,3},{3,2},{4,5},{5,4},{6,7},{7,6},{8,9},{9,8},{10,11... | collective-permute-start | bytes 196616 | tf_op jit(solution)/shard_map/ppermute | solution.py:22
  (8 other events, 70.2 us)

commit v2 on v1

--- a/solution.py
+++ b/solution.py
@@ -16,6 +16,7 @@
 BF16 = jnp.bfloat16
 VMEM = pl.BlockSpec(memory_space=pltpu.VMEM)
 SMEM = pl.BlockSpec(memory_space=pltpu.SMEM)
+HBM = pl.BlockSpec(memory_space=pl.ANY)
 
 
 def core_swap(value):
@@ -122,72 +123,85 @@
     return reduce(jnp.concatenate([total[None], value.reshape(rows // 8, 8, lanes)]), axis=0)
 
 
+def limits_kernel(docs_ref, info_ref):
+    rows = info_ref.shape[0] * ROWS
+    first = lax.axis_index("dp") * rows
+    window_first = first - SPAN * rows
+    info_ref[...] = jnp.zeros_like(info_ref)
+    for part in range(rows // ROWS):
+        chunk_low, chunk_high, low, high = chunk_range(
+            first + part * ROWS, window_first, docs_ref
+        )
+        info_ref[part, 0:1] = low - window_first
+        info_ref[part, 1:2] = high - window_first
+        info_ref[part, 2:3] = jnp.zeros_like(low) + chunk_low
+        info_ref[part, 3:4] = jnp.zeros_like(low) + (chunk_high - chunk_low)
+
+
+def by_count(count, most, body):
+    for n in range(1, most + 1):
+
+        @pl.when(count == n)
+        def _():
+            body(n)
+
+
 def weights_kernel(
-    docs_ref, queries_ref, grads_ref, key_ref, r1, r2, r3, s1, s2, s3,
-    range_ref, probs_ref, window_ref, own_ref, mine_ref, give_ref,
-    score_ref, peak_ref, sum_ref, total_ref,
+    info_ref, queries_ref, grads_ref, key_ref, r1, r2, r3, s1, s2, s3,
+    probs_ref, window_ref, own_ref, mine_ref, give_ref,
+    score_ref, total_ref,
 ):
     rows = key_ref.shape[0]
     stack = queries_ref.shape[1]
-    me, core = lax.axis_index("dp"), lax.axis_index("fsdp")
-    window_first = (me - SPAN) * rows
+    core = lax.axis_index("fsdp")
     place_window(
         core, window_ref, key_ref[...], (r1[...], r2[...], r3[...]), (s1[...], s2[...], s3[...])
     )
     total_ref[...] = jnp.zeros_like(total_ref)
     power = math.log2(math.e) / math.sqrt(128.0)
     index = lax.broadcasted_iota(jnp.int32, (CHUNK, ROWS), 0)
+
+    def part_step(part):
+        chunk_low = info_ref[part, 2:3][0, 0]
+        low = info_ref[part, 0:1] - chunk_low * CHUNK
+        high = info_ref[part, 1:2] - chunk_low * CHUNK
+
+        def chunks(count):
+            peak = jnp.full((8, stack), NEGATIVE, F32)
+            for i in range(count):
+                scores = nt_dot(window_ref[at_block(chunk_low + i, CHUNK), :], queries_ref[part])
+                place = index + i * CHUNK
+                seen = (place >= low) & (place < high)
+                seen = jnp.concatenate([seen] * (stack // ROWS), axis=1)
+                masked = jnp.where(seen, scores, NEGATIVE)
+                score_ref[i] = masked
+                peak = fold(peak, masked, jnp.max)
+            peak = jnp.max(peak, axis=0, keepdims=True)
+            total = jnp.zeros((8, stack), F32)
+            for i in range(count):
+                probs = jnp.exp2((score_ref[i] - peak) * power)
+                score_ref[i] = probs
+                total = fold(total, probs, jnp.sum)
+            inverse = 1.0 / jnp.sum(total, axis=0, keepdims=True)
+            for i in range(count):
+                probs = (score_ref[i] * inverse).astype(BF16)
+                probs_ref[part, i] = probs
+                total_ref[at_block(chunk_low + i, CHUNK), :] += jnp.dot(
+                    probs, grads_ref[part], preferred_element_type=F32
+                )
+
+        by_count(info_ref[part, 3:4][0, 0], probs_ref.shape[1], chunks)
+
     for part in range(rows // ROWS):
-        chunk_low, chunk_high, low, high = chunk_range(
-            me * rows + part * ROWS, window_first, docs_ref
-        )
-        range_ref[2 * part] = chunk_low
-        range_ref[2 * part + 1] = chunk_high
-        low = low - window_first
-        high = high - window_first
-        peak_ref[...] = jnp.full_like(peak_ref, NEGATIVE)
-        sum_ref[...] = jnp.zeros_like(sum_ref)
-
-        def score_step(chunk, _):
-            keys = window_ref[at_block(chunk, CHUNK), :]
-            scores = nt_dot(keys, queries_ref[part])
-            place = index + chunk * CHUNK
-            seen = (place >= low) & (place < high)
-            for h in range(0, stack, ROWS):
-                masked = jnp.where(seen, scores[:, h : h + ROWS], NEGATIVE)
-                score_ref[chunk, :, h : h + ROWS] = masked
-                peak_ref[:, h : h + ROWS] = fold(peak_ref[:, h : h + ROWS], masked, jnp.max)
-            return 0
-
-        lax.fori_loop(chunk_low, chunk_high, score_step, 0)
-        peak = jnp.max(peak_ref[...], axis=0, keepdims=True)
-
-        def exp_step(chunk, _):
-            probs = jnp.exp2((score_ref[chunk] - peak) * power)
-            score_ref[chunk] = probs
-            sum_ref[...] = fold(sum_ref[...], probs, jnp.sum)
-            return 0
-
-        lax.fori_loop(chunk_low, chunk_high, exp_step, 0)
-        inverse = 1.0 / jnp.sum(sum_ref[...], axis=0, keepdims=True)
-
-        def value_step(chunk, _):
-            probs = (score_ref[chunk] * inverse).astype(BF16)
-            probs_ref[part, chunk] = probs
-            total_ref[at_block(chunk, CHUNK), :] += jnp.dot(
-                probs, grads_ref[part], preferred_element_type=F32
-            )
-            return 0
-
-        lax.fori_loop(chunk_low, chunk_high, value_step, 0)
+        part_step(part)
     give_out(core, total_ref, own_ref, mine_ref, give_ref, 1.0)
 
 
 def scores_kernel(
-    range_ref, queries_ref, grads_ref, probs_ref, keys_ref, value_ref,
+    info_ref, queries_ref, grads_ref, probs_ref, keys_ref, value_ref,
     r1, r2, r3, s1, s2, s3,
-    grad_q_ref, own_ref, mine_ref, give_ref,
-    values_ref, product_ref, delta_ref, query_ref, total_ref,
+    query_ref, own_ref, mine_ref, give_ref,
+    values_ref, product_ref, total_ref,
 ):
     rows = value_ref.shape[0]
     stack = queries_ref.shape[1]
@@ -195,33 +209,29 @@
     place_window(core, values_ref, value_ref[...], (r1[0], r2[0], r3[0]), (s1[0], s2[0], s3[0]))
     total_ref[...] = jnp.zeros_like(total_ref)
     scaling = 1.0 / math.sqrt(128.0)
-    for part in range(rows // ROWS):
-        chunk_low, chunk_high = range_ref[2 * part], range_ref[2 * part + 1]
-        delta_ref[...] = jnp.zeros_like(delta_ref)
-        query_ref[...] = jnp.zeros_like(query_ref)
-
-        def delta_step(chunk, _):
-            product = nt_dot(values_ref[at_block(chunk, CHUNK), :], grads_ref[part])
-            product_ref[chunk] = product
-            terms = product * probs_ref[part, chunk].astype(F32)
-            delta_ref[...] = fold(delta_ref[...], terms, jnp.sum)
-            return 0
-
-        lax.fori_loop(chunk_low, chunk_high, delta_step, 0)
-        delta = jnp.sum(delta_ref[...], axis=0, keepdims=True)
-
-        def grad_step(chunk, _):
-            at = at_block(chunk, CHUNK)
-            grad = (probs_ref[part, chunk].astype(F32) * (product_ref[chunk] - delta)).astype(BF16)
-            total_ref[at, :] += jnp.dot(grad, queries_ref[part], preferred_element_type=F32)
-            query_ref[...] += tn_dot(keys_ref[at, :], grad)
-            return 0
-
-        lax.fori_loop(chunk_low, chunk_high, grad_step, 0)
-        for h in range(0, stack, ROWS):
-            grad_q_ref[part * ROWS : (part + 1) * ROWS, h : h + ROWS] = (
-                (query_ref[:, h : h + ROWS] * scaling).T.astype(BF16)
-            )
+
+    def part_step(part, _):
+        chunk_low = info_ref[part, 2:3][0, 0]
+
+        def chunks(count):
+            delta = jnp.zeros((8, stack), F32)
+            for i in range(count):
+                product = nt_dot(values_ref[at_block(chunk_low + i, CHUNK), :], grads_ref[part])
+                product_ref[i] = product
+                delta = fold(delta, product * probs_ref[part, i].astype(F32), jnp.sum)
+            delta = jnp.sum(delta, axis=0, keepdims=True)
+            query = jnp.zeros(query_ref.shape[1:], F32)
+            for i in range(count):
+                at = at_block(chunk_low + i, CHUNK)
+                grad = (probs_ref[part, i].astype(F32) * (product_ref[i] - delta)).astype(BF16)
+                total_ref[at, :] += jnp.dot(grad, queries_ref[part], preferred_element_type=F32)
+                query += tn_dot(keys_ref[at, :], grad)
+            query_ref[part] = query * scaling
+
+        by_count(info_ref[part, 3:4][0, 0], probs_ref.shape[1], chunks)
+        return 0
+
+    lax.fori_loop(0, rows // ROWS, part_step, 0)
     give_out(core, total_ref, own_ref, mine_ref, give_ref, scaling)
 
 
@@ -271,11 +281,34 @@
         outs[4 + k][...] = rows.astype(BF16)
 
 
+def finish_kernel(grad_ref, weight_ref, query_ref, out_hbm, query_hbm, out_ref, turned_ref, sems):
+    copies = []
+    for part in range(query_ref.shape[0]):
+        for h in range(0, query_ref.shape[2], ROWS):
+            turned_ref[part * ROWS : (part + 1) * ROWS, h : h + ROWS] = (
+                query_ref[part, :, h : h + ROWS].T.astype(BF16)
+            )
+    copies.append(pltpu.make_async_copy(turned_ref, query_hbm, sems.at[8]))
+    copies[-1].start()
+    step = out_ref.shape[1] // 8
+    for i in range(8):
+        cut = slice(i * step, (i + 1) * step)
+        out_ref[:, cut] = jnp.dot(
+            grad_ref[...], weight_ref[:, cut], preferred_element_type=F32
+        ).astype(BF16)
+        copies.append(
+            pltpu.make_async_copy(out_ref.at[:, cut], out_hbm.at[:, cut], sems.at[i])
+        )
+        copies[-1].start()
+    for copy in copies:
+        copy.wait()
+
+
 def call(kernel, outs, scratch, limit_mib, smem, *args):
     return pl.pallas_call(
         kernel,
         in_specs=[SMEM] * smem + [VMEM] * (len(args) - smem),
-        out_specs=[SMEM if len(shape) == 1 else VMEM for shape, _ in outs],
+        out_specs=[HBM if kernel is finish_kernel else VMEM for _ in outs],
         out_shape=[jax.ShapeDtypeStruct(shape, kind) for shape, kind in outs],
         scratch_shapes=scratch,
         compiler_params=pltpu.CompilerParams(vmem_limit_bytes=limit_mib << 20),
@@ -297,20 +330,24 @@
     direct = dp == 8
     steps = range(SPAN)
 
-    docs = jnp.concatenate([doc_lengths, prefix_spans])
+    (info,) = call(
+        limits_kernel,
+        [((parts, 8, ROWS), jnp.int32)],
+        [], 4, 1,
+        jnp.concatenate([doc_lengths, prefix_spans]),
+    )
     query_stack = stack_heads(queries, head)
     grad_stack = stack_heads(grad_out, head)
     mine = [fan_out(keys, k) for k in steps]
-    other = [core_swap(after(block, docs, query_stack, grad_stack)) for block in mine]
+    other = [core_swap(after(block, info, query_stack, grad_stack)) for block in mine]
     if direct:
         weight = after(weight, mine[0])
         z3, z2, z1 = (dp_swap(weight, 2 * k) for k in (3, 2, 1))
         cross0 = dp_swap(weight, 1)
 
-    ranges, probs, key_window, own_v, mine_v, give_v = call(
+    probs, key_window, own_v, mine_v, give_v = call(
         weights_kernel,
         [
-            ((2 * parts,), jnp.int32),
             ((parts, chunks, CHUNK, stack), BF16),
             ((window, head), BF16),
             ((rows, head), F32),
@@ -319,12 +356,10 @@
         ],
         [
             pltpu.VMEM((chunks, CHUNK, stack), F32),
-            pltpu.VMEM((8, stack), F32),
-            pltpu.VMEM((8, stack), F32),
             pltpu.VMEM((window, head), F32),
         ],
-        20, 1,
-        docs, query_stack, grad_stack, keys, *mine, *other,
+        20, 0,
+        info, query_stack, grad_stack, keys, *mine, *other,
     )
     got_v = core_swap(give_v)
     other_v = core_swap(own_v)
@@ -370,10 +405,10 @@
         grad_weight = lax.psum_scatter(
             tn_dot(grad_value, layer_input), "dp", scatter_dimension=0, tiled=True
         ).T
-    grad_queries, own_k, mine_k, give_k = call(
+    grad_stack_q, own_k, mine_k, give_k = call(
         scores_kernel,
         [
-            ((rows, heads * head), BF16),
+            ((parts, head, stack), F32),
             ((rows, head), F32),
             ((SPAN, rows, head), F32),
             ((SPAN, rows, head), BF16),
@@ -381,21 +416,27 @@
         [
             pltpu.VMEM((window, head), BF16),
             pltpu.VMEM((chunks, CHUNK, stack), F32),
-            pltpu.VMEM((8, stack), F32),
-            pltpu.VMEM((head, stack), F32),
             pltpu.VMEM((window, head), F32),
         ],
-        20, 1,
-        after(ranges, grad_value), query_stack, grad_stack, probs, key_window, value, *mine, *other,
+        20, 0,
+        after(info, grad_value), query_stack, grad_stack, probs, key_window, value, *mine, *other,
     )
     got_k = core_swap(give_k)
     mine = [
         fan_out((mine_k[k] + got_k[k].astype(F32)).astype(BF16), k) for k in steps
     ]
     other = [core_swap(block) for block in mine]
-    grad_input = jnp.dot(
-        grad_value, full_weight, preferred_element_type=F32
-    ).astype(BF16)
+    grad_input, grad_queries = call(
+        finish_kernel,
+        [((rows, depth), BF16), ((rows, heads * head), BF16)],
+        [
+            pltpu.VMEM((rows, depth), BF16),
+            pltpu.VMEM((rows, heads * head), BF16),
+            pltpu.SemaphoreType.DMA((9,)),
+        ],
+        12, 0,
+        grad_value, full_weight, grad_stack_q,
+    )
     grad_keys = sum_blocks(own_k, core_swap(own_k), mine, other).astype(BF16)
     return (grad_input, grad_queries, grad_keys, grad_weight)
 

time: 80.6 us -> 78.9 us (0.979)
  the two profiles are of different devices: /device:TPU:0 before, /device:TPU:11 now
where the time goes in v2:
time: 78.9 us; the launch traced here: 78.6 us
  starting transfers between devices  54.9 us (70%)
  waiting for transfers between devices  11.5 us (15%)
  Pallas kernels  8.71 us (11%)
  other arithmetic  2.34 us (3%)
  between operations  0.92 us (1%)
    ppermute x9, starting transfers between devices, fan_out(): lax.ppermute(value, BOTH, [(i, j) for i, j in pairs if 0 <= j < 2 * count])  25.2 us
    ppermute x14, starting transfers between devices, core_swap(): return lax.ppermute(value, 'fsdp', [(0, 1), (1, 0)])  17.3 us
    ppermute x14, starting transfers between devices, dp_swap(): return lax.ppermute(value, 'dp', [(i, i ^ mask) for i in range(count)])  12.4 us
    pallas_call x7, Pallas kernels, call(): pl.pallas_call(kernel, in_specs=[SMEM] * smem + [VMEM] * (len(args) - sme...  8.71 us
    ppermute x14, waiting for transfers between devices, dp_swap(): return lax.ppermute(value, 'dp', [(i, i ^ mask) for i in range(count)])  7.04 us
    ppermute x14, waiting for transfers between devices, core_swap(): return lax.ppermute(value, 'fsdp', [(0, 1), (1, 0)])  2.9 us
    ppermute x9, waiting for transfers between devices, fan_out(): lax.ppermute(value, BOTH, [(i, j) for i, j in pairs if 0 <= j < 2 * count])  1.58 us
  transfers between devices with their start and end apart: 37, of which 10 were waited for; matrix products, arithmetic and copies ran while one was open for 2% of the time, Pallas kernels for 10%

profile of v2, /device:TPU:11, one launch (start us, length us, event | category | flops | bytes accessed | tf_op | source)
XLA Modules:
  0.0 78.6 jit_solution(9024998699748257359)
XLA Ops:
  0.6 2.1 %collective-permute-start = (bf16[256,128]{1,0:T(8,128)(2,1)}, bf16[256,128]{1,0:T(8,128)(2,1)S(1)}, u32[]{:S(2)}, u32[]{:S(2)}) collective-permute-start(bf16[256,128]{1,0:T(8,128)(2,1)} %key_ref.1), channel_id=1, source_target_pairs={{2,8},{5,3},{6,12},{7,1},{8,2},{9,7},{11,5},{12,6},{13,11},{15,9},... | collective-permute-start | bytes 196616 | tf_op jit(solution)/shard_map/ppermute | solution.py:46
  2.7 4.3 %collective-permute-start.1 = (bf16[256,128]{1,0:T(8,128)(2,1)}, bf16[256,128]{1,0:T(8,128)(2,1)S(1)}, u32[]{:S(2)}, u32[]{:S(2)}) collective-permute-start(bf16[256,128]{1,0:T(8,128)(2,1)} %key_ref.1), channel_id=1, source_target_pairs={{1,7},{3,5},{4,0},{5,11},{6,2},{7,9},{8,4},{9,15},{10,6},{11,13},{... | collective-permute-start | bytes 196616 | tf_op jit(solution)/shard_map/ppermute | solution.py:46
  7.0 2.2 %collective-permute-start.2 = (bf16[256,128]{1,0:T(8,128)(2,1)}, bf16[256,128]{1,0:T(8,128)(2,1)S(1)}, u32[]{:S(2)}, u32[]{:S(2)}) collective-permute-start(bf16[256,128]{1,0:T(8,128)(2,1)} %key_ref.1), channel_id=1, source_target_pairs={{0,4},{1,3},{2,6},{3,1},{4,8},{5,7},{6,10},{7,5},{8,12},{9,11},{10... | collective-permute-start | bytes 196616 | tf_op jit(solution)/shard_map/ppermute | solution.py:46
  10.0 2.4 %collective-permute-start.8 = (bf16[16,4096]{1,0:T(8,128)(2,1)}, bf16[16,4096]{1,0:T(8,128)(2,1)S(1)}, u32[]{:S(2)}, u32[]{:S(2)}) collective-permute-start(bf16[16,4096]{1,0:T(8,128)(2,1)} %bitcast.20), channel_id=1, source_target_pairs={{0,8},{2,10},{4,12},{6,14},{8,0},{10,2},{12,4},{14,6},{1,9},{3,11}... | collective-permute-start | bytes 393224 | tf_op jit(solution)/shard_map/ppermute | solution.py:28
  13.5 3.5 %collective-permute-start.3 = (bf16[256,128]{1,0:T(8,128)(2,1)S(1)}, bf16[256,128]{1,0:T(8,128)(2,1)S(1)}, u32[]{:S(2)}, u32[]{:S(2)}) collective-permute-start(bf16[256,128]{1,0:T(8,128)(2,1)S(1)} %collective-permute-done.r1), channel_id=1, source_target_pairs={{0,1},{1,0},{2,3},{3,2},{4,5},{5,4},{6,7},{7,6},{8,9},{9,8},{10,11... | collective-permute-start | bytes 196616 | tf_op jit(solution)/shard_map/ppermute | solution.py:23
  17.1 0.8 %collective-permute-done.3.s1 = bf16[256,128]{1,0:T(8,128)(2,1)S(1)} collective-permute-done((bf16[256,128]{1,0:T(8,128)(2,1)S(1)}, bf16[256,128]{1,0:T(8,128)(2,1)S(1)}, u32[]{:S(2)}, u32[]{:S(2)}) %collective-permute-start.3) | collective-permute-done | bytes 65568 | tf_op jit(solution)/shard_map/ppermute | solution.py:23
  18.3 1.5 %collective-permute-start.11 = (bf16[16,4096]{1,0:T(8,128)(2,1)S(1)}, bf16[16,4096]{1,0:T(8,128)(2,1)S(1)}, u32[]{:S(2)}, u32[]{:S(2)}) collective-permute-start(bf16[16,4096]{1,0:T(8,128)(2,1)S(1)} %collective-permute-done.7.z1), channel_id=1, source_target_pairs={{0,2},{2,0},{4,6},{6,4},{8,10},{10,8},{12,14},{14,12},{1,3},{3,1},... | collective-permute-start | bytes 393224 | tf_op jit(solution)/shard_map/ppermute | solution.py:28
  20.0 4.0 %collective-permute-done.9.z3 = bf16[16,4096]{1,0:T(8,128)(2,1)S(1)} collective-permute-done((bf16[16,4096]{1,0:T(8,128)(2,1)}, bf16[16,4096]{1,0:T(8,128)(2,1)S(1)}, u32[]{:S(2)}, u32[]{:S(2)}) %collective-permute-start.9) | collective-permute-done | bytes 131104 | tf_op jit(solution)/shard_map/ppermute | solution.py:28
  23.9 2.0 %collective-permute-start.13 = (bf16[16,4096]{1,0:T(8,128)(2,1)S(1)}, bf16[16,4096]{1,0:T(8,128)(2,1)S(1)}, u32[]{:S(2)}, u32[]{:S(2)}) collective-permute-start(bf16[16,4096]{1,0:T(8,128)(2,1)S(1)} %collective-permute-done.9.z3), channel_id=1, source_target_pairs={{0,2},{2,0},{4,6},{6,4},{8,10},{10,8},{12,14},{14,12},{1,3},{3,1},... | collective-permute-start | bytes 393224 | tf_op jit(solution)/shard_map/ppermute | solution.py:28
  25.9 2.7 %shard_map.103 = (bf16[2,7,256,512]{3,2,1,0:T(8,128)(2,1)S(1)}, bf16[1792,128]{1,0:T(8,128)(2,1)S(1)}, f32[256,128]{1,0:T(8,128)S(1)}, f32[3,256,128]{2,1,0:T(8,128)S(1)}, bf16[3,256,128]{2,1,0:T(8,128)(2,1)S(1)}) custom-call(s32[2,8,128]{2,1,0:T(8,128)S(1)} %shard_map.102.info_ref, bf16[2,512,128]{2,1,0:T(8,128)(2,1)S(1)} %bitcast.15, ...), custom_call_target="tpu_custom_call" | custom-call | flops 1073741824 | bytes 4194304 | tf_op jit(solution)/shard_map/pallas_call | solution.py:308
  28.7 1.4 %collective-permute-start.15 = (bf16[3,256,128]{2,1,0:T(8,128)(2,1)S(1)}, bf16[3,256,128]{2,1,0:T(8,128)(2,1)S(1)}, u32[]{:S(2)}, u32[]{:S(2)}) collective-permute-start(bf16[3,256,128]{2,1,0:T(8,128)(2,1)S(1)} %get-tuple-element.42), channel_id=1, source_target_pairs={{0,1},{1,0},{2,3},{3,2},{4,5},{5,4},{6,7},{7,6},{8,9},{9,8},{10,11... | collective-permute-start | bytes 589832 | tf_op jit(solution)/shard_map/ppermute | solution.py:23
  30.1 1.6 %collective-permute-done.13.c3 = bf16[16,4096]{1,0:T(8,128)(2,1)S(1)} collective-permute-done((bf16[16,4096]{1,0:T(8,128)(2,1)S(1)}, bf16[16,4096]{1,0:T(8,128)(2,1)S(1)}, u32[]{:S(2)}, u32[]{:S(2)}) %collective-permute-start.13) | collective-permute-done | bytes 131104 | tf_op jit(solution)/shard_map/ppermute | solution.py:28
  32.5 1.0 %collective-permute-start.14 = (f32[256,128]{1,0:T(8,128)S(1)}, f32[256,128]{1,0:T(8,128)S(1)}, u32[]{:S(2)}, u32[]{:S(2)}) collective-permute-start(f32[256,128]{1,0:T(8,128)S(1)} %get-tuple-element.40.half_ref), channel_id=1, source_target_pairs={{0,1},{1,0},{2,3},{3,2},{4,5},{5,4},{6,7},{7,6},{8,9},{9,8},{10,11... | collective-permute-start | bytes 393224 | tf_op jit(solution)/shard_map/ppermute | solution.py:23
  33.5 1.0 %collective-permute-done.14.other_ref = f32[256,128]{1,0:T(8,128)S(1)} collective-permute-done((f32[256,128]{1,0:T(8,128)S(1)}, f32[256,128]{1,0:T(8,128)S(1)}, u32[]{:S(2)}, u32[]{:S(2)}) %collective-permute-start.14) | collective-permute-done | bytes 131104 | tf_op jit(solution)/shard_map/ppermute | solution.py:23
  34.5 2.7 %collective-permute-start.16 = (bf16[2,256,128]{2,1,0:T(8,128)(2,1)S(1)}, bf16[2,256,128]{2,1,0:T(8,128)(2,1)S(1)}, u32[]{:S(2)}, u32[]{:S(2)}) collective-permute-start(bf16[2,256,128]{2,1,0:T(8,128)(2,1)S(1)} %get-tuple-element.43), channel_id=1, source_target_pairs={{2,8},{5,3},{6,12},{7,1},{8,2},{9,7},{11,5},{12,6},{13,11},{15,9},... | collective-permute-start | bytes 393224 | tf_op jit(solution)/shard_map/ppermute | solution.py:46
  37.2 3.5 %collective-permute-start.17 = (bf16[2,256,128]{2,1,0:T(8,128)(2,1)S(1)}, bf16[2,256,128]{2,1,0:T(8,128)(2,1)S(1)}, u32[]{:S(2)}, u32[]{:S(2)}) collective-permute-start(bf16[2,256,128]{2,1,0:T(8,128)(2,1)S(1)} %get-tuple-element.44), channel_id=1, source_target_pairs={{1,7},{3,5},{4,0},{5,11},{6,2},{7,9},{8,4},{9,15},{10,6},{11,13},{... | collective-permute-start | bytes 393224 | tf_op jit(solution)/shard_map/ppermute | solution.py:46
  40.7 2.1 %collective-permute-start.18 = (bf16[2,256,128]{2,1,0:T(8,128)(2,1)S(1)}, bf16[2,256,128]{2,1,0:T(8,128)(2,1)S(1)}, u32[]{:S(2)}, u32[]{:S(2)}) collective-permute-start(bf16[2,256,128]{2,1,0:T(8,128)(2,1)S(1)} %get-tuple-element.45), channel_id=1, source_target_pairs={{0,4},{1,3},{2,6},{3,1},{4,8},{5,7},{6,10},{7,5},{8,12},{9,11},{10... | collective-permute-start | bytes 393224 | tf_op jit(solution)/shard_map/ppermute | solution.py:46
  42.9 1.6 %collective-permute-start.6 = (f32[256,128]{1,0:T(8,128)S(1)}, f32[256,128]{1,0:T(8,128)S(1)}, u32[]{:S(2)}, u32[]{:S(2)}) collective-permute-start(f32[256,128]{1,0:T(8,128)S(1)} %get-tuple-element.38.a_ref), channel_id=1, source_target_pairs={{0,1},{1,0},{2,3},{3,2},{4,5},{5,4},{6,7},{7,6},{8,9},{9,8},{10,11... | collective-permute-start | bytes 393224 | tf_op jit(solution)/shard_map/ppermute | solution.py:23
  45.2 1.6 %collective-permute-done.18.r3 = bf16[2,256,128]{2,1,0:T(8,128)(2,1)S(1)} collective-permute-done((bf16[2,256,128]{2,1,0:T(8,128)(2,1)S(1)}, bf16[2,256,128]{2,1,0:T(8,128)(2,1)S(1)}, u32[]{:S(2)}, u32[]{:S(2)}) %collective-permute-start.18) | collective-permute-done | bytes 131104 | tf_op jit(solution)/shard_map/ppermute | solution.py:46
  46.7 0.9 %collective-permute-start.21 = (bf16[2,256,128]{2,1,0:T(8,128)(2,1)S(1)}, bf16[2,256,128]{2,1,0:T(8,128)(2,1)S(1)}, u32[]{:S(2)}, u32[]{:S(2)}) collective-permute-start(bf16[2,256,128]{2,1,0:T(8,128)(2,1)S(1)} %collective-permute-done.18.r3), channel_id=1, source_target_pairs={{0,1},{1,0},{2,3},{3,2},{4,5},{5,4},{6,7},{7,6},{8,9},{9,8},{10,11... | collective-permute-start | bytes 393224 | tf_op jit(solution)/shard_map/ppermute | solution.py:23
  47.7 1.0 %collective-permute-done.21.s3 = bf16[2,256,128]{2,1,0:T(8,128)(2,1)S(1)} collective-permute-done((bf16[2,256,128]{2,1,0:T(8,128)(2,1)S(1)}, bf16[2,256,128]{2,1,0:T(8,128)(2,1)S(1)}, u32[]{:S(2)}, u32[]{:S(2)}) %collective-permute-start.21) | collective-permute-done | bytes 131104 | tf_op jit(solution)/shard_map/ppermute | solution.py:23
  49.4 1.5 %collective-permute-start.32 = (bf16[16,4096]{1,0:T(8,128)(2,1)S(1)}, bf16[16,4096]{1,0:T(8,128)(2,1)S(1)}, u32[]{:S(2)}, u32[]{:S(2)}) collective-permute-start(bf16[16,4096]{1,0:T(8,128)(2,1)S(1)} %get-tuple-element.62), channel_id=1, source_target_pairs={{0,2},{2,0},{4,6},{6,4},{8,10},{10,8},{12,14},{14,12},{1,3},{3,1},... | collective-permute-start | bytes 393224 | tf_op jit(solution)/shard_map/ppermute | solution.py:28
  50.9 1.4 %collective-permute-start.36 = (bf16[16,4096]{1,0:T(8,128)(2,1)S(1)}, bf16[16,4096]{1,0:T(8,128)(2,1)S(1)}, u32[]{:S(2)}, u32[]{:S(2)}) collective-permute-start(bf16[16,4096]{1,0:T(8,128)(2,1)S(1)} %get-tuple-element.65), channel_id=1, source_target_pairs={{0,2},{2,0},{4,6},{6,4},{8,10},{10,8},{12,14},{14,12},{1,3},{3,1},... | collective-permute-start | bytes 393224 | tf_op jit(solution)/shard_map/ppermute | solution.py:28
  52.3 2.2 %shard_map.107 = (f32[2,128,512]{2,1,0:T(8,128)S(1)}, f32[256,128]{1,0:T(8,128)S(1)}, f32[3,256,128]{2,1,0:T(8,128)S(1)}, bf16[3,256,128]{2,1,0:T(8,128)(2,1)S(1)}) custom-call(s32[2,8,128]{2,1,0:T(8,128)S(1)} %shard_map.102.info_ref, bf16[2,512,128]{2,1,0:T(8,128)(2,1)S(1)} %bitcast.16, bf16[2,512,128]{2,1,0:T(8,128)(2,1)S(1)} %bitcast.18, ...), custom_call_target="tpu_custom_call" | custom-call | flops 1073741824 | bytes 4194304 | tf_op jit(solution)/shard_map/pallas_call | solution.py:308
  54.5 1.5 %collective-permute-start.23 = (bf16[3,256,128]{2,1,0:T(8,128)(2,1)S(1)}, bf16[3,256,128]{2,1,0:T(8,128)(2,1)S(1)}, u32[]{:S(2)}, u32[]{:S(2)}) collective-permute-start(bf16[3,256,128]{2,1,0:T(8,128)(2,1)S(1)} %get-tuple-element.57), channel_id=1, source_target_pairs={{0,1},{1,0},{2,3},{3,2},{4,5},{5,4},{6,7},{7,6},{8,9},{9,8},{10,11... | collective-permute-start | bytes 589832 | tf_op jit(solution)/shard_map/ppermute | solution.py:23
  56.9 2.1 %collective-permute-start.33 = (bf16[16,4096]{1,0:T(8,128)(2,1)S(1)}, bf16[16,4096]{1,0:T(8,128)(2,1)S(1)}, u32[]{:S(2)}, u32[]{:S(2)}) collective-permute-start(bf16[16,4096]{1,0:T(8,128)(2,1)S(1)} %add_convert_fusion.1), channel_id=1, source_target_pairs={{0,8},{2,10},{4,12},{6,14},{8,0},{10,2},{12,4},{14,6},{1,9},{3,11}... | collective-permute-start | bytes 393224 | tf_op jit(solution)/shard_map/ppermute | solution.py:28
  60.3 3.1 %collective-permute-start.24 = (bf16[256,128]{1,0:T(8,128)(2,1)S(1)}, bf16[256,128]{1,0:T(8,128)(2,1)S(1)}, u32[]{:S(2)}, u32[]{:S(2)}) collective-permute-start(bf16[256,128]{1,0:T(8,128)(2,1)S(1)} %get-tuple-element.66), channel_id=1, source_target_pairs={{2,8},{5,3},{6,12},{7,1},{8,2},{9,7},{11,5},{12,6},{13,11},{15,9},... | collective-permute-start | bytes 196616 | tf_op jit(solution)/shard_map/ppermute | solution.py:46
  63.4 3.4 %collective-permute-start.26 = (bf16[256,128]{1,0:T(8,128)(2,1)S(1)}, bf16[256,128]{1,0:T(8,128)(2,1)S(1)}, u32[]{:S(2)}, u32[]{:S(2)}) collective-permute-start(bf16[256,128]{1,0:T(8,128)(2,1)S(1)} %get-tuple-element.68), channel_id=1, source_target_pairs={{1,7},{3,5},{4,0},{5,11},{6,2},{7,9},{8,4},{9,15},{10,6},{11,13},{... | collective-permute-start | bytes 196616 | tf_op jit(solution)/shard_map/ppermute | solution.py:46
  67.2 1.9 %collective-permute-start.28 = (bf16[256,128]{1,0:T(8,128)(2,1)S(1)}, bf16[256,128]{1,0:T(8,128)(2,1)S(1)}, u32[]{:S(2)}, u32[]{:S(2)}) collective-permute-start(bf16[256,128]{1,0:T(8,128)(2,1)S(1)} %get-tuple-element.67), channel_id=1, source_target_pairs={{0,4},{1,3},{2,6},{3,1},{4,8},{5,7},{6,10},{7,5},{8,12},{9,11},{10... | collective-permute-start | bytes 196616 | tf_op jit(solution)/shard_map/ppermute | solution.py:46
  69.1 1.7 %shard_map.108 = (bf16[256,4096]{1,0:T(8,128)(2,1)}, bf16[256,512]{1,0:T(8,128)(2,1)}) custom-call(bf16[256,128]{1,0:T(8,128)(2,1)S(1)} %get-tuple-element.46.grad_ref, bf16[128,4096]{1,0:T(8,128)(2,1)S(1)} %get-tuple-element.47.weight_ref, f32[2,128,512]{2,1,0:T(8,128)S(1)} %get-tuple-element.52.query_ref), custom_call_target="tpu_custom_call" | custom-call | flops 1073741824 | bytes 4194304 | tf_op jit(solution)/shard_map/pallas_call | solution.py:308
  70.8 3.7 %collective-permute-start.22 = (f32[256,128]{1,0:T(8,128)S(1)}, f32[256,128]{1,0:T(8,128)S(1)}, u32[]{:S(2)}, u32[]{:S(2)}) collective-permute-start(f32[256,128]{1,0:T(8,128)S(1)} %get-tuple-element.55), channel_id=1, source_target_pairs={{0,1},{1,0},{2,3},{3,2},{4,5},{5,4},{6,7},{7,6},{8,9},{9,8},{10,11... | collective-permute-start | bytes 393224 | tf_op jit(solution)/shard_map/ppermute | solution.py:23
  75.0 1.9 %collective-permute-start.29 = (bf16[256,128]{1,0:T(8,128)(2,1)S(1)}, bf16[256,128]{1,0:T(8,128)(2,1)S(1)}, u32[]{:S(2)}, u32[]{:S(2)}) collective-permute-start(bf16[256,128]{1,0:T(8,128)(2,1)S(1)} %collective-permute-done.28), channel_id=1, source_target_pairs={{0,1},{1,0},{2,3},{3,2},{4,5},{5,4},{6,7},{7,6},{8,9},{9,8},{10,11... | collective-permute-start | bytes 196616 | tf_op jit(solution)/shard_map/ppermute | solution.py:23
  (70 shorter events, 9.5 us)
Async XLA Ops:
  0.6 9.3 %collective-permute-start = (bf16[256,128]{1,0:T(8,128)(2,1)}, bf16[256,128]{1,0:T(8,128)(2,1)S(1)}, u32[]{:S(2)}, u32[]{:S(2)}) collective-permute-start(bf16[256,128]{1,0:T(8,128)(2,1)} %key_ref.1), channel_id=1, source_target_pairs={{2,8},{5,3},{6,12},{7,1},{8,2},{9,7},{11,5},{12,6},{13,11},{15,9},... | collective-permute-start | bytes 196616 | tf_op jit(solution)/shard_map/ppermute | solution.py:46
  2.7 10.8 %collective-permute-start.1 = (bf16[256,128]{1,0:T(8,128)(2,1)}, bf16[256,128]{1,0:T(8,128)(2,1)S(1)}, u32[]{:S(2)}, u32[]{:S(2)}) collective-permute-start(bf16[256,128]{1,0:T(8,128)(2,1)} %key_ref.1), channel_id=1, source_target_pairs={{1,7},{3,5},{4,0},{5,11},{6,2},{7,9},{8,4},{9,15},{10,6},{11,13},{... | collective-permute-start | bytes 196616 | tf_op jit(solution)/shard_map/ppermute | solution.py:46
  7.0 10.1 %collective-permute-start.2 = (bf16[256,128]{1,0:T(8,128)(2,1)}, bf16[256,128]{1,0:T(8,128)(2,1)S(1)}, u32[]{:S(2)}, u32[]{:S(2)}) collective-permute-start(bf16[256,128]{1,0:T(8,128)(2,1)} %key_ref.1), channel_id=1, source_target_pairs={{0,4},{1,3},{2,6},{3,1},{4,8},{5,7},{6,10},{7,5},{8,12},{9,11},{10... | collective-permute-start | bytes 196616 | tf_op jit(solution)/shard_map/ppermute | solution.py:46
  9.9 8.4 %collective-permute-start.7 = (bf16[16,4096]{1,0:T(8,128)(2,1)}, bf16[16,4096]{1,0:T(8,128)(2,1)S(1)}, u32[]{:S(2)}, u32[]{:S(2)}) collective-permute-start(bf16[16,4096]{1,0:T(8,128)(2,1)} %bitcast.19), channel_id=1, source_target_pairs={{0,4},{2,6},{4,0},{6,2},{8,12},{10,14},{12,8},{14,10},{1,5},{3,7},... | collective-permute-start | bytes 393224 | tf_op jit(solution)/shard_map/ppermute | solution.py:28
  10.0 9.8 %collective-permute-start.8 = (bf16[16,4096]{1,0:T(8,128)(2,1)}, bf16[16,4096]{1,0:T(8,128)(2,1)S(1)}, u32[]{:S(2)}, u32[]{:S(2)}) collective-permute-start(bf16[16,4096]{1,0:T(8,128)(2,1)} %bitcast.20), channel_id=1, source_target_pairs={{0,8},{2,10},{4,12},{6,14},{8,0},{10,2},{12,4},{14,6},{1,9},{3,11}... | collective-permute-start | bytes 393224 | tf_op jit(solution)/shard_map/ppermute | solution.py:28
  12.5 11.5 %collective-permute-start.9 = (bf16[16,4096]{1,0:T(8,128)(2,1)}, bf16[16,4096]{1,0:T(8,128)(2,1)S(1)}, u32[]{:S(2)}, u32[]{:S(2)}) collective-permute-start(bf16[16,4096]{1,0:T(8,128)(2,1)} %bitcast.21), channel_id=1, source_target_pairs={{0,12},{2,14},{4,8},{6,10},{8,4},{10,6},{12,0},{14,2},{1,13},{3,15... | collective-permute-start | bytes 393224 | tf_op jit(solution)/shard_map/ppermute | solution.py:28
  13.5 4.5 %collective-permute-start.3 = (bf16[256,128]{1,0:T(8,128)(2,1)S(1)}, bf16[256,128]{1,0:T(8,128)(2,1)S(1)}, u32[]{:S(2)}, u32[]{:S(2)}) collective-permute-start(bf16[256,128]{1,0:T(8,128)(2,1)S(1)} %collective-permute-done.r1), channel_id=1, source_target_pairs={{0,1},{1,0},{2,3},{3,2},{4,5},{5,4},{6,7},{7,6},{8,9},{9,8},{10,11... | collective-permute-start | bytes 196616 | tf_op jit(solution)/shard_map/ppermute | solution.py:23
  17.9 8.0 %collective-permute-start.5 = (bf16[256,128]{1,0:T(8,128)(2,1)S(1)}, bf16[256,128]{1,0:T(8,128)(2,1)S(1)}, u32[]{:S(2)}, u32[]{:S(2)}) collective-permute-start(bf16[256,128]{1,0:T(8,128)(2,1)S(1)} %collective-permute-done.2.r3), channel_id=1, source_target_pairs={{0,1},{1,0},{2,3},{3,2},{4,5},{5,4},{6,7},{7,6},{8,9},{9,8},{10,11... | collective-permute-start | bytes 196616 | tf_op jit(solution)/shard_map/ppermute | solution.py:23
  18.3 11.8 %collective-permute-start.10 = (bf16[16,4096]{1,0:T(8,128)(2,1)S(1)}, bf16[16,4096]{1,0:T(8,128)(2,1)S(1)}, u32[]{:S(2)}, u32[]{:S(2)}) collective-permute-start(bf16[16,4096]{1,0:T(8,128)(2,1)S(1)} %bitcast.22), channel_id=1, source_target_pairs={{0,2},{2,0},{4,6},{6,4},{8,10},{10,8},{12,14},{14,12},{1,3},{3,1},... | collective-permute-start | bytes 393224 | tf_op jit(solution)/shard_map/ppermute | solution.py:28
  18.3 11.8 %collective-permute-start.11 = (bf16[16,4096]{1,0:T(8,128)(2,1)S(1)}, bf16[16,4096]{1,0:T(8,128)(2,1)S(1)}, u32[]{:S(2)}, u32[]{:S(2)}) collective-permute-start(bf16[16,4096]{1,0:T(8,128)(2,1)S(1)} %collective-permute-done.7.z1), channel_id=1, source_target_pairs={{0,2},{2,0},{4,6},{6,4},{8,10},{10,8},{12,14},{14,12},{1,3},{3,1},... | collective-permute-start | bytes 393224 | tf_op jit(solution)/shard_map/ppermute | solution.py:28
  19.8 10.3 %collective-permute-start.12 = (bf16[16,4096]{1,0:T(8,128)(2,1)S(1)}, bf16[16,4096]{1,0:T(8,128)(2,1)S(1)}, u32[]{:S(2)}, u32[]{:S(2)}) collective-permute-start(bf16[16,4096]{1,0:T(8,128)(2,1)S(1)} %collective-permute-done.8.z2), channel_id=1, source_target_pairs={{0,2},{2,0},{4,6},{6,4},{8,10},{10,8},{12,14},{14,12},{1,3},{3,1},... | collective-permute-start | bytes 393224 | tf_op jit(solution)/shard_map/ppermute | solution.py:28
  23.9 7.8 %collective-permute-start.13 = (bf16[16,4096]{1,0:T(8,128)(2,1)S(1)}, bf16[16,4096]{1,0:T(8,128)(2,1)S(1)}, u32[]{:S(2)}, u32[]{:S(2)}) collective-permute-start(bf16[16,4096]{1,0:T(8,128)(2,1)S(1)} %collective-permute-done.9.z3), channel_id=1, source_target_pairs={{0,2},{2,0},{4,6},{6,4},{8,10},{10,8},{12,14},{14,12},{1,3},{3,1},... | collective-permute-start | bytes 393224 | tf_op jit(solution)/shard_map/ppermute | solution.py:28
  28.7 4.8 %collective-permute-start.15 = (bf16[3,256,128]{2,1,0:T(8,128)(2,1)S(1)}, bf16[3,256,128]{2,1,0:T(8,128)(2,1)S(1)}, u32[]{:S(2)}, u32[]{:S(2)}) collective-permute-start(bf16[3,256,128]{2,1,0:T(8,128)(2,1)S(1)} %get-tuple-element.42), channel_id=1, source_target_pairs={{0,1},{1,0},{2,3},{3,2},{4,5},{5,4},{6,7},{7,6},{8,9},{9,8},{10,11... | collective-permute-start | bytes 589832 | tf_op jit(solution)/shard_map/ppermute | solution.py:23
  34.5 9.9 %collective-permute-start.16 = (bf16[2,256,128]{2,1,0:T(8,128)(2,1)S(1)}, bf16[2,256,128]{2,1,0:T(8,128)(2,1)S(1)}, u32[]{:S(2)}, u32[]{:S(2)}) collective-permute-start(bf16[2,256,128]{2,1,0:T(8,128)(2,1)S(1)} %get-tuple-element.43), channel_id=1, source_target_pairs={{2,8},{5,3},{6,12},{7,1},{8,2},{9,7},{11,5},{12,6},{13,11},{15,9},... | collective-permute-start | bytes 393224 | tf_op jit(solution)/shard_map/ppermute | solution.py:46
  37.2 7.3 %collective-permute-start.17 = (bf16[2,256,128]{2,1,0:T(8,128)(2,1)S(1)}, bf16[2,256,128]{2,1,0:T(8,128)(2,1)S(1)}, u32[]{:S(2)}, u32[]{:S(2)}) collective-permute-start(bf16[2,256,128]{2,1,0:T(8,128)(2,1)S(1)} %get-tuple-element.44), channel_id=1, source_target_pairs={{1,7},{3,5},{4,0},{5,11},{6,2},{7,9},{8,4},{9,15},{10,6},{11,13},{... | collective-permute-start | bytes 393224 | tf_op jit(solution)/shard_map/ppermute | solution.py:46
  40.7 6.0 %collective-permute-start.18 = (bf16[2,256,128]{2,1,0:T(8,128)(2,1)S(1)}, bf16[2,256,128]{2,1,0:T(8,128)(2,1)S(1)}, u32[]{:S(2)}, u32[]{:S(2)}) collective-permute-start(bf16[2,256,128]{2,1,0:T(8,128)(2,1)S(1)} %get-tuple-element.45), channel_id=1, source_target_pairs={{0,4},{1,3},{2,6},{3,1},{4,8},{5,7},{6,10},{7,5},{8,12},{9,11},{10... | collective-permute-start | bytes 393224 | tf_op jit(solution)/shard_map/ppermute | solution.py:46
  42.9 4.8 %collective-permute-start.6 = (f32[256,128]{1,0:T(8,128)S(1)}, f32[256,128]{1,0:T(8,128)S(1)}, u32[]{:S(2)}, u32[]{:S(2)}) collective-permute-start(f32[256,128]{1,0:T(8,128)S(1)} %get-tuple-element.38.a_ref), channel_id=1, source_target_pairs={{0,1},{1,0},{2,3},{3,2},{4,5},{5,4},{6,7},{7,6},{8,9},{9,8},{10,11... | collective-permute-start | bytes 393224 | tf_op jit(solution)/shard_map/ppermute | solution.py:23
  44.5 3.2 %collective-permute-start.19 = (bf16[2,256,128]{2,1,0:T(8,128)(2,1)S(1)}, bf16[2,256,128]{2,1,0:T(8,128)(2,1)S(1)}, u32[]{:S(2)}, u32[]{:S(2)}) collective-permute-start(bf16[2,256,128]{2,1,0:T(8,128)(2,1)S(1)} %collective-permute-done.16.r1), channel_id=1, source_target_pairs={{0,1},{1,0},{2,3},{3,2},{4,5},{5,4},{6,7},{7,6},{8,9},{9,8},{10,11... | collective-permute-start | bytes 393224 | tf_op jit(solution)/shard_map/ppermute | solution.py:23
  49.3 6.8 %collective-permute-start.30 = (bf16[16,4096]{1,0:T(8,128)(2,1)S(1)}, bf16[16,4096]{1,0:T(8,128)(2,1)S(1)}, u32[]{:S(2)}, u32[]{:S(2)}) collective-permute-start(bf16[16,4096]{1,0:T(8,128)(2,1)S(1)} %get-tuple-element.60), channel_id=1, source_target_pairs={{0,2},{2,0},{4,6},{6,4},{8,10},{10,8},{12,14},{14,12},{1,3},{3,1},... | collective-permute-start | bytes 393224 | tf_op jit(solution)/shard_map/ppermute | solution.py:28
  49.4 7.5 %collective-permute-start.32 = (bf16[16,4096]{1,0:T(8,128)(2,1)S(1)}, bf16[16,4096]{1,0:T(8,128)(2,1)S(1)}, u32[]{:S(2)}, u32[]{:S(2)}) collective-permute-start(bf16[16,4096]{1,0:T(8,128)(2,1)S(1)} %get-tuple-element.62), channel_id=1, source_target_pairs={{0,2},{2,0},{4,6},{6,4},{8,10},{10,8},{12,14},{14,12},{1,3},{3,1},... | collective-permute-start | bytes 393224 | tf_op jit(solution)/shard_map/ppermute | solution.py:28
  50.8 8.9 %collective-permute-start.34 = (bf16[16,4096]{1,0:T(8,128)(2,1)S(1)}, bf16[16,4096]{1,0:T(8,128)(2,1)S(1)}, u32[]{:S(2)}, u32[]{:S(2)}) collective-permute-start(bf16[16,4096]{1,0:T(8,128)(2,1)S(1)} %get-tuple-element.64), channel_id=1, source_target_pairs={{0,2},{2,0},{4,6},{6,4},{8,10},{10,8},{12,14},{14,12},{1,3},{3,1},... | collective-permute-start | bytes 393224 | tf_op jit(solution)/shard_map/ppermute | solution.py:28
  50.9 12.5 %collective-permute-start.36 = (bf16[16,4096]{1,0:T(8,128)(2,1)S(1)}, bf16[16,4096]{1,0:T(8,128)(2,1)S(1)}, u32[]{:S(2)}, u32[]{:S(2)}) collective-permute-start(bf16[16,4096]{1,0:T(8,128)(2,1)S(1)} %get-tuple-element.65), channel_id=1, source_target_pairs={{0,2},{2,0},{4,6},{6,4},{8,10},{10,8},{12,14},{14,12},{1,3},{3,1},... | collective-permute-start | bytes 393224 | tf_op jit(solution)/shard_map/ppermute | solution.py:28
  54.5 5.7 %collective-permute-start.23 = (bf16[3,256,128]{2,1,0:T(8,128)(2,1)S(1)}, bf16[3,256,128]{2,1,0:T(8,128)(2,1)S(1)}, u32[]{:S(2)}, u32[]{:S(2)}) collective-permute-start(bf16[3,256,128]{2,1,0:T(8,128)(2,1)S(1)} %get-tuple-element.57), channel_id=1, source_target_pairs={{0,1},{1,0},{2,3},{3,2},{4,5},{5,4},{6,7},{7,6},{8,9},{9,8},{10,11... | collective-permute-start | bytes 589832 | tf_op jit(solution)/shard_map/ppermute | solution.py:23
  56.1 11.1 %collective-permute-start.31 = (bf16[16,4096]{1,0:T(8,128)(2,1)S(1)}, bf16[16,4096]{1,0:T(8,128)(2,1)S(1)}, u32[]{:S(2)}, u32[]{:S(2)}) collective-permute-start(bf16[16,4096]{1,0:T(8,128)(2,1)S(1)} %add_convert_fusion.2), channel_id=1, source_target_pairs={{0,12},{2,14},{4,8},{6,10},{8,4},{10,6},{12,0},{14,2},{1,13},{3,15... | collective-permute-start | bytes 393224 | tf_op jit(solution)/shard_map/ppermute | solution.py:28
  56.9 13.9 %collective-permute-start.33 = (bf16[16,4096]{1,0:T(8,128)(2,1)S(1)}, bf16[16,4096]{1,0:T(8,128)(2,1)S(1)}, u32[]{:S(2)}, u32[]{:S(2)}) collective-permute-start(bf16[16,4096]{1,0:T(8,128)(2,1)S(1)} %add_convert_fusion.1), channel_id=1, source_target_pairs={{0,8},{2,10},{4,12},{6,14},{8,0},{10,2},{12,4},{14,6},{1,9},{3,11}... | collective-permute-start | bytes 393224 | tf_op jit(solution)/shard_map/ppermute | solution.py:28
  59.7 17.3 %collective-permute-start.35 = (bf16[16,4096]{1,0:T(8,128)(2,1)S(1)}, bf16[16,4096]{1,0:T(8,128)(2,1)S(1)}, u32[]{:S(2)}, u32[]{:S(2)}) collective-permute-start(bf16[16,4096]{1,0:T(8,128)(2,1)S(1)} %add_convert_fusion), channel_id=1, source_target_pairs={{0,4},{2,6},{4,0},{6,2},{8,12},{10,14},{12,8},{14,10},{1,5},{3,7},... | collective-permute-start | bytes 393224 | tf_op jit(solution)/shard_map/ppermute | solution.py:28
  60.3 14.2 %collective-permute-start.24 = (bf16[256,128]{1,0:T(8,128)(2,1)S(1)}, bf16[256,128]{1,0:T(8,128)(2,1)S(1)}, u32[]{:S(2)}, u32[]{:S(2)}) collective-permute-start(bf16[256,128]{1,0:T(8,128)(2,1)S(1)} %get-tuple-element.66), channel_id=1, source_target_pairs={{2,8},{5,3},{6,12},{7,1},{8,2},{9,7},{11,5},{12,6},{13,11},{15,9},... | collective-permute-start | bytes 196616 | tf_op jit(solution)/shard_map/ppermute | solution.py:46
  63.4 11.2 %collective-permute-start.26 = (bf16[256,128]{1,0:T(8,128)(2,1)S(1)}, bf16[256,128]{1,0:T(8,128)(2,1)S(1)}, u32[]{:S(2)}, u32[]{:S(2)}) collective-permute-start(bf16[256,128]{1,0:T(8,128)(2,1)S(1)} %get-tuple-element.68), channel_id=1, source_target_pairs={{1,7},{3,5},{4,0},{5,11},{6,2},{7,9},{8,4},{9,15},{10,6},{11,13},{... | collective-permute-start | bytes 196616 | tf_op jit(solution)/shard_map/ppermute | solution.py:46
  67.2 7.8 %collective-permute-start.28 = (bf16[256,128]{1,0:T(8,128)(2,1)S(1)}, bf16[256,128]{1,0:T(8,128)(2,1)S(1)}, u32[]{:S(2)}, u32[]{:S(2)}) collective-permute-start(bf16[256,128]{1,0:T(8,128)(2,1)S(1)} %get-tuple-element.67), channel_id=1, source_target_pairs={{0,4},{1,3},{2,6},{3,1},{4,8},{5,7},{6,10},{7,5},{8,12},{9,11},{10... | collective-permute-start | bytes 196616 | tf_op jit(solution)/shard_map/ppermute | solution.py:46
  70.8 6.9 %collective-permute-start.22 = (f32[256,128]{1,0:T(8,128)S(1)}, f32[256,128]{1,0:T(8,128)S(1)}, u32[]{:S(2)}, u32[]{:S(2)}) collective-permute-start(f32[256,128]{1,0:T(8,128)S(1)} %get-tuple-element.55), channel_id=1, source_target_pairs={{0,1},{1,0},{2,3},{3,2},{4,5},{5,4},{6,7},{7,6},{8,9},{9,8},{10,11... | collective-permute-start | bytes 393224 | tf_op jit(solution)/shard_map/ppermute | solution.py:23
  74.5 3.2 %collective-permute-start.25 = (bf16[256,128]{1,0:T(8,128)(2,1)S(1)}, bf16[256,128]{1,0:T(8,128)(2,1)S(1)}, u32[]{:S(2)}, u32[]{:S(2)}) collective-permute-start(bf16[256,128]{1,0:T(8,128)(2,1)S(1)} %collective-permute-done.24), channel_id=1, source_target_pairs={{0,1},{1,0},{2,3},{3,2},{4,5},{5,4},{6,7},{7,6},{8,9},{9,8},{10,11... | collective-permute-start | bytes 196616 | tf_op jit(solution)/shard_map/ppermute | solution.py:23
  74.6 3.2 %collective-permute-start.27 = (bf16[256,128]{1,0:T(8,128)(2,1)S(1)}, bf16[256,128]{1,0:T(8,128)(2,1)S(1)}, u32[]{:S(2)}, u32[]{:S(2)}) collective-permute-start(bf16[256,128]{1,0:T(8,128)(2,1)S(1)} %collective-permute-done.26), channel_id=1, source_target_pairs={{0,1},{1,0},{2,3},{3,2},{4,5},{5,4},{6,7},{7,6},{8,9},{9,8},{10,11... | collective-permute-start | bytes 196616 | tf_op jit(solution)/shard_map/ppermute | solution.py:23
  (10 other events, 69.8 us)

commit v3 on v2

--- a/solution.py
+++ b/solution.py
@@ -330,20 +330,25 @@
     direct = dp == 8
     steps = range(SPAN)
 
+    docs = jnp.concatenate([doc_lengths, prefix_spans])
+    if direct:
+        z3, z2, z1 = (dp_swap(weight, 2 * k) for k in (3, 2, 1))
+        cross0 = dp_swap(weight, 1)
+        docs = after(docs, cross0)
     (info,) = call(
         limits_kernel,
         [((parts, 8, ROWS), jnp.int32)],
         [], 4, 1,
-        jnp.concatenate([doc_lengths, prefix_spans]),
+        docs,
     )
     query_stack = stack_heads(queries, head)
     grad_stack = stack_heads(grad_out, head)
-    mine = [fan_out(keys, k) for k in steps]
-    other = [core_swap(after(block, info, query_stack, grad_stack)) for block in mine]
+    mine = [fan_out(after(keys, info), k) for k in steps]
+    other = [core_swap(after(block, z1, z2) if direct else block) for block in mine]
+
     if direct:
-        weight = after(weight, mine[0])
-        z3, z2, z1 = (dp_swap(weight, 2 * k) for k in (3, 2, 1))
-        cross0 = dp_swap(weight, 1)
+        cross = [cross0] + [dp_swap(block, 1) for block in (z1, z2, z3)]
+        info = after(info, *cross[:3])
 
     probs, key_window, own_v, mine_v, give_v = call(
         weights_kernel,
@@ -365,7 +370,6 @@
     other_v = core_swap(own_v)
 
     if direct:
-        cross = [cross0] + [dp_swap(block, 1) for block in (z1, z2, z3)]
         value_part, full_weight = call(
             value_kernel,
             [((rows, head), F32), ((head, depth), BF16)],

time: 78.9 us -> 75 us (0.951)
  waiting for transfers between devices: 11.5 us -> 8.9 us
  starting transfers between devices: 54.9 us -> 53.9 us
    ppermute x14, waiting for transfers between devices: 7.04 us -> 4.04 us  [dp_swap(): return lax.ppermute(value, 'dp', [(i, i ^ mask) for i in range(count)])]
  transfers between devices with their start and end apart: 37 -> 37, of which waited for: 10 -> 11; matrix products, arithmetic and copies ran while one was open for 2% -> 2% of each run, Pallas kernels for 10% -> 10%
where the time goes in v3:
time: 75 us; the launch traced here: 74.6 us
  starting transfers between devices  53.9 us (72%)
  waiting for transfers between devices  8.9 us (12%)
  Pallas kernels  8.29 us (11%)
  other arithmetic  2.34 us (3%)
  between operations  0.98 us (1%)
    ppermute x9, starting transfers between devices, fan_out(): lax.ppermute(value, BOTH, [(i, j) for i, j in pairs if 0 <= j < 2 * count])  24.9 us
    ppermute x14, starting transfers between devices, core_swap(): return lax.ppermute(value, 'fsdp', [(0, 1), (1, 0)])  17.2 us
    ppermute x14, starting transfers between devices, dp_swap(): return lax.ppermute(value, 'dp', [(i, i ^ mask) for i in range(count)])  11.8 us
    pallas_call x7, Pallas kernels, call(): pl.pallas_call(kernel, in_specs=[SMEM] * smem + [VMEM] * (len(args) - sme...  8.29 us
    ppermute x14, waiting for transfers between devices, dp_swap(): return lax.ppermute(value, 'dp', [(i, i ^ mask) for i in range(count)])  4.04 us
    ppermute x14, waiting for transfers between devices, core_swap(): return lax.ppermute(value, 'fsdp', [(0, 1), (1, 0)])  2.98 us
    ppermute x9, waiting for transfers between devices, fan_out(): lax.ppermute(value, BOTH, [(i, j) for i, j in pairs if 0 <= j < 2 * count])  1.88 us
  transfers between devices with their start and end apart: 37, of which 11 were waited for; matrix products, arithmetic and copies ran while one was open for 2% of the time, Pallas kernels for 10%

profile of v3, /device:TPU:11, one launch (start us, length us, event | category | flops | bytes accessed | tf_op | source)
XLA Modules:
  0.0 74.6 jit_solution(6284166075804668422)
XLA Ops:
  1.0 2.5 %collective-permute-start.3 = (bf16[16,4096]{1,0:T(8,128)(2,1)}, bf16[16,4096]{1,0:T(8,128)(2,1)S(1)}, u32[]{:S(2)}, u32[]{:S(2)}) collective-permute-start(bf16[16,4096]{1,0:T(8,128)(2,1)} %bitcast.21), channel_id=1, source_target_pairs={{0,8},{2,10},{4,12},{6,14},{8,0},{10,2},{12,4},{14,6},{1,9},{3,11}... | collective-permute-start | bytes 393224 | tf_op jit(solution)/shard_map/ppermute | solution.py:28
  4.2 1.1 %collective-permute-done.c0 = bf16[16,4096]{1,0:T(8,128)(2,1)S(1)} collective-permute-done((bf16[16,4096]{1,0:T(8,128)(2,1)}, bf16[16,4096]{1,0:T(8,128)(2,1)S(1)}, u32[]{:S(2)}, u32[]{:S(2)}) %collective-permute-start) | collective-permute-done | bytes 131104 | tf_op jit(solution)/shard_map/ppermute | solution.py:28
  5.9 2.2 %collective-permute-start.7 = (bf16[256,128]{1,0:T(8,128)(2,1)S(1)}, bf16[256,128]{1,0:T(8,128)(2,1)S(1)}, u32[]{:S(2)}, u32[]{:S(2)}) collective-permute-start(bf16[256,128]{1,0:T(8,128)(2,1)S(1)} %copy-done.2), channel_id=1, source_target_pairs={{0,4},{1,3},{2,6},{3,1},{4,8},{5,7},{6,10},{7,5},{8,12},{9,11},{10... | collective-permute-start | bytes 196616 | tf_op jit(solution)/shard_map/ppermute | solution.py:46
  8.1 1.4 %collective-permute-start.12 = (bf16[16,4096]{1,0:T(8,128)(2,1)S(1)}, bf16[16,4096]{1,0:T(8,128)(2,1)S(1)}, u32[]{:S(2)}, u32[]{:S(2)}) collective-permute-start(bf16[16,4096]{1,0:T(8,128)(2,1)S(1)} %bitcast.22), channel_id=1, source_target_pairs={{0,12},{2,14},{4,8},{6,10},{8,4},{10,6},{12,0},{14,2},{1,13},{3,15... | collective-permute-start | bytes 393224 | tf_op jit(solution)/shard_map/ppermute | solution.py:28
  9.5 1.2 %collective-permute-start.2 = (bf16[16,4096]{1,0:T(8,128)(2,1)S(1)}, bf16[16,4096]{1,0:T(8,128)(2,1)S(1)}, u32[]{:S(2)}, u32[]{:S(2)}) collective-permute-start(bf16[16,4096]{1,0:T(8,128)(2,1)S(1)} %collective-permute-done.1.z1), channel_id=1, source_target_pairs={{0,2},{2,0},{4,6},{6,4},{8,10},{10,8},{12,14},{14,12},{1,3},{3,1},... | collective-permute-start | bytes 393224 | tf_op jit(solution)/shard_map/ppermute | solution.py:28
  10.7 4.1 %collective-permute-start.5 = (bf16[256,128]{1,0:T(8,128)(2,1)S(1)}, bf16[256,128]{1,0:T(8,128)(2,1)S(1)}, u32[]{:S(2)}, u32[]{:S(2)}) collective-permute-start(bf16[256,128]{1,0:T(8,128)(2,1)S(1)} %copy-done.2), channel_id=1, source_target_pairs={{2,8},{5,3},{6,12},{7,1},{8,2},{9,7},{11,5},{12,6},{13,11},{15,9},... | collective-permute-start | bytes 196616 | tf_op jit(solution)/shard_map/ppermute | solution.py:46
  14.7 2.1 %collective-permute-start.6 = (bf16[256,128]{1,0:T(8,128)(2,1)S(1)}, bf16[256,128]{1,0:T(8,128)(2,1)S(1)}, u32[]{:S(2)}, u32[]{:S(2)}) collective-permute-start(bf16[256,128]{1,0:T(8,128)(2,1)S(1)} %copy-done.2), channel_id=1, source_target_pairs={{1,7},{3,5},{4,0},{5,11},{6,2},{7,9},{8,4},{9,15},{10,6},{11,13},{... | collective-permute-start | bytes 196616 | tf_op jit(solution)/shard_map/ppermute | solution.py:46
  16.9 1.1 %collective-permute-start.4 = (bf16[16,4096]{1,0:T(8,128)(2,1)S(1)}, bf16[16,4096]{1,0:T(8,128)(2,1)S(1)}, u32[]{:S(2)}, u32[]{:S(2)}) collective-permute-start(bf16[16,4096]{1,0:T(8,128)(2,1)S(1)} %collective-permute-done.3.z2), channel_id=1, source_target_pairs={{0,2},{2,0},{4,6},{6,4},{8,10},{10,8},{12,14},{14,12},{1,3},{3,1},... | collective-permute-start | bytes 393224 | tf_op jit(solution)/shard_map/ppermute | solution.py:28
  18.0 3.7 %collective-permute-start.10 = (bf16[256,128]{1,0:T(8,128)(2,1)S(1)}, bf16[256,128]{1,0:T(8,128)(2,1)S(1)}, u32[]{:S(2)}, u32[]{:S(2)}) collective-permute-start(bf16[256,128]{1,0:T(8,128)(2,1)S(1)} %collective-permute-done.7.r3), channel_id=1, source_target_pairs={{0,1},{1,0},{2,3},{3,2},{4,5},{5,4},{6,7},{7,6},{8,9},{9,8},{10,11... | collective-permute-start | bytes 196616 | tf_op jit(solution)/shard_map/ppermute | solution.py:23
  21.6 1.7 %collective-permute-start.8 = (bf16[256,128]{1,0:T(8,128)(2,1)S(1)}, bf16[256,128]{1,0:T(8,128)(2,1)S(1)}, u32[]{:S(2)}, u32[]{:S(2)}) collective-permute-start(bf16[256,128]{1,0:T(8,128)(2,1)S(1)} %collective-permute-done.5.r1), channel_id=1, source_target_pairs={{0,1},{1,0},{2,3},{3,2},{4,5},{5,4},{6,7},{7,6},{8,9},{9,8},{10,11... | collective-permute-start | bytes 196616 | tf_op jit(solution)/shard_map/ppermute | solution.py:23
  24.6 2.5 %shard_map.103 = (bf16[2,7,256,512]{3,2,1,0:T(8,128)(2,1)S(1)}, bf16[1792,128]{1,0:T(8,128)(2,1)S(1)}, f32[256,128]{1,0:T(8,128)S(1)}, f32[3,256,128]{2,1,0:T(8,128)S(1)}, bf16[3,256,128]{2,1,0:T(8,128)(2,1)S(1)}) custom-call(s32[2,8,128]{2,1,0:T(8,128)S(1)} %shard_map.102.info_ref, bf16[2,512,128]{2,1,0:T(8,128)(2,1)S(1)} %bitcast.15, ...), custom_call_target="tpu_custom_call" | custom-call | flops 1073741824 | bytes 4194304 | tf_op jit(solution)/shard_map/pallas_call | solution.py:308
  28.9 1.3 %collective-permute-start.14 = (f32[256,128]{1,0:T(8,128)S(1)}, f32[256,128]{1,0:T(8,128)S(1)}, u32[]{:S(2)}, u32[]{:S(2)}) collective-permute-start(f32[256,128]{1,0:T(8,128)S(1)} %get-tuple-element.44.half_ref), channel_id=1, source_target_pairs={{0,1},{1,0},{2,3},{3,2},{4,5},{5,4},{6,7},{7,6},{8,9},{9,8},{10,11... | collective-permute-start | bytes 393224 | tf_op jit(solution)/shard_map/ppermute | solution.py:23
  30.2 1.0 %collective-permute-done.14.other_ref = f32[256,128]{1,0:T(8,128)S(1)} collective-permute-done((f32[256,128]{1,0:T(8,128)S(1)}, f32[256,128]{1,0:T(8,128)S(1)}, u32[]{:S(2)}, u32[]{:S(2)}) %collective-permute-start.14) | collective-permute-done | bytes 131104 | tf_op jit(solution)/shard_map/ppermute | solution.py:23
  31.3 2.0 %collective-permute-start.16 = (bf16[2,256,128]{2,1,0:T(8,128)(2,1)S(1)}, bf16[2,256,128]{2,1,0:T(8,128)(2,1)S(1)}, u32[]{:S(2)}, u32[]{:S(2)}) collective-permute-start(bf16[2,256,128]{2,1,0:T(8,128)(2,1)S(1)} %get-tuple-element.47), channel_id=1, source_target_pairs={{2,8},{5,3},{6,12},{7,1},{8,2},{9,7},{11,5},{12,6},{13,11},{15,9},... | collective-permute-start | bytes 393224 | tf_op jit(solution)/shard_map/ppermute | solution.py:46
  33.3 4.2 %collective-permute-start.17 = (bf16[2,256,128]{2,1,0:T(8,128)(2,1)S(1)}, bf16[2,256,128]{2,1,0:T(8,128)(2,1)S(1)}, u32[]{:S(2)}, u32[]{:S(2)}) collective-permute-start(bf16[2,256,128]{2,1,0:T(8,128)(2,1)S(1)} %get-tuple-element.48), channel_id=1, source_target_pairs={{1,7},{3,5},{4,0},{5,11},{6,2},{7,9},{8,4},{9,15},{10,6},{11,13},{... | collective-permute-start | bytes 393224 | tf_op jit(solution)/shard_map/ppermute | solution.py:46
  37.5 2.1 %collective-permute-start.18 = (bf16[2,256,128]{2,1,0:T(8,128)(2,1)S(1)}, bf16[2,256,128]{2,1,0:T(8,128)(2,1)S(1)}, u32[]{:S(2)}, u32[]{:S(2)}) collective-permute-start(bf16[2,256,128]{2,1,0:T(8,128)(2,1)S(1)} %get-tuple-element.49), channel_id=1, source_target_pairs={{0,4},{1,3},{2,6},{3,1},{4,8},{5,7},{6,10},{7,5},{8,12},{9,11},{10... | collective-permute-start | bytes 393224 | tf_op jit(solution)/shard_map/ppermute | solution.py:46
  39.6 1.3 %collective-permute-start.11 = (f32[256,128]{1,0:T(8,128)S(1)}, f32[256,128]{1,0:T(8,128)S(1)}, u32[]{:S(2)}, u32[]{:S(2)}) collective-permute-start(f32[256,128]{1,0:T(8,128)S(1)} %get-tuple-element.43.a_ref), channel_id=1, source_target_pairs={{0,1},{1,0},{2,3},{3,2},{4,5},{5,4},{6,7},{7,6},{8,9},{9,8},{10,11... | collective-permute-start | bytes 393224 | tf_op jit(solution)/shard_map/ppermute | solution.py:23
  41.6 1.9 %collective-permute-done.18.r3 = bf16[2,256,128]{2,1,0:T(8,128)(2,1)S(1)} collective-permute-done((bf16[2,256,128]{2,1,0:T(8,128)(2,1)S(1)}, bf16[2,256,128]{2,1,0:T(8,128)(2,1)S(1)}, u32[]{:S(2)}, u32[]{:S(2)}) %collective-permute-start.18) | collective-permute-done | bytes 131104 | tf_op jit(solution)/shard_map/ppermute | solution.py:46
  43.5 0.8 %collective-permute-start.21 = (bf16[2,256,128]{2,1,0:T(8,128)(2,1)S(1)}, bf16[2,256,128]{2,1,0:T(8,128)(2,1)S(1)}, u32[]{:S(2)}, u32[]{:S(2)}) collective-permute-start(bf16[2,256,128]{2,1,0:T(8,128)(2,1)S(1)} %collective-permute-done.18.r3), channel_id=1, source_target_pairs={{0,1},{1,0},{2,3},{3,2},{4,5},{5,4},{6,7},{7,6},{8,9},{9,8},{10,11... | collective-permute-start | bytes 393224 | tf_op jit(solution)/shard_map/ppermute | solution.py:23
  44.3 1.0 %collective-permute-done.21.s3 = bf16[2,256,128]{2,1,0:T(8,128)(2,1)S(1)} collective-permute-done((bf16[2,256,128]{2,1,0:T(8,128)(2,1)S(1)}, bf16[2,256,128]{2,1,0:T(8,128)(2,1)S(1)}, u32[]{:S(2)}, u32[]{:S(2)}) %collective-permute-start.21) | collective-permute-done | bytes 131104 | tf_op jit(solution)/shard_map/ppermute | solution.py:23
  46.0 1.5 %collective-permute-start.32 = (bf16[16,4096]{1,0:T(8,128)(2,1)S(1)}, bf16[16,4096]{1,0:T(8,128)(2,1)S(1)}, u32[]{:S(2)}, u32[]{:S(2)}) collective-permute-start(bf16[16,4096]{1,0:T(8,128)(2,1)S(1)} %get-tuple-element.66), channel_id=1, source_target_pairs={{0,2},{2,0},{4,6},{6,4},{8,10},{10,8},{12,14},{14,12},{1,3},{3,1},... | collective-permute-start | bytes 393224 | tf_op jit(solution)/shard_map/ppermute | solution.py:28
  47.5 1.4 %collective-permute-start.36 = (bf16[16,4096]{1,0:T(8,128)(2,1)S(1)}, bf16[16,4096]{1,0:T(8,128)(2,1)S(1)}, u32[]{:S(2)}, u32[]{:S(2)}) collective-permute-start(bf16[16,4096]{1,0:T(8,128)(2,1)S(1)} %get-tuple-element.69), channel_id=1, source_target_pairs={{0,2},{2,0},{4,6},{6,4},{8,10},{10,8},{12,14},{14,12},{1,3},{3,1},... | collective-permute-start | bytes 393224 | tf_op jit(solution)/shard_map/ppermute | solution.py:28
  48.9 2.1 %shard_map.107 = (f32[2,128,512]{2,1,0:T(8,128)S(1)}, f32[256,128]{1,0:T(8,128)S(1)}, f32[3,256,128]{2,1,0:T(8,128)S(1)}, bf16[3,256,128]{2,1,0:T(8,128)(2,1)S(1)}) custom-call(s32[2,8,128]{2,1,0:T(8,128)S(1)} %shard_map.102.info_ref, bf16[2,512,128]{2,1,0:T(8,128)(2,1)S(1)} %bitcast.16, bf16[2,512,128]{2,1,0:T(8,128)(2,1)S(1)} %bitcast.18, ...), custom_call_target="tpu_custom_call" | custom-call | flops 1073741824 | bytes 4194304 | tf_op jit(solution)/shard_map/pallas_call | solution.py:308
  51.0 1.5 %collective-permute-start.23 = (bf16[3,256,128]{2,1,0:T(8,128)(2,1)S(1)}, bf16[3,256,128]{2,1,0:T(8,128)(2,1)S(1)}, u32[]{:S(2)}, u32[]{:S(2)}) collective-permute-start(bf16[3,256,128]{2,1,0:T(8,128)(2,1)S(1)} %get-tuple-element.61), channel_id=1, source_target_pairs={{0,1},{1,0},{2,3},{3,2},{4,5},{5,4},{6,7},{7,6},{8,9},{9,8},{10,11... | collective-permute-start | bytes 589832 | tf_op jit(solution)/shard_map/ppermute | solution.py:23
  53.5 1.5 %collective-permute-start.33 = (bf16[16,4096]{1,0:T(8,128)(2,1)S(1)}, bf16[16,4096]{1,0:T(8,128)(2,1)S(1)}, u32[]{:S(2)}, u32[]{:S(2)}) collective-permute-start(bf16[16,4096]{1,0:T(8,128)(2,1)S(1)} %add_convert_fusion.1), channel_id=1, source_target_pairs={{0,8},{2,10},{4,12},{6,14},{8,0},{10,2},{12,4},{14,6},{1,9},{3,11}... | collective-permute-start | bytes 393224 | tf_op jit(solution)/shard_map/ppermute | solution.py:28
  55.0 1.3 %collective-permute-done.34 = bf16[16,4096]{1,0:T(8,128)(2,1)S(1)} collective-permute-done((bf16[16,4096]{1,0:T(8,128)(2,1)S(1)}, bf16[16,4096]{1,0:T(8,128)(2,1)S(1)}, u32[]{:S(2)}, u32[]{:S(2)}) %collective-permute-start.34) | collective-permute-done | bytes 131104 | tf_op jit(solution)/shard_map/ppermute | solution.py:28
  56.5 3.4 %collective-permute-start.24 = (bf16[256,128]{1,0:T(8,128)(2,1)S(1)}, bf16[256,128]{1,0:T(8,128)(2,1)S(1)}, u32[]{:S(2)}, u32[]{:S(2)}) collective-permute-start(bf16[256,128]{1,0:T(8,128)(2,1)S(1)} %get-tuple-element.70), channel_id=1, source_target_pairs={{2,8},{5,3},{6,12},{7,1},{8,2},{9,7},{11,5},{12,6},{13,11},{15,9},... | collective-permute-start | bytes 196616 | tf_op jit(solution)/shard_map/ppermute | solution.py:46
  59.9 3.0 %collective-permute-start.26 = (bf16[256,128]{1,0:T(8,128)(2,1)S(1)}, bf16[256,128]{1,0:T(8,128)(2,1)S(1)}, u32[]{:S(2)}, u32[]{:S(2)}) collective-permute-start(bf16[256,128]{1,0:T(8,128)(2,1)S(1)} %get-tuple-element.72), channel_id=1, source_target_pairs={{1,7},{3,5},{4,0},{5,11},{6,2},{7,9},{8,4},{9,15},{10,6},{11,13},{... | collective-permute-start | bytes 196616 | tf_op jit(solution)/shard_map/ppermute | solution.py:46
  63.6 1.9 %collective-permute-start.28 = (bf16[256,128]{1,0:T(8,128)(2,1)S(1)}, bf16[256,128]{1,0:T(8,128)(2,1)S(1)}, u32[]{:S(2)}, u32[]{:S(2)}) collective-permute-start(bf16[256,128]{1,0:T(8,128)(2,1)S(1)} %get-tuple-element.71), channel_id=1, source_target_pairs={{0,4},{1,3},{2,6},{3,1},{4,8},{5,7},{6,10},{7,5},{8,12},{9,11},{10... | collective-permute-start | bytes 196616 | tf_op jit(solution)/shard_map/ppermute | solution.py:46
  65.5 1.7 %shard_map.108 = (bf16[256,4096]{1,0:T(8,128)(2,1)}, bf16[256,512]{1,0:T(8,128)(2,1)}) custom-call(bf16[256,128]{1,0:T(8,128)(2,1)S(1)} %get-tuple-element.50.grad_ref, bf16[128,4096]{1,0:T(8,128)(2,1)S(1)} %get-tuple-element.51.weight_ref, f32[2,128,512]{2,1,0:T(8,128)S(1)} %get-tuple-element.56.query_ref), custom_call_target="tpu_custom_call" | custom-call | flops 1073741824 | bytes 4194304 | tf_op jit(solution)/shard_map/pallas_call | solution.py:308
  67.2 3.4 %collective-permute-start.22 = (f32[256,128]{1,0:T(8,128)S(1)}, f32[256,128]{1,0:T(8,128)S(1)}, u32[]{:S(2)}, u32[]{:S(2)}) collective-permute-start(f32[256,128]{1,0:T(8,128)S(1)} %get-tuple-element.59), channel_id=1, source_target_pairs={{0,1},{1,0},{2,3},{3,2},{4,5},{5,4},{6,7},{7,6},{8,9},{9,8},{10,11... | collective-permute-start | bytes 393224 | tf_op jit(solution)/shard_map/ppermute | solution.py:23
  71.1 1.9 %collective-permute-start.29 = (bf16[256,128]{1,0:T(8,128)(2,1)S(1)}, bf16[256,128]{1,0:T(8,128)(2,1)S(1)}, u32[]{:S(2)}, u32[]{:S(2)}) collective-permute-start(bf16[256,128]{1,0:T(8,128)(2,1)S(1)} %collective-permute-done.28), channel_id=1, source_target_pairs={{0,1},{1,0},{2,3},{3,2},{4,5},{5,4},{6,7},{7,6},{8,9},{9,8},{10,11... | collective-permute-start | bytes 196616 | tf_op jit(solution)/shard_map/ppermute | solution.py:23
  (70 shorter events, 10.1 us)
Async XLA Ops:
  0.7 4.6 %collective-permute-start = (bf16[16,4096]{1,0:T(8,128)(2,1)}, bf16[16,4096]{1,0:T(8,128)(2,1)S(1)}, u32[]{:S(2)}, u32[]{:S(2)}) collective-permute-start(bf16[16,4096]{1,0:T(8,128)(2,1)} %bitcast.19), channel_id=1, source_target_pairs={{0,2},{2,0},{4,6},{6,4},{8,10},{10,8},{12,14},{14,12},{1,3},{3,1},... | collective-permute-start | bytes 393224 | tf_op jit(solution)/shard_map/ppermute | solution.py:28
  1.0 8.5 %collective-permute-start.1 = (bf16[16,4096]{1,0:T(8,128)(2,1)}, bf16[16,4096]{1,0:T(8,128)(2,1)S(1)}, u32[]{:S(2)}, u32[]{:S(2)}) collective-permute-start(bf16[16,4096]{1,0:T(8,128)(2,1)} %bitcast.20), channel_id=1, source_target_pairs={{0,4},{2,6},{4,0},{6,2},{8,12},{10,14},{12,8},{14,10},{1,5},{3,7},... | collective-permute-start | bytes 393224 | tf_op jit(solution)/shard_map/ppermute | solution.py:28
  1.0 13.8 %collective-permute-start.3 = (bf16[16,4096]{1,0:T(8,128)(2,1)}, bf16[16,4096]{1,0:T(8,128)(2,1)S(1)}, u32[]{:S(2)}, u32[]{:S(2)}) collective-permute-start(bf16[16,4096]{1,0:T(8,128)(2,1)} %bitcast.21), channel_id=1, source_target_pairs={{0,8},{2,10},{4,12},{6,14},{8,0},{10,2},{12,4},{14,6},{1,9},{3,11}... | collective-permute-start | bytes 393224 | tf_op jit(solution)/shard_map/ppermute | solution.py:28
  5.9 11.0 %collective-permute-start.7 = (bf16[256,128]{1,0:T(8,128)(2,1)S(1)}, bf16[256,128]{1,0:T(8,128)(2,1)S(1)}, u32[]{:S(2)}, u32[]{:S(2)}) collective-permute-start(bf16[256,128]{1,0:T(8,128)(2,1)S(1)} %copy-done.2), channel_id=1, source_target_pairs={{0,4},{1,3},{2,6},{3,1},{4,8},{5,7},{6,10},{7,5},{8,12},{9,11},{10... | collective-permute-start | bytes 196616 | tf_op jit(solution)/shard_map/ppermute | solution.py:46
  8.1 15.3 %collective-permute-start.12 = (bf16[16,4096]{1,0:T(8,128)(2,1)S(1)}, bf16[16,4096]{1,0:T(8,128)(2,1)S(1)}, u32[]{:S(2)}, u32[]{:S(2)}) collective-permute-start(bf16[16,4096]{1,0:T(8,128)(2,1)S(1)} %bitcast.22), channel_id=1, source_target_pairs={{0,12},{2,14},{4,8},{6,10},{8,4},{10,6},{12,0},{14,2},{1,13},{3,15... | collective-permute-start | bytes 393224 | tf_op jit(solution)/shard_map/ppermute | solution.py:28
  9.5 13.9 %collective-permute-start.2 = (bf16[16,4096]{1,0:T(8,128)(2,1)S(1)}, bf16[16,4096]{1,0:T(8,128)(2,1)S(1)}, u32[]{:S(2)}, u32[]{:S(2)}) collective-permute-start(bf16[16,4096]{1,0:T(8,128)(2,1)S(1)} %collective-permute-done.1.z1), channel_id=1, source_target_pairs={{0,2},{2,0},{4,6},{6,4},{8,10},{10,8},{12,14},{14,12},{1,3},{3,1},... | collective-permute-start | bytes 393224 | tf_op jit(solution)/shard_map/ppermute | solution.py:28
  10.7 7.3 %collective-permute-start.5 = (bf16[256,128]{1,0:T(8,128)(2,1)S(1)}, bf16[256,128]{1,0:T(8,128)(2,1)S(1)}, u32[]{:S(2)}, u32[]{:S(2)}) collective-permute-start(bf16[256,128]{1,0:T(8,128)(2,1)S(1)} %copy-done.2), channel_id=1, source_target_pairs={{2,8},{5,3},{6,12},{7,1},{8,2},{9,7},{11,5},{12,6},{13,11},{15,9},... | collective-permute-start | bytes 196616 | tf_op jit(solution)/shard_map/ppermute | solution.py:46
  14.7 6.9 %collective-permute-start.6 = (bf16[256,128]{1,0:T(8,128)(2,1)S(1)}, bf16[256,128]{1,0:T(8,128)(2,1)S(1)}, u32[]{:S(2)}, u32[]{:S(2)}) collective-permute-start(bf16[256,128]{1,0:T(8,128)(2,1)S(1)} %copy-done.2), channel_id=1, source_target_pairs={{1,7},{3,5},{4,0},{5,11},{6,2},{7,9},{8,4},{9,15},{10,6},{11,13},{... | collective-permute-start | bytes 196616 | tf_op jit(solution)/shard_map/ppermute | solution.py:46
  16.9 6.9 %collective-permute-start.4 = (bf16[16,4096]{1,0:T(8,128)(2,1)S(1)}, bf16[16,4096]{1,0:T(8,128)(2,1)S(1)}, u32[]{:S(2)}, u32[]{:S(2)}) collective-permute-start(bf16[16,4096]{1,0:T(8,128)(2,1)S(1)} %collective-permute-done.3.z2), channel_id=1, source_target_pairs={{0,2},{2,0},{4,6},{6,4},{8,10},{10,8},{12,14},{14,12},{1,3},{3,1},... | collective-permute-start | bytes 393224 | tf_op jit(solution)/shard_map/ppermute | solution.py:28
  18.0 5.8 %collective-permute-start.10 = (bf16[256,128]{1,0:T(8,128)(2,1)S(1)}, bf16[256,128]{1,0:T(8,128)(2,1)S(1)}, u32[]{:S(2)}, u32[]{:S(2)}) collective-permute-start(bf16[256,128]{1,0:T(8,128)(2,1)S(1)} %collective-permute-done.7.r3), channel_id=1, source_target_pairs={{0,1},{1,0},{2,3},{3,2},{4,5},{5,4},{6,7},{7,6},{8,9},{9,8},{10,11... | collective-permute-start | bytes 196616 | tf_op jit(solution)/shard_map/ppermute | solution.py:23
  23.4 4.7 %collective-permute-start.13 = (bf16[16,4096]{1,0:T(8,128)(2,1)S(1)}, bf16[16,4096]{1,0:T(8,128)(2,1)S(1)}, u32[]{:S(2)}, u32[]{:S(2)}) collective-permute-start(bf16[16,4096]{1,0:T(8,128)(2,1)S(1)} %collective-permute-done.12.z3), channel_id=1, source_target_pairs={{0,2},{2,0},{4,6},{6,4},{8,10},{10,8},{12,14},{14,12},{1,3},{3,1},... | collective-permute-start | bytes 393224 | tf_op jit(solution)/shard_map/ppermute | solution.py:28
  27.1 4.1 %collective-permute-start.15 = (bf16[3,256,128]{2,1,0:T(8,128)(2,1)S(1)}, bf16[3,256,128]{2,1,0:T(8,128)(2,1)S(1)}, u32[]{:S(2)}, u32[]{:S(2)}) collective-permute-start(bf16[3,256,128]{2,1,0:T(8,128)(2,1)S(1)} %get-tuple-element.46), channel_id=1, source_target_pairs={{0,1},{1,0},{2,3},{3,2},{4,5},{5,4},{6,7},{7,6},{8,9},{9,8},{10,11... | collective-permute-start | bytes 589832 | tf_op jit(solution)/shard_map/ppermute | solution.py:23
  31.3 9.6 %collective-permute-start.16 = (bf16[2,256,128]{2,1,0:T(8,128)(2,1)S(1)}, bf16[2,256,128]{2,1,0:T(8,128)(2,1)S(1)}, u32[]{:S(2)}, u32[]{:S(2)}) collective-permute-start(bf16[2,256,128]{2,1,0:T(8,128)(2,1)S(1)} %get-tuple-element.47), channel_id=1, source_target_pairs={{2,8},{5,3},{6,12},{7,1},{8,2},{9,7},{11,5},{12,6},{13,11},{15,9},... | collective-permute-start | bytes 393224 | tf_op jit(solution)/shard_map/ppermute | solution.py:46
  33.3 8.1 %collective-permute-start.17 = (bf16[2,256,128]{2,1,0:T(8,128)(2,1)S(1)}, bf16[2,256,128]{2,1,0:T(8,128)(2,1)S(1)}, u32[]{:S(2)}, u32[]{:S(2)}) collective-permute-start(bf16[2,256,128]{2,1,0:T(8,128)(2,1)S(1)} %get-tuple-element.48), channel_id=1, source_target_pairs={{1,7},{3,5},{4,0},{5,11},{6,2},{7,9},{8,4},{9,15},{10,6},{11,13},{... | collective-permute-start | bytes 393224 | tf_op jit(solution)/shard_map/ppermute | solution.py:46
  37.5 6.0 %collective-permute-start.18 = (bf16[2,256,128]{2,1,0:T(8,128)(2,1)S(1)}, bf16[2,256,128]{2,1,0:T(8,128)(2,1)S(1)}, u32[]{:S(2)}, u32[]{:S(2)}) collective-permute-start(bf16[2,256,128]{2,1,0:T(8,128)(2,1)S(1)} %get-tuple-element.49), channel_id=1, source_target_pairs={{0,4},{1,3},{2,6},{3,1},{4,8},{5,7},{6,10},{7,5},{8,12},{9,11},{10... | collective-permute-start | bytes 393224 | tf_op jit(solution)/shard_map/ppermute | solution.py:46
  39.6 4.7 %collective-permute-start.11 = (f32[256,128]{1,0:T(8,128)S(1)}, f32[256,128]{1,0:T(8,128)S(1)}, u32[]{:S(2)}, u32[]{:S(2)}) collective-permute-start(f32[256,128]{1,0:T(8,128)S(1)} %get-tuple-element.43.a_ref), channel_id=1, source_target_pairs={{0,1},{1,0},{2,3},{3,2},{4,5},{5,4},{6,7},{7,6},{8,9},{9,8},{10,11... | collective-permute-start | bytes 393224 | tf_op jit(solution)/shard_map/ppermute | solution.py:23
  40.9 3.4 %collective-permute-start.19 = (bf16[2,256,128]{2,1,0:T(8,128)(2,1)S(1)}, bf16[2,256,128]{2,1,0:T(8,128)(2,1)S(1)}, u32[]{:S(2)}, u32[]{:S(2)}) collective-permute-start(bf16[2,256,128]{2,1,0:T(8,128)(2,1)S(1)} %collective-permute-done.16.r1), channel_id=1, source_target_pairs={{0,1},{1,0},{2,3},{3,2},{4,5},{5,4},{6,7},{7,6},{8,9},{9,8},{10,11... | collective-permute-start | bytes 393224 | tf_op jit(solution)/shard_map/ppermute | solution.py:23
  41.4 2.8 %collective-permute-start.20 = (bf16[2,256,128]{2,1,0:T(8,128)(2,1)S(1)}, bf16[2,256,128]{2,1,0:T(8,128)(2,1)S(1)}, u32[]{:S(2)}, u32[]{:S(2)}) collective-permute-start(bf16[2,256,128]{2,1,0:T(8,128)(2,1)S(1)} %collective-permute-done.17.r2), channel_id=1, source_target_pairs={{0,1},{1,0},{2,3},{3,2},{4,5},{5,4},{6,7},{7,6},{8,9},{9,8},{10,11... | collective-permute-start | bytes 393224 | tf_op jit(solution)/shard_map/ppermute | solution.py:23
  45.9 6.6 %collective-permute-start.30 = (bf16[16,4096]{1,0:T(8,128)(2,1)S(1)}, bf16[16,4096]{1,0:T(8,128)(2,1)S(1)}, u32[]{:S(2)}, u32[]{:S(2)}) collective-permute-start(bf16[16,4096]{1,0:T(8,128)(2,1)S(1)} %get-tuple-element.64), channel_id=1, source_target_pairs={{0,2},{2,0},{4,6},{6,4},{8,10},{10,8},{12,14},{14,12},{1,3},{3,1},... | collective-permute-start | bytes 393224 | tf_op jit(solution)/shard_map/ppermute | solution.py:28
  46.0 7.5 %collective-permute-start.32 = (bf16[16,4096]{1,0:T(8,128)(2,1)S(1)}, bf16[16,4096]{1,0:T(8,128)(2,1)S(1)}, u32[]{:S(2)}, u32[]{:S(2)}) collective-permute-start(bf16[16,4096]{1,0:T(8,128)(2,1)S(1)} %get-tuple-element.66), channel_id=1, source_target_pairs={{0,2},{2,0},{4,6},{6,4},{8,10},{10,8},{12,14},{14,12},{1,3},{3,1},... | collective-permute-start | bytes 393224 | tf_op jit(solution)/shard_map/ppermute | solution.py:28
  47.4 8.9 %collective-permute-start.34 = (bf16[16,4096]{1,0:T(8,128)(2,1)S(1)}, bf16[16,4096]{1,0:T(8,128)(2,1)S(1)}, u32[]{:S(2)}, u32[]{:S(2)}) collective-permute-start(bf16[16,4096]{1,0:T(8,128)(2,1)S(1)} %get-tuple-element.68), channel_id=1, source_target_pairs={{0,2},{2,0},{4,6},{6,4},{8,10},{10,8},{12,14},{14,12},{1,3},{3,1},... | collective-permute-start | bytes 393224 | tf_op jit(solution)/shard_map/ppermute | solution.py:28
  47.5 12.4 %collective-permute-start.36 = (bf16[16,4096]{1,0:T(8,128)(2,1)S(1)}, bf16[16,4096]{1,0:T(8,128)(2,1)S(1)}, u32[]{:S(2)}, u32[]{:S(2)}) collective-permute-start(bf16[16,4096]{1,0:T(8,128)(2,1)S(1)} %get-tuple-element.69), channel_id=1, source_target_pairs={{0,2},{2,0},{4,6},{6,4},{8,10},{10,8},{12,14},{14,12},{1,3},{3,1},... | collective-permute-start | bytes 393224 | tf_op jit(solution)/shard_map/ppermute | solution.py:28
  51.0 5.4 %collective-permute-start.23 = (bf16[3,256,128]{2,1,0:T(8,128)(2,1)S(1)}, bf16[3,256,128]{2,1,0:T(8,128)(2,1)S(1)}, u32[]{:S(2)}, u32[]{:S(2)}) collective-permute-start(bf16[3,256,128]{2,1,0:T(8,128)(2,1)S(1)} %get-tuple-element.61), channel_id=1, source_target_pairs={{0,1},{1,0},{2,3},{3,2},{4,5},{5,4},{6,7},{7,6},{8,9},{9,8},{10,11... | collective-permute-start | bytes 589832 | tf_op jit(solution)/shard_map/ppermute | solution.py:23
  52.6 11.0 %collective-permute-start.31 = (bf16[16,4096]{1,0:T(8,128)(2,1)S(1)}, bf16[16,4096]{1,0:T(8,128)(2,1)S(1)}, u32[]{:S(2)}, u32[]{:S(2)}) collective-permute-start(bf16[16,4096]{1,0:T(8,128)(2,1)S(1)} %add_convert_fusion.2), channel_id=1, source_target_pairs={{0,12},{2,14},{4,8},{6,10},{8,4},{10,6},{12,0},{14,2},{1,13},{3,15... | collective-permute-start | bytes 393224 | tf_op jit(solution)/shard_map/ppermute | solution.py:28
  53.5 13.7 %collective-permute-start.33 = (bf16[16,4096]{1,0:T(8,128)(2,1)S(1)}, bf16[16,4096]{1,0:T(8,128)(2,1)S(1)}, u32[]{:S(2)}, u32[]{:S(2)}) collective-permute-start(bf16[16,4096]{1,0:T(8,128)(2,1)S(1)} %add_convert_fusion.1), channel_id=1, source_target_pairs={{0,8},{2,10},{4,12},{6,14},{8,0},{10,2},{12,4},{14,6},{1,9},{3,11}... | collective-permute-start | bytes 393224 | tf_op jit(solution)/shard_map/ppermute | solution.py:28
  56.3 16.7 %collective-permute-start.35 = (bf16[16,4096]{1,0:T(8,128)(2,1)S(1)}, bf16[16,4096]{1,0:T(8,128)(2,1)S(1)}, u32[]{:S(2)}, u32[]{:S(2)}) collective-permute-start(bf16[16,4096]{1,0:T(8,128)(2,1)S(1)} %add_convert_fusion), channel_id=1, source_target_pairs={{0,4},{2,6},{4,0},{6,2},{8,12},{10,14},{12,8},{14,10},{1,5},{3,7},... | collective-permute-start | bytes 393224 | tf_op jit(solution)/shard_map/ppermute | solution.py:28
  56.5 14.1 %collective-permute-start.24 = (bf16[256,128]{1,0:T(8,128)(2,1)S(1)}, bf16[256,128]{1,0:T(8,128)(2,1)S(1)}, u32[]{:S(2)}, u32[]{:S(2)}) collective-permute-start(bf16[256,128]{1,0:T(8,128)(2,1)S(1)} %get-tuple-element.70), channel_id=1, source_target_pairs={{2,8},{5,3},{6,12},{7,1},{8,2},{9,7},{11,5},{12,6},{13,11},{15,9},... | collective-permute-start | bytes 196616 | tf_op jit(solution)/shard_map/ppermute | solution.py:46
  59.9 10.8 %collective-permute-start.26 = (bf16[256,128]{1,0:T(8,128)(2,1)S(1)}, bf16[256,128]{1,0:T(8,128)(2,1)S(1)}, u32[]{:S(2)}, u32[]{:S(2)}) collective-permute-start(bf16[256,128]{1,0:T(8,128)(2,1)S(1)} %get-tuple-element.72), channel_id=1, source_target_pairs={{1,7},{3,5},{4,0},{5,11},{6,2},{7,9},{8,4},{9,15},{10,6},{11,13},{... | collective-permute-start | bytes 196616 | tf_op jit(solution)/shard_map/ppermute | solution.py:46
  63.6 7.5 %collective-permute-start.28 = (bf16[256,128]{1,0:T(8,128)(2,1)S(1)}, bf16[256,128]{1,0:T(8,128)(2,1)S(1)}, u32[]{:S(2)}, u32[]{:S(2)}) collective-permute-start(bf16[256,128]{1,0:T(8,128)(2,1)S(1)} %get-tuple-element.71), channel_id=1, source_target_pairs={{0,4},{1,3},{2,6},{3,1},{4,8},{5,7},{6,10},{7,5},{8,12},{9,11},{10... | collective-permute-start | bytes 196616 | tf_op jit(solution)/shard_map/ppermute | solution.py:46
  67.2 6.6 %collective-permute-start.22 = (f32[256,128]{1,0:T(8,128)S(1)}, f32[256,128]{1,0:T(8,128)S(1)}, u32[]{:S(2)}, u32[]{:S(2)}) collective-permute-start(f32[256,128]{1,0:T(8,128)S(1)} %get-tuple-element.59), channel_id=1, source_target_pairs={{0,1},{1,0},{2,3},{3,2},{4,5},{5,4},{6,7},{7,6},{8,9},{9,8},{10,11... | collective-permute-start | bytes 393224 | tf_op jit(solution)/shard_map/ppermute | solution.py:23
  70.6 3.2 %collective-permute-start.25 = (bf16[256,128]{1,0:T(8,128)(2,1)S(1)}, bf16[256,128]{1,0:T(8,128)(2,1)S(1)}, u32[]{:S(2)}, u32[]{:S(2)}) collective-permute-start(bf16[256,128]{1,0:T(8,128)(2,1)S(1)} %collective-permute-done.24), channel_id=1, source_target_pairs={{0,1},{1,0},{2,3},{3,2},{4,5},{5,4},{6,7},{7,6},{8,9},{9,8},{10,11... | collective-permute-start | bytes 196616 | tf_op jit(solution)/shard_map/ppermute | solution.py:23
  70.7 3.2 %collective-permute-start.27 = (bf16[256,128]{1,0:T(8,128)(2,1)S(1)}, bf16[256,128]{1,0:T(8,128)(2,1)S(1)}, u32[]{:S(2)}, u32[]{:S(2)}) collective-permute-start(bf16[256,128]{1,0:T(8,128)(2,1)S(1)} %collective-permute-done.26), channel_id=1, source_target_pairs={{0,1},{1,0},{2,3},{3,2},{4,5},{5,4},{6,7},{7,6},{8,9},{9,8},{10,11... | collective-permute-start | bytes 196616 | tf_op jit(solution)/shard_map/ppermute | solution.py:23
  (10 other events, 70.1 us)

commit v4 on v3

--- a/solution.py
+++ b/solution.py
@@ -28,21 +28,20 @@
     return lax.ppermute(value, "dp", [(i, i ^ mask) for i in range(count)])
 
 
-def reach(step, core, odd):
-    turn = 1 - 2 * odd
-    return ((-3 * turn, turn - 2), (-2, turn + 2), (2, turn))[step][core]
-
-
-def offset(step, core, odd, sign):
-    turn = 1 - 2 * odd
-    near = ((0, -2), (-2, 2), (2, 0))[step]
-    first = -3 * turn if step == 0 else sign * near[0]
-    return jnp.where(core == 0, first, sign * near[1] + turn)
+def partner(step, me):
+    turn = 1 - 2 * (me % 2)
+    row = 2 - 4 * ((me // 2) % 2)
+    return ((-3 * turn, 3 * turn), (row, -turn), (-row, turn))[step]
+
+
+def offset(step, core):
+    near, there = partner(step, lax.axis_index("dp"))
+    return jnp.where(core == 0, near, there)
 
 
 def fan_out(value, step):
     count = lax.axis_size("dp")
-    pairs = [(2 * i + c, 2 * (i + reach(step, c, i % 2)) + c) for i in range(count) for c in (0, 1)]
+    pairs = [(2 * i + c, 2 * (i + partner(step, i)[c]) + c) for i in range(count) for c in (0, 1)]
     return lax.ppermute(value, BOTH, [(i, j) for i, j in pairs if 0 <= j < 2 * count])
 
 
@@ -87,20 +86,18 @@
 
 def place_window(core, window_ref, own, mine, other):
     rows = own.shape[0]
-    odd = lax.rem(lax.axis_index("dp"), 2)
     window_ref[SPAN * rows : (SPAN + 1) * rows, :] = own
     for k in range(SPAN):
-        window_ref[at_block(SPAN + offset(k, core, odd, -1), rows), :] = mine[k]
-        window_ref[at_block(SPAN + offset(k, 1 - core, odd, -1), rows), :] = other[k]
+        window_ref[at_block(SPAN + offset(k, core), rows), :] = mine[k]
+        window_ref[at_block(SPAN + offset(k, 1 - core), rows), :] = other[k]
 
 
 def give_out(core, total_ref, own_ref, mine_ref, give_ref, factor):
     rows = own_ref.shape[0]
-    odd = lax.rem(lax.axis_index("dp"), 2)
     own_ref[...] = total_ref[SPAN * rows : (SPAN + 1) * rows, :] * factor
     for k in range(SPAN):
-        mine_ref[k] = total_ref[at_block(SPAN + offset(k, core, odd, 1), rows), :] * factor
-        there = total_ref[at_block(SPAN + offset(k, 1 - core, odd, 1), rows), :] * factor
+        mine_ref[k] = total_ref[at_block(SPAN + offset(k, core), rows), :] * factor
+        there = total_ref[at_block(SPAN + offset(k, 1 - core), rows), :] * factor
         give_ref[k] = there.astype(BF16)
 
 

time: 75 us -> 73.4 us (0.979)
  the two profiles are of different devices: /device:TPU:11 before, /device:TPU:0 now
where the time goes in v4:
time: 73.4 us; the launch traced here: 72 us
  starting transfers between devices  53.6 us (73%)
  waiting for transfers between devices  8.21 us (11%)
  Pallas kernels  6.66 us (9%)
  other arithmetic  2.34 us (3%)
  between operations  0.97 us (1%)
    ppermute x14, starting transfers between devices, dp_swap(): return lax.ppermute(value, 'dp', [(i, i ^ mask) for i in range(count)])  32.5 us
    ppermute x9, starting transfers between devices, fan_out(): lax.ppermute(value, BOTH, [(i, j) for i, j in pairs if 0 <= j < 2 * count])  12.4 us
    ppermute x14, starting transfers between devices, core_swap(): return lax.ppermute(value, 'fsdp', [(0, 1), (1, 0)])  8.65 us
    pallas_call x7, Pallas kernels, call(): pl.pallas_call(kernel, in_specs=[SMEM] * smem + [VMEM] * (len(args) - sme...  6.66 us
    ppermute x14, waiting for transfers between devices, dp_swap(): return lax.ppermute(value, 'dp', [(i, i ^ mask) for i in range(count)])  3.67 us
    ppermute x14, waiting for transfers between devices, core_swap(): return lax.ppermute(value, 'fsdp', [(0, 1), (1, 0)])  2.72 us
    ppermute x9, waiting for transfers between devices, fan_out(): lax.ppermute(value, BOTH, [(i, j) for i, j in pairs if 0 <= j < 2 * count])  1.82 us
  transfers between devices with their start and end apart: 37, of which 9 were waited for; matrix products, arithmetic and copies ran while one was open for 3% of the time, Pallas kernels for 8%

profile of v4, /device:TPU:0, one launch (start us, length us, event | category | flops | bytes accessed | tf_op | source)
XLA Modules:
  0.0 72.0 jit_solution(5337286130562668654)
XLA Ops:
  0.7 3.0 %collective-permute-start = (bf16[16,4096]{1,0:T(8,128)(2,1)}, bf16[16,4096]{1,0:T(8,128)(2,1)S(1)}, u32[]{:S(2)}, u32[]{:S(2)}) collective-permute-start(bf16[16,4096]{1,0:T(8,128)(2,1)} %bitcast.19), channel_id=1, source_target_pairs={{0,2},{2,0},{4,6},{6,4},{8,10},{10,8},{12,14},{14,12},{1,3},{3,1},... | collective-permute-start | bytes 393224 | tf_op jit(solution)/shard_map/ppermute | solution.py:28
  3.7 1.6 %collective-permute-start.1 = (bf16[16,4096]{1,0:T(8,128)(2,1)}, bf16[16,4096]{1,0:T(8,128)(2,1)S(1)}, u32[]{:S(2)}, u32[]{:S(2)}) collective-permute-start(bf16[16,4096]{1,0:T(8,128)(2,1)} %bitcast.20), channel_id=1, source_target_pairs={{0,4},{2,6},{4,0},{6,2},{8,12},{10,14},{12,8},{14,10},{1,5},{3,7},... | collective-permute-start | bytes 393224 | tf_op jit(solution)/shard_map/ppermute | solution.py:28
  5.2 2.6 %collective-permute-start.3 = (bf16[16,4096]{1,0:T(8,128)(2,1)}, bf16[16,4096]{1,0:T(8,128)(2,1)S(1)}, u32[]{:S(2)}, u32[]{:S(2)}) collective-permute-start(bf16[16,4096]{1,0:T(8,128)(2,1)} %bitcast.21), channel_id=1, source_target_pairs={{0,8},{2,10},{4,12},{6,14},{8,0},{10,2},{12,4},{14,6},{1,9},{3,11}... | collective-permute-start | bytes 393224 | tf_op jit(solution)/shard_map/ppermute | solution.py:28
  7.8 0.7 %pad_add_fusion.docs_ref = s32[8]{0:T(128)S(1)} fusion(s32[4]{0:T(128)} %param.13, s32[4]{0:T(128)} %param.12), kind=kLoop, calls=%fused_computation.11 | loop fusion | flops 8 | bytes 64 | tf_op jit(solution)/shard_map/concatenate | solution.py:330
  9.9 2.7 %collective-permute-start.12 = (bf16[16,4096]{1,0:T(8,128)(2,1)S(1)}, bf16[16,4096]{1,0:T(8,128)(2,1)S(1)}, u32[]{:S(2)}, u32[]{:S(2)}) collective-permute-start(bf16[16,4096]{1,0:T(8,128)(2,1)S(1)} %bitcast.22), channel_id=1, source_target_pairs={{0,12},{2,14},{4,8},{6,10},{8,4},{10,6},{12,0},{14,2},{1,13},{3,15... | collective-permute-start | bytes 393224 | tf_op jit(solution)/shard_map/ppermute | solution.py:28
  12.6 1.5 %collective-permute-start.2 = (bf16[16,4096]{1,0:T(8,128)(2,1)S(1)}, bf16[16,4096]{1,0:T(8,128)(2,1)S(1)}, u32[]{:S(2)}, u32[]{:S(2)}) collective-permute-start(bf16[16,4096]{1,0:T(8,128)(2,1)S(1)} %collective-permute-done.1.z1), channel_id=1, source_target_pairs={{0,2},{2,0},{4,6},{6,4},{8,10},{10,8},{12,14},{14,12},{1,3},{3,1},... | collective-permute-start | bytes 393224 | tf_op jit(solution)/shard_map/ppermute | solution.py:28
  14.7 3.2 %collective-permute-start.6 = (bf16[256,128]{1,0:T(8,128)(2,1)S(1)}, bf16[256,128]{1,0:T(8,128)(2,1)S(1)}, u32[]{:S(2)}, u32[]{:S(2)}) collective-permute-start(bf16[256,128]{1,0:T(8,128)(2,1)S(1)} %copy-done.2), channel_id=1, source_target_pairs={{0,4},{2,6},{3,5},{4,0},{5,3},{6,2},{7,9},{8,12},{9,7},{10,14},{11... | collective-permute-start | bytes 196616 | tf_op jit(solution)/shard_map/ppermute | solution.py:45
  17.9 3.8 %collective-permute-start.4 = (bf16[16,4096]{1,0:T(8,128)(2,1)S(1)}, bf16[16,4096]{1,0:T(8,128)(2,1)S(1)}, u32[]{:S(2)}, u32[]{:S(2)}) collective-permute-start(bf16[16,4096]{1,0:T(8,128)(2,1)S(1)} %collective-permute-done.3.z2), channel_id=1, source_target_pairs={{0,2},{2,0},{4,6},{6,4},{8,10},{10,8},{12,14},{14,12},{1,3},{3,1},... | collective-permute-start | bytes 393224 | tf_op jit(solution)/shard_map/ppermute | solution.py:28
  22.7 3.7 %collective-permute-start.13 = (bf16[16,4096]{1,0:T(8,128)(2,1)S(1)}, bf16[16,4096]{1,0:T(8,128)(2,1)S(1)}, u32[]{:S(2)}, u32[]{:S(2)}) collective-permute-start(bf16[16,4096]{1,0:T(8,128)(2,1)S(1)} %collective-permute-done.12.z3), channel_id=1, source_target_pairs={{0,2},{2,0},{4,6},{6,4},{8,10},{10,8},{12,14},{14,12},{1,3},{3,1},... | collective-permute-start | bytes 393224 | tf_op jit(solution)/shard_map/ppermute | solution.py:28
  26.7 1.5 %shard_map.103 = (bf16[2,7,256,512]{3,2,1,0:T(8,128)(2,1)S(1)}, bf16[1792,128]{1,0:T(8,128)(2,1)S(1)}, f32[256,128]{1,0:T(8,128)S(1)}, f32[3,256,128]{2,1,0:T(8,128)S(1)}, bf16[3,256,128]{2,1,0:T(8,128)(2,1)S(1)}) custom-call(s32[2,8,128]{2,1,0:T(8,128)S(1)} %shard_map.102.info_ref, bf16[2,512,128]{2,1,0:T(8,128)(2,1)S(1)} %bitcast.15, ...), custom_call_target="tpu_custom_call" | custom-call | flops 1073741824 | bytes 4194304 | tf_op jit(solution)/shard_map/pallas_call | solution.py:305
  28.3 1.8 %collective-permute-done.13.c3 = bf16[16,4096]{1,0:T(8,128)(2,1)S(1)} collective-permute-done((bf16[16,4096]{1,0:T(8,128)(2,1)S(1)}, bf16[16,4096]{1,0:T(8,128)(2,1)S(1)}, u32[]{:S(2)}, u32[]{:S(2)}) %collective-permute-start.13) | collective-permute-done | bytes 131104 | tf_op jit(solution)/shard_map/ppermute | solution.py:28
  30.1 0.8 %shard_map.104 = (f32[256,128]{1,0:T(8,128)S(1)}, bf16[128,4096]{1,0:T(8,128)(2,1)S(1)}) custom-call(bf16[256,4096]{1,0:T(8,128)(2,1)S(1)} %copy-done, bf16[16,4096]{1,0:T(8,128)(2,1)S(1)} %bitcast.23, bf16[16,4096]{1,0:T(8,128)(2,1)S(1)} %collective-permute-done.1.z1, bf16[16,4096]{1,0:T(8,128)(2,1)S(1)} %collective-permute-done.3.z2, ...), custom_call_target="tpu_custom_call" | custom-call | flops 1073741824 | bytes 4194304 | tf_op jit(solution)/shard_map/pallas_call | solution.py:305
  31.0 1.3 %collective-permute-done.14.other_ref = f32[256,128]{1,0:T(8,128)S(1)} collective-permute-done((f32[256,128]{1,0:T(8,128)S(1)}, f32[256,128]{1,0:T(8,128)S(1)}, u32[]{:S(2)}, u32[]{:S(2)}) %collective-permute-start.14) | collective-permute-done | bytes 131104 | tf_op jit(solution)/shard_map/ppermute | solution.py:23
  33.1 2.0 %collective-permute-start.17 = (bf16[2,256,128]{2,1,0:T(8,128)(2,1)S(1)}, bf16[2,256,128]{2,1,0:T(8,128)(2,1)S(1)}, u32[]{:S(2)}, u32[]{:S(2)}) collective-permute-start(bf16[2,256,128]{2,1,0:T(8,128)(2,1)S(1)} %get-tuple-element.48), channel_id=1, source_target_pairs={{0,4},{2,6},{3,5},{4,0},{5,3},{6,2},{7,9},{8,12},{9,7},{10,14},{11... | collective-permute-start | bytes 393224 | tf_op jit(solution)/shard_map/ppermute | solution.py:45
  35.0 0.9 %collective-permute-start.18 = (bf16[2,256,128]{2,1,0:T(8,128)(2,1)S(1)}, bf16[2,256,128]{2,1,0:T(8,128)(2,1)S(1)}, u32[]{:S(2)}, u32[]{:S(2)}) collective-permute-start(bf16[2,256,128]{2,1,0:T(8,128)(2,1)S(1)} %get-tuple-element.49), channel_id=1, source_target_pairs={{1,3},{3,1},{4,8},{5,7},{6,10},{7,5},{8,4},{9,11},{10,6},{11,9},{1... | collective-permute-start | bytes 393224 | tf_op jit(solution)/shard_map/ppermute | solution.py:45
  35.9 4.5 %collective-permute-start.11 = (f32[256,128]{1,0:T(8,128)S(1)}, f32[256,128]{1,0:T(8,128)S(1)}, u32[]{:S(2)}, u32[]{:S(2)}) collective-permute-start(f32[256,128]{1,0:T(8,128)S(1)} %get-tuple-element.43.a_ref), channel_id=1, source_target_pairs={{0,1},{1,0},{2,3},{3,2},{4,5},{5,4},{6,7},{7,6},{8,9},{9,8},{10,11... | collective-permute-start | bytes 393224 | tf_op jit(solution)/shard_map/ppermute | solution.py:23
  40.5 1.4 %collective-permute-done.17.r2 = bf16[2,256,128]{2,1,0:T(8,128)(2,1)S(1)} collective-permute-done((bf16[2,256,128]{2,1,0:T(8,128)(2,1)S(1)}, bf16[2,256,128]{2,1,0:T(8,128)(2,1)S(1)}, u32[]{:S(2)}, u32[]{:S(2)}) %collective-permute-start.17) | collective-permute-done | bytes 131104 | tf_op jit(solution)/shard_map/ppermute | solution.py:45
  41.8 1.3 %collective-permute-start.21 = (bf16[2,256,128]{2,1,0:T(8,128)(2,1)S(1)}, bf16[2,256,128]{2,1,0:T(8,128)(2,1)S(1)}, u32[]{:S(2)}, u32[]{:S(2)}) collective-permute-start(bf16[2,256,128]{2,1,0:T(8,128)(2,1)S(1)} %collective-permute-done.18.r3), channel_id=1, source_target_pairs={{0,1},{1,0},{2,3},{3,2},{4,5},{5,4},{6,7},{7,6},{8,9},{9,8},{10,11... | collective-permute-start | bytes 393224 | tf_op jit(solution)/shard_map/ppermute | solution.py:23
  43.2 0.9 %collective-permute-done.21.s3 = bf16[2,256,128]{2,1,0:T(8,128)(2,1)S(1)} collective-permute-done((bf16[2,256,128]{2,1,0:T(8,128)(2,1)S(1)}, bf16[2,256,128]{2,1,0:T(8,128)(2,1)S(1)}, u32[]{:S(2)}, u32[]{:S(2)}) %collective-permute-start.21) | collective-permute-done | bytes 131104 | tf_op jit(solution)/shard_map/ppermute | solution.py:23
  44.7 2.9 %collective-permute-start.30 = (bf16[16,4096]{1,0:T(8,128)(2,1)S(1)}, bf16[16,4096]{1,0:T(8,128)(2,1)S(1)}, u32[]{:S(2)}, u32[]{:S(2)}) collective-permute-start(bf16[16,4096]{1,0:T(8,128)(2,1)S(1)} %get-tuple-element.64), channel_id=1, source_target_pairs={{0,2},{2,0},{4,6},{6,4},{8,10},{10,8},{12,14},{14,12},{1,3},{3,1},... | collective-permute-start | bytes 393224 | tf_op jit(solution)/shard_map/ppermute | solution.py:28
  47.7 1.9 %collective-permute-start.34 = (bf16[16,4096]{1,0:T(8,128)(2,1)S(1)}, bf16[16,4096]{1,0:T(8,128)(2,1)S(1)}, u32[]{:S(2)}, u32[]{:S(2)}) collective-permute-start(bf16[16,4096]{1,0:T(8,128)(2,1)S(1)} %get-tuple-element.68), channel_id=1, source_target_pairs={{0,2},{2,0},{4,6},{6,4},{8,10},{10,8},{12,14},{14,12},{1,3},{3,1},... | collective-permute-start | bytes 393224 | tf_op jit(solution)/shard_map/ppermute | solution.py:28
  49.7 1.4 %shard_map.107 = (f32[2,128,512]{2,1,0:T(8,128)S(1)}, f32[256,128]{1,0:T(8,128)S(1)}, f32[3,256,128]{2,1,0:T(8,128)S(1)}, bf16[3,256,128]{2,1,0:T(8,128)(2,1)S(1)}) custom-call(s32[2,8,128]{2,1,0:T(8,128)S(1)} %shard_map.102.info_ref, bf16[2,512,128]{2,1,0:T(8,128)(2,1)S(1)} %bitcast.16, bf16[2,512,128]{2,1,0:T(8,128)(2,1)S(1)} %bitcast.18, ...), custom_call_target="tpu_custom_call" | custom-call | flops 1073741824 | bytes 4194304 | tf_op jit(solution)/shard_map/pallas_call | solution.py:305
  51.2 0.7 collective-permute-done.30
  51.9 2.8 %collective-permute-start.31 = (bf16[16,4096]{1,0:T(8,128)(2,1)S(1)}, bf16[16,4096]{1,0:T(8,128)(2,1)S(1)}, u32[]{:S(2)}, u32[]{:S(2)}) collective-permute-start(bf16[16,4096]{1,0:T(8,128)(2,1)S(1)} %add_convert_fusion.2), channel_id=1, source_target_pairs={{0,12},{2,14},{4,8},{6,10},{8,4},{10,6},{12,0},{14,2},{1,13},{3,15... | collective-permute-start | bytes 393224 | tf_op jit(solution)/shard_map/ppermute | solution.py:28
  54.7 4.6 %collective-permute-start.33 = (bf16[16,4096]{1,0:T(8,128)(2,1)S(1)}, bf16[16,4096]{1,0:T(8,128)(2,1)S(1)}, u32[]{:S(2)}, u32[]{:S(2)}) collective-permute-start(bf16[16,4096]{1,0:T(8,128)(2,1)S(1)} %add_convert_fusion.1), channel_id=1, source_target_pairs={{0,8},{2,10},{4,12},{6,14},{8,0},{10,2},{12,4},{14,6},{1,9},{3,11}... | collective-permute-start | bytes 393224 | tf_op jit(solution)/shard_map/ppermute | solution.py:28
  59.4 1.3 %collective-permute-start.35 = (bf16[16,4096]{1,0:T(8,128)(2,1)S(1)}, bf16[16,4096]{1,0:T(8,128)(2,1)S(1)}, u32[]{:S(2)}, u32[]{:S(2)}) collective-permute-start(bf16[16,4096]{1,0:T(8,128)(2,1)S(1)} %add_convert_fusion), channel_id=1, source_target_pairs={{0,4},{2,6},{4,0},{6,2},{8,12},{10,14},{12,8},{14,10},{1,5},{3,7},... | collective-permute-start | bytes 393224 | tf_op jit(solution)/shard_map/ppermute | solution.py:28
  61.4 3.1 %collective-permute-start.26 = (bf16[256,128]{1,0:T(8,128)(2,1)S(1)}, bf16[256,128]{1,0:T(8,128)(2,1)S(1)}, u32[]{:S(2)}, u32[]{:S(2)}) collective-permute-start(bf16[256,128]{1,0:T(8,128)(2,1)S(1)} %get-tuple-element.72), channel_id=1, source_target_pairs={{0,4},{2,6},{3,5},{4,0},{5,3},{6,2},{7,9},{8,12},{9,7},{10,14},{11... | collective-permute-start | bytes 196616 | tf_op jit(solution)/shard_map/ppermute | solution.py:45
  65.2 1.7 %shard_map.108 = (bf16[256,4096]{1,0:T(8,128)(2,1)}, bf16[256,512]{1,0:T(8,128)(2,1)}) custom-call(bf16[256,128]{1,0:T(8,128)(2,1)S(1)} %get-tuple-element.50.grad_ref, bf16[128,4096]{1,0:T(8,128)(2,1)S(1)} %get-tuple-element.51.weight_ref, f32[2,128,512]{2,1,0:T(8,128)S(1)} %get-tuple-element.56.query_ref), custom_call_target="tpu_custom_call" | custom-call | flops 1073741824 | bytes 4194304 | tf_op jit(solution)/shard_map/pallas_call | solution.py:305
  66.9 1.1 %collective-permute-done.33 = bf16[16,4096]{1,0:T(8,128)(2,1)S(1)} collective-permute-done((bf16[16,4096]{1,0:T(8,128)(2,1)S(1)}, bf16[16,4096]{1,0:T(8,128)(2,1)S(1)}, u32[]{:S(2)}, u32[]{:S(2)}) %collective-permute-start.33) | collective-permute-done | bytes 131104 | tf_op jit(solution)/shard_map/ppermute | solution.py:28
  68.0 1.5 %collective-permute-start.22 = (f32[256,128]{1,0:T(8,128)S(1)}, f32[256,128]{1,0:T(8,128)S(1)}, u32[]{:S(2)}, u32[]{:S(2)}) collective-permute-start(f32[256,128]{1,0:T(8,128)S(1)} %get-tuple-element.59), channel_id=1, source_target_pairs={{0,1},{1,0},{2,3},{3,2},{4,5},{5,4},{6,7},{7,6},{8,9},{9,8},{10,11... | collective-permute-start | bytes 393224 | tf_op jit(solution)/shard_map/ppermute | solution.py:23
  70.1 0.8 %add_bitcast_fusion = f32[4096,16]{0,1:T(8,128)} fusion(bf16[16,4096]{1,0:T(8,128)(2,1)S(1)} %collective-permute-done.36, bf16[16,4096]{1,0:T(8,128)(2,1)S(1)} %collective-permute-done.35, bf16[16,4096]{1,0:T(8,128)(2,1)S(1)} %collective-permute-done.33, f32[16,4096]{1,0:T(8,128)S(1)} %get-tuple-element.62, bf16[16,4096]{1,0:T(8,128)(2,1)S(1)} %collective-permute-done.31), kind=kLoop, calls=%fused_computation | loop fusion | flops 524288 | bytes 1048576 | tf_op jit(solution)/shard_map/transpose | solution.py:401
  71.3 0.7 add_convert_fusion.3
  (70 shorter events, 7.5 us)
Async XLA Ops:
  0.7 7.9 %collective-permute-start = (bf16[16,4096]{1,0:T(8,128)(2,1)}, bf16[16,4096]{1,0:T(8,128)(2,1)S(1)}, u32[]{:S(2)}, u32[]{:S(2)}) collective-permute-start(bf16[16,4096]{1,0:T(8,128)(2,1)} %bitcast.19), channel_id=1, source_target_pairs={{0,2},{2,0},{4,6},{6,4},{8,10},{10,8},{12,14},{14,12},{1,3},{3,1},... | collective-permute-start | bytes 393224 | tf_op jit(solution)/shard_map/ppermute | solution.py:28
  3.7 8.9 %collective-permute-start.1 = (bf16[16,4096]{1,0:T(8,128)(2,1)}, bf16[16,4096]{1,0:T(8,128)(2,1)S(1)}, u32[]{:S(2)}, u32[]{:S(2)}) collective-permute-start(bf16[16,4096]{1,0:T(8,128)(2,1)} %bitcast.20), channel_id=1, source_target_pairs={{0,4},{2,6},{4,0},{6,2},{8,12},{10,14},{12,8},{14,10},{1,5},{3,7},... | collective-permute-start | bytes 393224 | tf_op jit(solution)/shard_map/ppermute | solution.py:28
  5.2 9.5 %collective-permute-start.3 = (bf16[16,4096]{1,0:T(8,128)(2,1)}, bf16[16,4096]{1,0:T(8,128)(2,1)S(1)}, u32[]{:S(2)}, u32[]{:S(2)}) collective-permute-start(bf16[16,4096]{1,0:T(8,128)(2,1)} %bitcast.21), channel_id=1, source_target_pairs={{0,8},{2,10},{4,12},{6,14},{8,0},{10,2},{12,4},{14,6},{1,9},{3,11}... | collective-permute-start | bytes 393224 | tf_op jit(solution)/shard_map/ppermute | solution.py:28
  9.2 8.7 %collective-permute-start.7 = (bf16[256,128]{1,0:T(8,128)(2,1)S(1)}, bf16[256,128]{1,0:T(8,128)(2,1)S(1)}, u32[]{:S(2)}, u32[]{:S(2)}) collective-permute-start(bf16[256,128]{1,0:T(8,128)(2,1)S(1)} %copy-done.2), channel_id=1, source_target_pairs={{1,3},{3,1},{4,8},{5,7},{6,10},{7,5},{8,4},{9,11},{10,6},{11,9},{1... | collective-permute-start | bytes 196616 | tf_op jit(solution)/shard_map/ppermute | solution.py:45
  9.9 12.4 %collective-permute-start.12 = (bf16[16,4096]{1,0:T(8,128)(2,1)S(1)}, bf16[16,4096]{1,0:T(8,128)(2,1)S(1)}, u32[]{:S(2)}, u32[]{:S(2)}) collective-permute-start(bf16[16,4096]{1,0:T(8,128)(2,1)S(1)} %bitcast.22), channel_id=1, source_target_pairs={{0,12},{2,14},{4,8},{6,10},{8,4},{10,6},{12,0},{14,2},{1,13},{3,15... | collective-permute-start | bytes 393224 | tf_op jit(solution)/shard_map/ppermute | solution.py:28
  12.6 10.1 %collective-permute-start.2 = (bf16[16,4096]{1,0:T(8,128)(2,1)S(1)}, bf16[16,4096]{1,0:T(8,128)(2,1)S(1)}, u32[]{:S(2)}, u32[]{:S(2)}) collective-permute-start(bf16[16,4096]{1,0:T(8,128)(2,1)S(1)} %collective-permute-done.1.z1), channel_id=1, source_target_pairs={{0,2},{2,0},{4,6},{6,4},{8,10},{10,8},{12,14},{14,12},{1,3},{3,1},... | collective-permute-start | bytes 393224 | tf_op jit(solution)/shard_map/ppermute | solution.py:28
  14.1 7.6 %collective-permute-start.5 = (bf16[256,128]{1,0:T(8,128)(2,1)S(1)}, bf16[256,128]{1,0:T(8,128)(2,1)S(1)}, u32[]{:S(2)}, u32[]{:S(2)}) collective-permute-start(bf16[256,128]{1,0:T(8,128)(2,1)S(1)} %copy-done.2), channel_id=1, source_target_pairs={{1,7},{2,8},{5,11},{6,12},{7,1},{8,2},{9,15},{11,5},{12,6},{15,9},... | collective-permute-start | bytes 196616 | tf_op jit(solution)/shard_map/ppermute | solution.py:45
  14.7 7.4 %collective-permute-start.6 = (bf16[256,128]{1,0:T(8,128)(2,1)S(1)}, bf16[256,128]{1,0:T(8,128)(2,1)S(1)}, u32[]{:S(2)}, u32[]{:S(2)}) collective-permute-start(bf16[256,128]{1,0:T(8,128)(2,1)S(1)} %copy-done.2), channel_id=1, source_target_pairs={{0,4},{2,6},{3,5},{4,0},{5,3},{6,2},{7,9},{8,12},{9,7},{10,14},{11... | collective-permute-start | bytes 196616 | tf_op jit(solution)/shard_map/ppermute | solution.py:45
  17.9 8.7 %collective-permute-start.4 = (bf16[16,4096]{1,0:T(8,128)(2,1)S(1)}, bf16[16,4096]{1,0:T(8,128)(2,1)S(1)}, u32[]{:S(2)}, u32[]{:S(2)}) collective-permute-start(bf16[16,4096]{1,0:T(8,128)(2,1)S(1)} %collective-permute-done.3.z2), channel_id=1, source_target_pairs={{0,2},{2,0},{4,6},{6,4},{8,10},{10,8},{12,14},{14,12},{1,3},{3,1},... | collective-permute-start | bytes 393224 | tf_op jit(solution)/shard_map/ppermute | solution.py:28
  21.7 4.9 %collective-permute-start.10 = (bf16[256,128]{1,0:T(8,128)(2,1)S(1)}, bf16[256,128]{1,0:T(8,128)(2,1)S(1)}, u32[]{:S(2)}, u32[]{:S(2)}) collective-permute-start(bf16[256,128]{1,0:T(8,128)(2,1)S(1)} %collective-permute-done.7.r3), channel_id=1, source_target_pairs={{0,1},{1,0},{2,3},{3,2},{4,5},{5,4},{6,7},{7,6},{8,9},{9,8},{10,11... | collective-permute-start | bytes 196616 | tf_op jit(solution)/shard_map/ppermute | solution.py:23
  22.2 4.5 %collective-permute-start.8 = (bf16[256,128]{1,0:T(8,128)(2,1)S(1)}, bf16[256,128]{1,0:T(8,128)(2,1)S(1)}, u32[]{:S(2)}, u32[]{:S(2)}) collective-permute-start(bf16[256,128]{1,0:T(8,128)(2,1)S(1)} %collective-permute-done.5.r1), channel_id=1, source_target_pairs={{0,1},{1,0},{2,3},{3,2},{4,5},{5,4},{6,7},{7,6},{8,9},{9,8},{10,11... | collective-permute-start | bytes 196616 | tf_op jit(solution)/shard_map/ppermute | solution.py:23
  22.2 4.4 %collective-permute-start.9 = (bf16[256,128]{1,0:T(8,128)(2,1)S(1)}, bf16[256,128]{1,0:T(8,128)(2,1)S(1)}, u32[]{:S(2)}, u32[]{:S(2)}) collective-permute-start(bf16[256,128]{1,0:T(8,128)(2,1)S(1)} %collective-permute-done.6.r2), channel_id=1, source_target_pairs={{0,1},{1,0},{2,3},{3,2},{4,5},{5,4},{6,7},{7,6},{8,9},{9,8},{10,11... | collective-permute-start | bytes 196616 | tf_op jit(solution)/shard_map/ppermute | solution.py:23
  22.7 7.4 %collective-permute-start.13 = (bf16[16,4096]{1,0:T(8,128)(2,1)S(1)}, bf16[16,4096]{1,0:T(8,128)(2,1)S(1)}, u32[]{:S(2)}, u32[]{:S(2)}) collective-permute-start(bf16[16,4096]{1,0:T(8,128)(2,1)S(1)} %collective-permute-done.12.z3), channel_id=1, source_target_pairs={{0,2},{2,0},{4,6},{6,4},{8,10},{10,8},{12,14},{14,12},{1,3},{3,1},... | collective-permute-start | bytes 393224 | tf_op jit(solution)/shard_map/ppermute | solution.py:28
  28.2 4.1 %collective-permute-start.15 = (bf16[3,256,128]{2,1,0:T(8,128)(2,1)S(1)}, bf16[3,256,128]{2,1,0:T(8,128)(2,1)S(1)}, u32[]{:S(2)}, u32[]{:S(2)}) collective-permute-start(bf16[3,256,128]{2,1,0:T(8,128)(2,1)S(1)} %get-tuple-element.46), channel_id=1, source_target_pairs={{0,1},{1,0},{2,3},{3,2},{4,5},{5,4},{6,7},{7,6},{8,9},{9,8},{10,11... | collective-permute-start | bytes 589832 | tf_op jit(solution)/shard_map/ppermute | solution.py:23
  32.4 8.0 %collective-permute-start.16 = (bf16[2,256,128]{2,1,0:T(8,128)(2,1)S(1)}, bf16[2,256,128]{2,1,0:T(8,128)(2,1)S(1)}, u32[]{:S(2)}, u32[]{:S(2)}) collective-permute-start(bf16[2,256,128]{2,1,0:T(8,128)(2,1)S(1)} %get-tuple-element.47), channel_id=1, source_target_pairs={{1,7},{2,8},{5,11},{6,12},{7,1},{8,2},{9,15},{11,5},{12,6},{15,9},... | collective-permute-start | bytes 393224 | tf_op jit(solution)/shard_map/ppermute | solution.py:45
  33.1 8.8 %collective-permute-start.17 = (bf16[2,256,128]{2,1,0:T(8,128)(2,1)S(1)}, bf16[2,256,128]{2,1,0:T(8,128)(2,1)S(1)}, u32[]{:S(2)}, u32[]{:S(2)}) collective-permute-start(bf16[2,256,128]{2,1,0:T(8,128)(2,1)S(1)} %get-tuple-element.48), channel_id=1, source_target_pairs={{0,4},{2,6},{3,5},{4,0},{5,3},{6,2},{7,9},{8,12},{9,7},{10,14},{11... | collective-permute-start | bytes 393224 | tf_op jit(solution)/shard_map/ppermute | solution.py:45
  35.0 6.8 %collective-permute-start.18 = (bf16[2,256,128]{2,1,0:T(8,128)(2,1)S(1)}, bf16[2,256,128]{2,1,0:T(8,128)(2,1)S(1)}, u32[]{:S(2)}, u32[]{:S(2)}) collective-permute-start(bf16[2,256,128]{2,1,0:T(8,128)(2,1)S(1)} %get-tuple-element.49), channel_id=1, source_target_pairs={{1,3},{3,1},{4,8},{5,7},{6,10},{7,5},{8,4},{9,11},{10,6},{11,9},{1... | collective-permute-start | bytes 393224 | tf_op jit(solution)/shard_map/ppermute | solution.py:45
  35.9 7.2 %collective-permute-start.11 = (f32[256,128]{1,0:T(8,128)S(1)}, f32[256,128]{1,0:T(8,128)S(1)}, u32[]{:S(2)}, u32[]{:S(2)}) collective-permute-start(f32[256,128]{1,0:T(8,128)S(1)} %get-tuple-element.43.a_ref), channel_id=1, source_target_pairs={{0,1},{1,0},{2,3},{3,2},{4,5},{5,4},{6,7},{7,6},{8,9},{9,8},{10,11... | collective-permute-start | bytes 393224 | tf_op jit(solution)/shard_map/ppermute | solution.py:23
  40.4 2.7 %collective-permute-start.19 = (bf16[2,256,128]{2,1,0:T(8,128)(2,1)S(1)}, bf16[2,256,128]{2,1,0:T(8,128)(2,1)S(1)}, u32[]{:S(2)}, u32[]{:S(2)}) collective-permute-start(bf16[2,256,128]{2,1,0:T(8,128)(2,1)S(1)} %collective-permute-done.16.r1), channel_id=1, source_target_pairs={{0,1},{1,0},{2,3},{3,2},{4,5},{5,4},{6,7},{7,6},{8,9},{9,8},{10,11... | collective-permute-start | bytes 393224 | tf_op jit(solution)/shard_map/ppermute | solution.py:23
  41.8 2.2 %collective-permute-start.21 = (bf16[2,256,128]{2,1,0:T(8,128)(2,1)S(1)}, bf16[2,256,128]{2,1,0:T(8,128)(2,1)S(1)}, u32[]{:S(2)}, u32[]{:S(2)}) collective-permute-start(bf16[2,256,128]{2,1,0:T(8,128)(2,1)S(1)} %collective-permute-done.18.r3), channel_id=1, source_target_pairs={{0,1},{1,0},{2,3},{3,2},{4,5},{5,4},{6,7},{7,6},{8,9},{9,8},{10,11... | collective-permute-start | bytes 393224 | tf_op jit(solution)/shard_map/ppermute | solution.py:23
  44.7 7.1 %collective-permute-start.30 = (bf16[16,4096]{1,0:T(8,128)(2,1)S(1)}, bf16[16,4096]{1,0:T(8,128)(2,1)S(1)}, u32[]{:S(2)}, u32[]{:S(2)}) collective-permute-start(bf16[16,4096]{1,0:T(8,128)(2,1)S(1)} %get-tuple-element.64), channel_id=1, source_target_pairs={{0,2},{2,0},{4,6},{6,4},{8,10},{10,8},{12,14},{14,12},{1,3},{3,1},... | collective-permute-start | bytes 393224 | tf_op jit(solution)/shard_map/ppermute | solution.py:28
  47.6 7.1 %collective-permute-start.32 = (bf16[16,4096]{1,0:T(8,128)(2,1)S(1)}, bf16[16,4096]{1,0:T(8,128)(2,1)S(1)}, u32[]{:S(2)}, u32[]{:S(2)}) collective-permute-start(bf16[16,4096]{1,0:T(8,128)(2,1)S(1)} %get-tuple-element.66), channel_id=1, source_target_pairs={{0,2},{2,0},{4,6},{6,4},{8,10},{10,8},{12,14},{14,12},{1,3},{3,1},... | collective-permute-start | bytes 393224 | tf_op jit(solution)/shard_map/ppermute | solution.py:28
  47.7 11.7 %collective-permute-start.34 = (bf16[16,4096]{1,0:T(8,128)(2,1)S(1)}, bf16[16,4096]{1,0:T(8,128)(2,1)S(1)}, u32[]{:S(2)}, u32[]{:S(2)}) collective-permute-start(bf16[16,4096]{1,0:T(8,128)(2,1)S(1)} %get-tuple-element.68), channel_id=1, source_target_pairs={{0,2},{2,0},{4,6},{6,4},{8,10},{10,8},{12,14},{14,12},{1,3},{3,1},... | collective-permute-start | bytes 393224 | tf_op jit(solution)/shard_map/ppermute | solution.py:28
  49.6 11.8 %collective-permute-start.36 = (bf16[16,4096]{1,0:T(8,128)(2,1)S(1)}, bf16[16,4096]{1,0:T(8,128)(2,1)S(1)}, u32[]{:S(2)}, u32[]{:S(2)}) collective-permute-start(bf16[16,4096]{1,0:T(8,128)(2,1)S(1)} %get-tuple-element.69), channel_id=1, source_target_pairs={{0,2},{2,0},{4,6},{6,4},{8,10},{10,8},{12,14},{14,12},{1,3},{3,1},... | collective-permute-start | bytes 393224 | tf_op jit(solution)/shard_map/ppermute | solution.py:28
  51.1 9.6 %collective-permute-start.23 = (bf16[3,256,128]{2,1,0:T(8,128)(2,1)S(1)}, bf16[3,256,128]{2,1,0:T(8,128)(2,1)S(1)}, u32[]{:S(2)}, u32[]{:S(2)}) collective-permute-start(bf16[3,256,128]{2,1,0:T(8,128)(2,1)S(1)} %get-tuple-element.61), channel_id=1, source_target_pairs={{0,1},{1,0},{2,3},{3,2},{4,5},{5,4},{6,7},{7,6},{8,9},{9,8},{10,11... | collective-permute-start | bytes 589832 | tf_op jit(solution)/shard_map/ppermute | solution.py:23
  51.9 12.6 %collective-permute-start.31 = (bf16[16,4096]{1,0:T(8,128)(2,1)S(1)}, bf16[16,4096]{1,0:T(8,128)(2,1)S(1)}, u32[]{:S(2)}, u32[]{:S(2)}) collective-permute-start(bf16[16,4096]{1,0:T(8,128)(2,1)S(1)} %add_convert_fusion.2), channel_id=1, source_target_pairs={{0,12},{2,14},{4,8},{6,10},{8,4},{10,6},{12,0},{14,2},{1,13},{3,15... | collective-permute-start | bytes 393224 | tf_op jit(solution)/shard_map/ppermute | solution.py:28
  54.7 13.3 %collective-permute-start.33 = (bf16[16,4096]{1,0:T(8,128)(2,1)S(1)}, bf16[16,4096]{1,0:T(8,128)(2,1)S(1)}, u32[]{:S(2)}, u32[]{:S(2)}) collective-permute-start(bf16[16,4096]{1,0:T(8,128)(2,1)S(1)} %add_convert_fusion.1), channel_id=1, source_target_pairs={{0,8},{2,10},{4,12},{6,14},{8,0},{10,2},{12,4},{14,6},{1,9},{3,11}... | collective-permute-start | bytes 393224 | tf_op jit(solution)/shard_map/ppermute | solution.py:28
  59.4 10.8 %collective-permute-start.35 = (bf16[16,4096]{1,0:T(8,128)(2,1)S(1)}, bf16[16,4096]{1,0:T(8,128)(2,1)S(1)}, u32[]{:S(2)}, u32[]{:S(2)}) collective-permute-start(bf16[16,4096]{1,0:T(8,128)(2,1)S(1)} %add_convert_fusion), channel_id=1, source_target_pairs={{0,4},{2,6},{4,0},{6,2},{8,12},{10,14},{12,8},{14,10},{1,5},{3,7},... | collective-permute-start | bytes 393224 | tf_op jit(solution)/shard_map/ppermute | solution.py:28
  60.7 8.8 %collective-permute-start.24 = (bf16[256,128]{1,0:T(8,128)(2,1)S(1)}, bf16[256,128]{1,0:T(8,128)(2,1)S(1)}, u32[]{:S(2)}, u32[]{:S(2)}) collective-permute-start(bf16[256,128]{1,0:T(8,128)(2,1)S(1)} %get-tuple-element.70), channel_id=1, source_target_pairs={{1,7},{2,8},{5,11},{6,12},{7,1},{8,2},{9,15},{11,5},{12,6},{15,9},... | collective-permute-start | bytes 196616 | tf_op jit(solution)/shard_map/ppermute | solution.py:45
  61.4 8.2 %collective-permute-start.26 = (bf16[256,128]{1,0:T(8,128)(2,1)S(1)}, bf16[256,128]{1,0:T(8,128)(2,1)S(1)}, u32[]{:S(2)}, u32[]{:S(2)}) collective-permute-start(bf16[256,128]{1,0:T(8,128)(2,1)S(1)} %get-tuple-element.72), channel_id=1, source_target_pairs={{0,4},{2,6},{3,5},{4,0},{5,3},{6,2},{7,9},{8,12},{9,7},{10,14},{11... | collective-permute-start | bytes 196616 | tf_op jit(solution)/shard_map/ppermute | solution.py:45
  64.5 5.5 %collective-permute-start.28 = (bf16[256,128]{1,0:T(8,128)(2,1)S(1)}, bf16[256,128]{1,0:T(8,128)(2,1)S(1)}, u32[]{:S(2)}, u32[]{:S(2)}) collective-permute-start(bf16[256,128]{1,0:T(8,128)(2,1)S(1)} %get-tuple-element.71), channel_id=1, source_target_pairs={{1,3},{3,1},{4,8},{5,7},{6,10},{7,5},{8,4},{9,11},{10,6},{11,9},{1... | collective-permute-start | bytes 196616 | tf_op jit(solution)/shard_map/ppermute | solution.py:45
  68.0 2.9 %collective-permute-start.22 = (f32[256,128]{1,0:T(8,128)S(1)}, f32[256,128]{1,0:T(8,128)S(1)}, u32[]{:S(2)}, u32[]{:S(2)}) collective-permute-start(f32[256,128]{1,0:T(8,128)S(1)} %get-tuple-element.59), channel_id=1, source_target_pairs={{0,1},{1,0},{2,3},{3,2},{4,5},{5,4},{6,7},{7,6},{8,9},{9,8},{10,11... | collective-permute-start | bytes 393224 | tf_op jit(solution)/shard_map/ppermute | solution.py:23
  (10 other events, 71.7 us)

commit v5 on v4

--- a/solution.py
+++ b/solution.py
@@ -31,7 +31,7 @@
 def partner(step, me):
     turn = 1 - 2 * (me % 2)
     row = 2 - 4 * ((me // 2) % 2)
-    return ((-3 * turn, 3 * turn), (row, -turn), (-row, turn))[step]
+    return ((row, turn), (-row, -turn), (-3 * turn, 3 * turn))[step]
 
 
 def offset(step, core):

time: 73.4 us -> 71.7 us (0.977)
  starting transfers between devices: 53.6 us -> 47.3 us
  waiting for transfers between devices: 8.21 us -> 12.2 us
  Pallas kernels: 6.66 us -> 7.47 us
    ppermute x14, waiting for transfers between devices: 3.67 us -> 9.42 us  [dp_swap(): return lax.ppermute(value, 'dp', [(i, i ^ mask) for i in range(count)])]
    ppermute x9, starting transfers between devices: 12.4 us -> 8.72 us  [fan_out(): lax.ppermute(value, BOTH, [(i, j) for i, j in pairs if 0 <= j < 2 * count])]
    ppermute x14, starting transfers between devices: 32.5 us -> 30.1 us  [dp_swap(): return lax.ppermute(value, 'dp', [(i, i ^ mask) for i in range(count)])]
    ppermute x9, waiting for transfers between devices: 1.82 us -> 0.02 us  [fan_out(): lax.ppermute(value, BOTH, [(i, j) for i, j in pairs if 0 <= j < 2 * count])]
    pallas_call x7, Pallas kernels: 6.66 us -> 7.47 us  [call(): pl.pallas_call(kernel, in_specs=[SMEM] * smem + [VMEM] * (len(args) - sme...]
  transfers between devices with their start and end apart: 37 -> 37, of which waited for: 9 -> 8; matrix products, arithmetic and copies ran while one was open for 3% -> 3% of each run, Pallas kernels for 8% -> 10%
where the time goes in v5:
time: 71.7 us; the launch traced here: 70.4 us
  starting transfers between devices  47.3 us (66%)
  waiting for transfers between devices  12.2 us (17%)
  Pallas kernels  7.47 us (10%)
  other arithmetic  2.34 us (3%)
  between operations  0.91 us (1%)
    ppermute x14, starting transfers between devices, dp_swap(): return lax.ppermute(value, 'dp', [(i, i ^ mask) for i in range(count)])  30.1 us
    ppermute x14, waiting for transfers between devices, dp_swap(): return lax.ppermute(value, 'dp', [(i, i ^ mask) for i in range(count)])  9.42 us
    ppermute x9, starting transfers between devices, fan_out(): lax.ppermute(value, BOTH, [(i, j) for i, j in pairs if 0 <= j < 2 * count])  8.72 us
    ppermute x14, starting transfers between devices, core_swap(): return lax.ppermute(value, 'fsdp', [(0, 1), (1, 0)])  8.45 us
    pallas_call x7, Pallas kernels, call(): pl.pallas_call(kernel, in_specs=[SMEM] * smem + [VMEM] * (len(args) - sme...  7.47 us
    ppermute x14, waiting for transfers between devices, core_swap(): return lax.ppermute(value, 'fsdp', [(0, 1), (1, 0)])  2.71 us
  transfers between devices with their start and end apart: 37, of which 8 were waited for; matrix products, arithmetic and copies ran while one was open for 3% of the time, Pallas kernels for 10%

profile of v5, /device:TPU:0, one launch (start us, length us, event | category | flops | bytes accessed | tf_op | source)
XLA Modules:
  0.0 70.4 jit_solution(1395088998019444187)
XLA Ops:
  0.7 3.0 %collective-permute-start = (bf16[16,4096]{1,0:T(8,128)(2,1)}, bf16[16,4096]{1,0:T(8,128)(2,1)S(1)}, u32[]{:S(2)}, u32[]{:S(2)}) collective-permute-start(bf16[16,4096]{1,0:T(8,128)(2,1)} %bitcast.19), channel_id=1, source_target_pairs={{0,2},{2,0},{4,6},{6,4},{8,10},{10,8},{12,14},{14,12},{1,3},{3,1},... | collective-permute-start | bytes 393224 | tf_op jit(solution)/shard_map/ppermute | solution.py:28
  3.7 1.6 %collective-permute-start.1 = (bf16[16,4096]{1,0:T(8,128)(2,1)}, bf16[16,4096]{1,0:T(8,128)(2,1)S(1)}, u32[]{:S(2)}, u32[]{:S(2)}) collective-permute-start(bf16[16,4096]{1,0:T(8,128)(2,1)} %bitcast.20), channel_id=1, source_target_pairs={{0,4},{2,6},{4,0},{6,2},{8,12},{10,14},{12,8},{14,10},{1,5},{3,7},... | collective-permute-start | bytes 393224 | tf_op jit(solution)/shard_map/ppermute | solution.py:28
  5.2 2.6 %collective-permute-start.3 = (bf16[16,4096]{1,0:T(8,128)(2,1)}, bf16[16,4096]{1,0:T(8,128)(2,1)S(1)}, u32[]{:S(2)}, u32[]{:S(2)}) collective-permute-start(bf16[16,4096]{1,0:T(8,128)(2,1)} %bitcast.21), channel_id=1, source_target_pairs={{0,8},{2,10},{4,12},{6,14},{8,0},{10,2},{12,4},{14,6},{1,9},{3,11}... | collective-permute-start | bytes 393224 | tf_op jit(solution)/shard_map/ppermute | solution.py:28
  7.8 0.7 %pad_add_fusion.docs_ref = s32[8]{0:T(128)S(1)} fusion(s32[4]{0:T(128)} %param.13, s32[4]{0:T(128)} %param.12), kind=kLoop, calls=%fused_computation.11 | loop fusion | flops 8 | bytes 64 | tf_op jit(solution)/shard_map/concatenate | solution.py:330
  9.2 0.7 collective-permute-start.7
  9.9 5.2 %collective-permute-start.12 = (bf16[16,4096]{1,0:T(8,128)(2,1)S(1)}, bf16[16,4096]{1,0:T(8,128)(2,1)S(1)}, u32[]{:S(2)}, u32[]{:S(2)}) collective-permute-start(bf16[16,4096]{1,0:T(8,128)(2,1)S(1)} %bitcast.22), channel_id=1, source_target_pairs={{0,12},{2,14},{4,8},{6,10},{8,4},{10,6},{12,0},{14,2},{1,13},{3,15... | collective-permute-start | bytes 393224 | tf_op jit(solution)/shard_map/ppermute | solution.py:28
  15.1 0.8 %collective-permute-start.5 = (bf16[256,128]{1,0:T(8,128)(2,1)S(1)}, bf16[256,128]{1,0:T(8,128)(2,1)S(1)}, u32[]{:S(2)}, u32[]{:S(2)}) collective-permute-start(bf16[256,128]{1,0:T(8,128)(2,1)S(1)} %copy-done.2), channel_id=1, source_target_pairs={{0,4},{1,3},{2,6},{3,1},{4,0},{5,7},{6,2},{7,5},{8,12},{9,11},{10,... | collective-permute-start | bytes 196616 | tf_op jit(solution)/shard_map/ppermute | solution.py:45
  15.9 0.7 collective-permute-start.6
  16.6 5.2 %collective-permute-start.4 = (bf16[16,4096]{1,0:T(8,128)(2,1)S(1)}, bf16[16,4096]{1,0:T(8,128)(2,1)S(1)}, u32[]{:S(2)}, u32[]{:S(2)}) collective-permute-start(bf16[16,4096]{1,0:T(8,128)(2,1)S(1)} %collective-permute-done.3.z2), channel_id=1, source_target_pairs={{0,2},{2,0},{4,6},{6,4},{8,10},{10,8},{12,14},{14,12},{1,3},{3,1},... | collective-permute-start | bytes 393224 | tf_op jit(solution)/shard_map/ppermute | solution.py:28
  22.9 2.6 %collective-permute-done.4.c2 = bf16[16,4096]{1,0:T(8,128)(2,1)S(1)} collective-permute-done((bf16[16,4096]{1,0:T(8,128)(2,1)S(1)}, bf16[16,4096]{1,0:T(8,128)(2,1)S(1)}, u32[]{:S(2)}, u32[]{:S(2)}) %collective-permute-start.4) | collective-permute-done | bytes 131104 | tf_op jit(solution)/shard_map/ppermute | solution.py:28
  25.5 2.0 %shard_map.103 = (bf16[2,7,256,512]{3,2,1,0:T(8,128)(2,1)S(1)}, bf16[1792,128]{1,0:T(8,128)(2,1)S(1)}, f32[256,128]{1,0:T(8,128)S(1)}, f32[3,256,128]{2,1,0:T(8,128)S(1)}, bf16[3,256,128]{2,1,0:T(8,128)(2,1)S(1)}) custom-call(s32[2,8,128]{2,1,0:T(8,128)S(1)} %shard_map.102.info_ref, bf16[2,512,128]{2,1,0:T(8,128)(2,1)S(1)} %bitcast.15, ...), custom_call_target="tpu_custom_call" | custom-call | flops 1073741824 | bytes 4194304 | tf_op jit(solution)/shard_map/pallas_call | solution.py:305
  27.6 0.7 collective-permute-done.13.c3
  28.3 0.8 %shard_map.104 = (f32[256,128]{1,0:T(8,128)S(1)}, bf16[128,4096]{1,0:T(8,128)(2,1)S(1)}) custom-call(bf16[256,4096]{1,0:T(8,128)(2,1)S(1)} %copy-done, bf16[16,4096]{1,0:T(8,128)(2,1)S(1)} %bitcast.23, bf16[16,4096]{1,0:T(8,128)(2,1)S(1)} %collective-permute-done.1.z1, bf16[16,4096]{1,0:T(8,128)(2,1)S(1)} %collective-permute-done.3.z2, ...), custom_call_target="tpu_custom_call" | custom-call | flops 1073741824 | bytes 4194304 | tf_op jit(solution)/shard_map/pallas_call | solution.py:305
  29.2 1.3 %collective-permute-done.14.other_ref = f32[256,128]{1,0:T(8,128)S(1)} collective-permute-done((f32[256,128]{1,0:T(8,128)S(1)}, f32[256,128]{1,0:T(8,128)S(1)}, u32[]{:S(2)}, u32[]{:S(2)}) %collective-permute-start.14) | collective-permute-done | bytes 131104 | tf_op jit(solution)/shard_map/ppermute | solution.py:23
  30.6 1.8 %collective-permute-start.16 = (bf16[2,256,128]{2,1,0:T(8,128)(2,1)S(1)}, bf16[2,256,128]{2,1,0:T(8,128)(2,1)S(1)}, u32[]{:S(2)}, u32[]{:S(2)}) collective-permute-start(bf16[2,256,128]{2,1,0:T(8,128)(2,1)S(1)} %get-tuple-element.47), channel_id=1, source_target_pairs={{0,4},{1,3},{2,6},{3,1},{4,0},{5,7},{6,2},{7,5},{8,12},{9,11},{10,... | collective-permute-start | bytes 393224 | tf_op jit(solution)/shard_map/ppermute | solution.py:45
  32.3 0.7 collective-permute-start.17
  33.0 0.9 %collective-permute-start.18 = (bf16[2,256,128]{2,1,0:T(8,128)(2,1)S(1)}, bf16[2,256,128]{2,1,0:T(8,128)(2,1)S(1)}, u32[]{:S(2)}, u32[]{:S(2)}) collective-permute-start(bf16[2,256,128]{2,1,0:T(8,128)(2,1)S(1)} %get-tuple-element.49), channel_id=1, source_target_pairs={{1,7},{2,8},{5,11},{6,12},{7,1},{8,2},{9,15},{11,5},{12,6},{15,9},... | collective-permute-start | bytes 393224 | tf_op jit(solution)/shard_map/ppermute | solution.py:45
  33.9 4.4 %collective-permute-start.11 = (f32[256,128]{1,0:T(8,128)S(1)}, f32[256,128]{1,0:T(8,128)S(1)}, u32[]{:S(2)}, u32[]{:S(2)}) collective-permute-start(f32[256,128]{1,0:T(8,128)S(1)} %get-tuple-element.43.a_ref), channel_id=1, source_target_pairs={{0,1},{1,0},{2,3},{3,2},{4,5},{5,4},{6,7},{7,6},{8,9},{9,8},{10,11... | collective-permute-start | bytes 393224 | tf_op jit(solution)/shard_map/ppermute | solution.py:23
  38.8 1.5 %collective-permute-start.21 = (bf16[2,256,128]{2,1,0:T(8,128)(2,1)S(1)}, bf16[2,256,128]{2,1,0:T(8,128)(2,1)S(1)}, u32[]{:S(2)}, u32[]{:S(2)}) collective-permute-start(bf16[2,256,128]{2,1,0:T(8,128)(2,1)S(1)} %collective-permute-done.18.r3), channel_id=1, source_target_pairs={{0,1},{1,0},{2,3},{3,2},{4,5},{5,4},{6,7},{7,6},{8,9},{9,8},{10,11... | collective-permute-start | bytes 393224 | tf_op jit(solution)/shard_map/ppermute | solution.py:23
  40.4 1.0 %collective-permute-done.21.s3 = bf16[2,256,128]{2,1,0:T(8,128)(2,1)S(1)} collective-permute-done((bf16[2,256,128]{2,1,0:T(8,128)(2,1)S(1)}, bf16[2,256,128]{2,1,0:T(8,128)(2,1)S(1)}, u32[]{:S(2)}, u32[]{:S(2)}) %collective-permute-start.21) | collective-permute-done | bytes 131104 | tf_op jit(solution)/shard_map/ppermute | solution.py:23
  42.0 5.2 %collective-permute-start.30 = (bf16[16,4096]{1,0:T(8,128)(2,1)S(1)}, bf16[16,4096]{1,0:T(8,128)(2,1)S(1)}, u32[]{:S(2)}, u32[]{:S(2)}) collective-permute-start(bf16[16,4096]{1,0:T(8,128)(2,1)S(1)} %get-tuple-element.64), channel_id=1, source_target_pairs={{0,2},{2,0},{4,6},{6,4},{8,10},{10,8},{12,14},{14,12},{1,3},{3,1},... | collective-permute-start | bytes 393224 | tf_op jit(solution)/shard_map/ppermute | solution.py:28
  47.3 1.9 %collective-permute-start.34 = (bf16[16,4096]{1,0:T(8,128)(2,1)S(1)}, bf16[16,4096]{1,0:T(8,128)(2,1)S(1)}, u32[]{:S(2)}, u32[]{:S(2)}) collective-permute-start(bf16[16,4096]{1,0:T(8,128)(2,1)S(1)} %get-tuple-element.68), channel_id=1, source_target_pairs={{0,2},{2,0},{4,6},{6,4},{8,10},{10,8},{12,14},{14,12},{1,3},{3,1},... | collective-permute-start | bytes 393224 | tf_op jit(solution)/shard_map/ppermute | solution.py:28
  49.3 1.7 %shard_map.107 = (f32[2,128,512]{2,1,0:T(8,128)S(1)}, f32[256,128]{1,0:T(8,128)S(1)}, f32[3,256,128]{2,1,0:T(8,128)S(1)}, bf16[3,256,128]{2,1,0:T(8,128)(2,1)S(1)}) custom-call(s32[2,8,128]{2,1,0:T(8,128)S(1)} %shard_map.102.info_ref, bf16[2,512,128]{2,1,0:T(8,128)(2,1)S(1)} %bitcast.16, bf16[2,512,128]{2,1,0:T(8,128)(2,1)S(1)} %bitcast.18, ...), custom_call_target="tpu_custom_call" | custom-call | flops 1073741824 | bytes 4194304 | tf_op jit(solution)/shard_map/pallas_call | solution.py:305
  51.5 1.7 %collective-permute-start.31 = (bf16[16,4096]{1,0:T(8,128)(2,1)S(1)}, bf16[16,4096]{1,0:T(8,128)(2,1)S(1)}, u32[]{:S(2)}, u32[]{:S(2)}) collective-permute-start(bf16[16,4096]{1,0:T(8,128)(2,1)S(1)} %add_convert_fusion.2), channel_id=1, source_target_pairs={{0,12},{2,14},{4,8},{6,10},{8,4},{10,6},{12,0},{14,2},{1,13},{3,15... | collective-permute-start | bytes 393224 | tf_op jit(solution)/shard_map/ppermute | solution.py:28
  53.2 1.1 %collective-permute-done.32 = bf16[16,4096]{1,0:T(8,128)(2,1)S(1)} collective-permute-done((bf16[16,4096]{1,0:T(8,128)(2,1)S(1)}, bf16[16,4096]{1,0:T(8,128)(2,1)S(1)}, u32[]{:S(2)}, u32[]{:S(2)}) %collective-permute-start.32) | collective-permute-done | bytes 131104 | tf_op jit(solution)/shard_map/ppermute | solution.py:28
  54.3 3.1 %collective-permute-start.33 = (bf16[16,4096]{1,0:T(8,128)(2,1)S(1)}, bf16[16,4096]{1,0:T(8,128)(2,1)S(1)}, u32[]{:S(2)}, u32[]{:S(2)}) collective-permute-start(bf16[16,4096]{1,0:T(8,128)(2,1)S(1)} %add_convert_fusion.1), channel_id=1, source_target_pairs={{0,8},{2,10},{4,12},{6,14},{8,0},{10,2},{12,4},{14,6},{1,9},{3,11}... | collective-permute-start | bytes 393224 | tf_op jit(solution)/shard_map/ppermute | solution.py:28
  57.7 1.9 %collective-permute-start.24 = (bf16[256,128]{1,0:T(8,128)(2,1)S(1)}, bf16[256,128]{1,0:T(8,128)(2,1)S(1)}, u32[]{:S(2)}, u32[]{:S(2)}) collective-permute-start(bf16[256,128]{1,0:T(8,128)(2,1)S(1)} %get-tuple-element.70), channel_id=1, source_target_pairs={{0,4},{1,3},{2,6},{3,1},{4,0},{5,7},{6,2},{7,5},{8,12},{9,11},{10,... | collective-permute-start | bytes 196616 | tf_op jit(solution)/shard_map/ppermute | solution.py:45
  60.3 0.7 collective-permute-start.28
  61.0 1.7 %shard_map.108 = (bf16[256,4096]{1,0:T(8,128)(2,1)}, bf16[256,512]{1,0:T(8,128)(2,1)}) custom-call(bf16[256,128]{1,0:T(8,128)(2,1)S(1)} %get-tuple-element.50.grad_ref, bf16[128,4096]{1,0:T(8,128)(2,1)S(1)} %get-tuple-element.51.weight_ref, f32[2,128,512]{2,1,0:T(8,128)S(1)} %get-tuple-element.56.query_ref), custom_call_target="tpu_custom_call" | custom-call | flops 1073741824 | bytes 4194304 | tf_op jit(solution)/shard_map/pallas_call | solution.py:305
  62.7 4.7 %collective-permute-done.33 = bf16[16,4096]{1,0:T(8,128)(2,1)S(1)} collective-permute-done((bf16[16,4096]{1,0:T(8,128)(2,1)S(1)}, bf16[16,4096]{1,0:T(8,128)(2,1)S(1)}, u32[]{:S(2)}, u32[]{:S(2)}) %collective-permute-start.33) | collective-permute-done | bytes 131104 | tf_op jit(solution)/shard_map/ppermute | solution.py:28
  68.5 0.8 %add_bitcast_fusion = f32[4096,16]{0,1:T(8,128)} fusion(bf16[16,4096]{1,0:T(8,128)(2,1)S(1)} %collective-permute-done.36, bf16[16,4096]{1,0:T(8,128)(2,1)S(1)} %collective-permute-done.35, bf16[16,4096]{1,0:T(8,128)(2,1)S(1)} %collective-permute-done.33, f32[16,4096]{1,0:T(8,128)S(1)} %get-tuple-element.62, bf16[16,4096]{1,0:T(8,128)(2,1)S(1)} %collective-permute-done.31), kind=kLoop, calls=%fused_computation | loop fusion | flops 524288 | bytes 1048576 | tf_op jit(solution)/shard_map/transpose | solution.py:401
  69.7 0.7 add_convert_fusion.3
  (70 shorter events, 6.2 us)
Async XLA Ops:
  0.7 7.9 %collective-permute-start = (bf16[16,4096]{1,0:T(8,128)(2,1)}, bf16[16,4096]{1,0:T(8,128)(2,1)S(1)}, u32[]{:S(2)}, u32[]{:S(2)}) collective-permute-start(bf16[16,4096]{1,0:T(8,128)(2,1)} %bitcast.19), channel_id=1, source_target_pairs={{0,2},{2,0},{4,6},{6,4},{8,10},{10,8},{12,14},{14,12},{1,3},{3,1},... | collective-permute-start | bytes 393224 | tf_op jit(solution)/shard_map/ppermute | solution.py:28
  3.7 11.4 %collective-permute-start.1 = (bf16[16,4096]{1,0:T(8,128)(2,1)}, bf16[16,4096]{1,0:T(8,128)(2,1)S(1)}, u32[]{:S(2)}, u32[]{:S(2)}) collective-permute-start(bf16[16,4096]{1,0:T(8,128)(2,1)} %bitcast.20), channel_id=1, source_target_pairs={{0,4},{2,6},{4,0},{6,2},{8,12},{10,14},{12,8},{14,10},{1,5},{3,7},... | collective-permute-start | bytes 393224 | tf_op jit(solution)/shard_map/ppermute | solution.py:28
  5.2 10.7 %collective-permute-start.3 = (bf16[16,4096]{1,0:T(8,128)(2,1)}, bf16[16,4096]{1,0:T(8,128)(2,1)S(1)}, u32[]{:S(2)}, u32[]{:S(2)}) collective-permute-start(bf16[16,4096]{1,0:T(8,128)(2,1)} %bitcast.21), channel_id=1, source_target_pairs={{0,8},{2,10},{4,12},{6,14},{8,0},{10,2},{12,4},{14,6},{1,9},{3,11}... | collective-permute-start | bytes 393224 | tf_op jit(solution)/shard_map/ppermute | solution.py:28
  9.2 7.4 %collective-permute-start.7 = (bf16[256,128]{1,0:T(8,128)(2,1)S(1)}, bf16[256,128]{1,0:T(8,128)(2,1)S(1)}, u32[]{:S(2)}, u32[]{:S(2)}) collective-permute-start(bf16[256,128]{1,0:T(8,128)(2,1)S(1)} %copy-done.2), channel_id=1, source_target_pairs={{1,7},{2,8},{5,11},{6,12},{7,1},{8,2},{9,15},{11,5},{12,6},{15,9},... | collective-permute-start | bytes 196616 | tf_op jit(solution)/shard_map/ppermute | solution.py:45
  9.9 12.5 %collective-permute-start.12 = (bf16[16,4096]{1,0:T(8,128)(2,1)S(1)}, bf16[16,4096]{1,0:T(8,128)(2,1)S(1)}, u32[]{:S(2)}, u32[]{:S(2)}) collective-permute-start(bf16[16,4096]{1,0:T(8,128)(2,1)S(1)} %bitcast.22), channel_id=1, source_target_pairs={{0,12},{2,14},{4,8},{6,10},{8,4},{10,6},{12,0},{14,2},{1,13},{3,15... | collective-permute-start | bytes 393224 | tf_op jit(solution)/shard_map/ppermute | solution.py:28
  15.1 7.4 %collective-permute-start.2 = (bf16[16,4096]{1,0:T(8,128)(2,1)S(1)}, bf16[16,4096]{1,0:T(8,128)(2,1)S(1)}, u32[]{:S(2)}, u32[]{:S(2)}) collective-permute-start(bf16[16,4096]{1,0:T(8,128)(2,1)S(1)} %collective-permute-done.1.z1), channel_id=1, source_target_pairs={{0,2},{2,0},{4,6},{6,4},{8,10},{10,8},{12,14},{14,12},{1,3},{3,1},... | collective-permute-start | bytes 393224 | tf_op jit(solution)/shard_map/ppermute | solution.py:28
  15.1 6.8 %collective-permute-start.5 = (bf16[256,128]{1,0:T(8,128)(2,1)S(1)}, bf16[256,128]{1,0:T(8,128)(2,1)S(1)}, u32[]{:S(2)}, u32[]{:S(2)}) collective-permute-start(bf16[256,128]{1,0:T(8,128)(2,1)S(1)} %copy-done.2), channel_id=1, source_target_pairs={{0,4},{1,3},{2,6},{3,1},{4,0},{5,7},{6,2},{7,5},{8,12},{9,11},{10,... | collective-permute-start | bytes 196616 | tf_op jit(solution)/shard_map/ppermute | solution.py:45
  15.9 5.9 %collective-permute-start.6 = (bf16[256,128]{1,0:T(8,128)(2,1)S(1)}, bf16[256,128]{1,0:T(8,128)(2,1)S(1)}, u32[]{:S(2)}, u32[]{:S(2)}) collective-permute-start(bf16[256,128]{1,0:T(8,128)(2,1)S(1)} %copy-done.2), channel_id=1, source_target_pairs={{3,5},{4,8},{5,3},{6,10},{7,9},{8,4},{9,7},{10,6},{11,13},{13,11},... | collective-permute-start | bytes 196616 | tf_op jit(solution)/shard_map/ppermute | solution.py:45
  16.6 8.9 %collective-permute-start.4 = (bf16[16,4096]{1,0:T(8,128)(2,1)S(1)}, bf16[16,4096]{1,0:T(8,128)(2,1)S(1)}, u32[]{:S(2)}, u32[]{:S(2)}) collective-permute-start(bf16[16,4096]{1,0:T(8,128)(2,1)S(1)} %collective-permute-done.3.z2), channel_id=1, source_target_pairs={{0,2},{2,0},{4,6},{6,4},{8,10},{10,8},{12,14},{14,12},{1,3},{3,1},... | collective-permute-start | bytes 393224 | tf_op jit(solution)/shard_map/ppermute | solution.py:28
  21.9 3.6 %collective-permute-start.10 = (bf16[256,128]{1,0:T(8,128)(2,1)S(1)}, bf16[256,128]{1,0:T(8,128)(2,1)S(1)}, u32[]{:S(2)}, u32[]{:S(2)}) collective-permute-start(bf16[256,128]{1,0:T(8,128)(2,1)S(1)} %collective-permute-done.7.r3), channel_id=1, source_target_pairs={{0,1},{1,0},{2,3},{3,2},{4,5},{5,4},{6,7},{7,6},{8,9},{9,8},{10,11... | collective-permute-start | bytes 196616 | tf_op jit(solution)/shard_map/ppermute | solution.py:23
  21.9 3.6 %collective-permute-start.8 = (bf16[256,128]{1,0:T(8,128)(2,1)S(1)}, bf16[256,128]{1,0:T(8,128)(2,1)S(1)}, u32[]{:S(2)}, u32[]{:S(2)}) collective-permute-start(bf16[256,128]{1,0:T(8,128)(2,1)S(1)} %collective-permute-done.5.r1), channel_id=1, source_target_pairs={{0,1},{1,0},{2,3},{3,2},{4,5},{5,4},{6,7},{7,6},{8,9},{9,8},{10,11... | collective-permute-start | bytes 196616 | tf_op jit(solution)/shard_map/ppermute | solution.py:23
  22.4 3.1 %collective-permute-start.9 = (bf16[256,128]{1,0:T(8,128)(2,1)S(1)}, bf16[256,128]{1,0:T(8,128)(2,1)S(1)}, u32[]{:S(2)}, u32[]{:S(2)}) collective-permute-start(bf16[256,128]{1,0:T(8,128)(2,1)S(1)} %collective-permute-done.6.r2), channel_id=1, source_target_pairs={{0,1},{1,0},{2,3},{3,2},{4,5},{5,4},{6,7},{7,6},{8,9},{9,8},{10,11... | collective-permute-start | bytes 196616 | tf_op jit(solution)/shard_map/ppermute | solution.py:23
  22.5 5.8 %collective-permute-start.13 = (bf16[16,4096]{1,0:T(8,128)(2,1)S(1)}, bf16[16,4096]{1,0:T(8,128)(2,1)S(1)}, u32[]{:S(2)}, u32[]{:S(2)}) collective-permute-start(bf16[16,4096]{1,0:T(8,128)(2,1)S(1)} %collective-permute-done.12.z3), channel_id=1, source_target_pairs={{0,2},{2,0},{4,6},{6,4},{8,10},{10,8},{12,14},{14,12},{1,3},{3,1},... | collective-permute-start | bytes 393224 | tf_op jit(solution)/shard_map/ppermute | solution.py:28
  27.6 2.9 %collective-permute-start.15 = (bf16[3,256,128]{2,1,0:T(8,128)(2,1)S(1)}, bf16[3,256,128]{2,1,0:T(8,128)(2,1)S(1)}, u32[]{:S(2)}, u32[]{:S(2)}) collective-permute-start(bf16[3,256,128]{2,1,0:T(8,128)(2,1)S(1)} %get-tuple-element.46), channel_id=1, source_target_pairs={{0,1},{1,0},{2,3},{3,2},{4,5},{5,4},{6,7},{7,6},{8,9},{9,8},{10,11... | collective-permute-start | bytes 589832 | tf_op jit(solution)/shard_map/ppermute | solution.py:23
  30.6 7.8 %collective-permute-start.16 = (bf16[2,256,128]{2,1,0:T(8,128)(2,1)S(1)}, bf16[2,256,128]{2,1,0:T(8,128)(2,1)S(1)}, u32[]{:S(2)}, u32[]{:S(2)}) collective-permute-start(bf16[2,256,128]{2,1,0:T(8,128)(2,1)S(1)} %get-tuple-element.47), channel_id=1, source_target_pairs={{0,4},{1,3},{2,6},{3,1},{4,0},{5,7},{6,2},{7,5},{8,12},{9,11},{10,... | collective-permute-start | bytes 393224 | tf_op jit(solution)/shard_map/ppermute | solution.py:45
  32.3 6.1 %collective-permute-start.17 = (bf16[2,256,128]{2,1,0:T(8,128)(2,1)S(1)}, bf16[2,256,128]{2,1,0:T(8,128)(2,1)S(1)}, u32[]{:S(2)}, u32[]{:S(2)}) collective-permute-start(bf16[2,256,128]{2,1,0:T(8,128)(2,1)S(1)} %get-tuple-element.48), channel_id=1, source_target_pairs={{3,5},{4,8},{5,3},{6,10},{7,9},{8,4},{9,7},{10,6},{11,13},{13,11},... | collective-permute-start | bytes 393224 | tf_op jit(solution)/shard_map/ppermute | solution.py:45
  33.0 5.9 %collective-permute-start.18 = (bf16[2,256,128]{2,1,0:T(8,128)(2,1)S(1)}, bf16[2,256,128]{2,1,0:T(8,128)(2,1)S(1)}, u32[]{:S(2)}, u32[]{:S(2)}) collective-permute-start(bf16[2,256,128]{2,1,0:T(8,128)(2,1)S(1)} %get-tuple-element.49), channel_id=1, source_target_pairs={{1,7},{2,8},{5,11},{6,12},{7,1},{8,2},{9,15},{11,5},{12,6},{15,9},... | collective-permute-start | bytes 393224 | tf_op jit(solution)/shard_map/ppermute | solution.py:45
  33.9 6.5 %collective-permute-start.11 = (f32[256,128]{1,0:T(8,128)S(1)}, f32[256,128]{1,0:T(8,128)S(1)}, u32[]{:S(2)}, u32[]{:S(2)}) collective-permute-start(f32[256,128]{1,0:T(8,128)S(1)} %get-tuple-element.43.a_ref), channel_id=1, source_target_pairs={{0,1},{1,0},{2,3},{3,2},{4,5},{5,4},{6,7},{7,6},{8,9},{9,8},{10,11... | collective-permute-start | bytes 393224 | tf_op jit(solution)/shard_map/ppermute | solution.py:23
  38.3 2.1 %collective-permute-start.19 = (bf16[2,256,128]{2,1,0:T(8,128)(2,1)S(1)}, bf16[2,256,128]{2,1,0:T(8,128)(2,1)S(1)}, u32[]{:S(2)}, u32[]{:S(2)}) collective-permute-start(bf16[2,256,128]{2,1,0:T(8,128)(2,1)S(1)} %collective-permute-done.16.r1), channel_id=1, source_target_pairs={{0,1},{1,0},{2,3},{3,2},{4,5},{5,4},{6,7},{7,6},{8,9},{9,8},{10,11... | collective-permute-start | bytes 393224 | tf_op jit(solution)/shard_map/ppermute | solution.py:23
  38.4 2.0 %collective-permute-start.20 = (bf16[2,256,128]{2,1,0:T(8,128)(2,1)S(1)}, bf16[2,256,128]{2,1,0:T(8,128)(2,1)S(1)}, u32[]{:S(2)}, u32[]{:S(2)}) collective-permute-start(bf16[2,256,128]{2,1,0:T(8,128)(2,1)S(1)} %collective-permute-done.17.r2), channel_id=1, source_target_pairs={{0,1},{1,0},{2,3},{3,2},{4,5},{5,4},{6,7},{7,6},{8,9},{9,8},{10,11... | collective-permute-start | bytes 393224 | tf_op jit(solution)/shard_map/ppermute | solution.py:23
  38.8 2.5 %collective-permute-start.21 = (bf16[2,256,128]{2,1,0:T(8,128)(2,1)S(1)}, bf16[2,256,128]{2,1,0:T(8,128)(2,1)S(1)}, u32[]{:S(2)}, u32[]{:S(2)}) collective-permute-start(bf16[2,256,128]{2,1,0:T(8,128)(2,1)S(1)} %collective-permute-done.18.r3), channel_id=1, source_target_pairs={{0,1},{1,0},{2,3},{3,2},{4,5},{5,4},{6,7},{7,6},{8,9},{9,8},{10,11... | collective-permute-start | bytes 393224 | tf_op jit(solution)/shard_map/ppermute | solution.py:23
  42.0 9.5 %collective-permute-start.30 = (bf16[16,4096]{1,0:T(8,128)(2,1)S(1)}, bf16[16,4096]{1,0:T(8,128)(2,1)S(1)}, u32[]{:S(2)}, u32[]{:S(2)}) collective-permute-start(bf16[16,4096]{1,0:T(8,128)(2,1)S(1)} %get-tuple-element.64), channel_id=1, source_target_pairs={{0,2},{2,0},{4,6},{6,4},{8,10},{10,8},{12,14},{14,12},{1,3},{3,1},... | collective-permute-start | bytes 393224 | tf_op jit(solution)/shard_map/ppermute | solution.py:28
  47.2 7.1 %collective-permute-start.32 = (bf16[16,4096]{1,0:T(8,128)(2,1)S(1)}, bf16[16,4096]{1,0:T(8,128)(2,1)S(1)}, u32[]{:S(2)}, u32[]{:S(2)}) collective-permute-start(bf16[16,4096]{1,0:T(8,128)(2,1)S(1)} %get-tuple-element.66), channel_id=1, source_target_pairs={{0,2},{2,0},{4,6},{6,4},{8,10},{10,8},{12,14},{14,12},{1,3},{3,1},... | collective-permute-start | bytes 393224 | tf_op jit(solution)/shard_map/ppermute | solution.py:28
  47.3 10.1 %collective-permute-start.34 = (bf16[16,4096]{1,0:T(8,128)(2,1)S(1)}, bf16[16,4096]{1,0:T(8,128)(2,1)S(1)}, u32[]{:S(2)}, u32[]{:S(2)}) collective-permute-start(bf16[16,4096]{1,0:T(8,128)(2,1)S(1)} %get-tuple-element.68), channel_id=1, source_target_pairs={{0,2},{2,0},{4,6},{6,4},{8,10},{10,8},{12,14},{14,12},{1,3},{3,1},... | collective-permute-start | bytes 393224 | tf_op jit(solution)/shard_map/ppermute | solution.py:28
  49.2 10.4 %collective-permute-start.36 = (bf16[16,4096]{1,0:T(8,128)(2,1)S(1)}, bf16[16,4096]{1,0:T(8,128)(2,1)S(1)}, u32[]{:S(2)}, u32[]{:S(2)}) collective-permute-start(bf16[16,4096]{1,0:T(8,128)(2,1)S(1)} %get-tuple-element.69), channel_id=1, source_target_pairs={{0,2},{2,0},{4,6},{6,4},{8,10},{10,8},{12,14},{14,12},{1,3},{3,1},... | collective-permute-start | bytes 393224 | tf_op jit(solution)/shard_map/ppermute | solution.py:28
  51.0 6.6 %collective-permute-start.23 = (bf16[3,256,128]{2,1,0:T(8,128)(2,1)S(1)}, bf16[3,256,128]{2,1,0:T(8,128)(2,1)S(1)}, u32[]{:S(2)}, u32[]{:S(2)}) collective-permute-start(bf16[3,256,128]{2,1,0:T(8,128)(2,1)S(1)} %get-tuple-element.61), channel_id=1, source_target_pairs={{0,1},{1,0},{2,3},{3,2},{4,5},{5,4},{6,7},{7,6},{8,9},{9,8},{10,11... | collective-permute-start | bytes 589832 | tf_op jit(solution)/shard_map/ppermute | solution.py:23
  51.5 8.8 %collective-permute-start.31 = (bf16[16,4096]{1,0:T(8,128)(2,1)S(1)}, bf16[16,4096]{1,0:T(8,128)(2,1)S(1)}, u32[]{:S(2)}, u32[]{:S(2)}) collective-permute-start(bf16[16,4096]{1,0:T(8,128)(2,1)S(1)} %add_convert_fusion.2), channel_id=1, source_target_pairs={{0,12},{2,14},{4,8},{6,10},{8,4},{10,6},{12,0},{14,2},{1,13},{3,15... | collective-permute-start | bytes 393224 | tf_op jit(solution)/shard_map/ppermute | solution.py:28
  54.3 13.0 %collective-permute-start.33 = (bf16[16,4096]{1,0:T(8,128)(2,1)S(1)}, bf16[16,4096]{1,0:T(8,128)(2,1)S(1)}, u32[]{:S(2)}, u32[]{:S(2)}) collective-permute-start(bf16[16,4096]{1,0:T(8,128)(2,1)S(1)} %add_convert_fusion.1), channel_id=1, source_target_pairs={{0,8},{2,10},{4,12},{6,14},{8,0},{10,2},{12,4},{14,6},{1,9},{3,11}... | collective-permute-start | bytes 393224 | tf_op jit(solution)/shard_map/ppermute | solution.py:28
  57.4 11.1 %collective-permute-start.35 = (bf16[16,4096]{1,0:T(8,128)(2,1)S(1)}, bf16[16,4096]{1,0:T(8,128)(2,1)S(1)}, u32[]{:S(2)}, u32[]{:S(2)}) collective-permute-start(bf16[16,4096]{1,0:T(8,128)(2,1)S(1)} %add_convert_fusion), channel_id=1, source_target_pairs={{0,4},{2,6},{4,0},{6,2},{8,12},{10,14},{12,8},{14,10},{1,5},{3,7},... | collective-permute-start | bytes 393224 | tf_op jit(solution)/shard_map/ppermute | solution.py:28
  57.7 10.2 %collective-permute-start.24 = (bf16[256,128]{1,0:T(8,128)(2,1)S(1)}, bf16[256,128]{1,0:T(8,128)(2,1)S(1)}, u32[]{:S(2)}, u32[]{:S(2)}) collective-permute-start(bf16[256,128]{1,0:T(8,128)(2,1)S(1)} %get-tuple-element.70), channel_id=1, source_target_pairs={{0,4},{1,3},{2,6},{3,1},{4,0},{5,7},{6,2},{7,5},{8,12},{9,11},{10,... | collective-permute-start | bytes 196616 | tf_op jit(solution)/shard_map/ppermute | solution.py:45
  59.6 8.4 %collective-permute-start.26 = (bf16[256,128]{1,0:T(8,128)(2,1)S(1)}, bf16[256,128]{1,0:T(8,128)(2,1)S(1)}, u32[]{:S(2)}, u32[]{:S(2)}) collective-permute-start(bf16[256,128]{1,0:T(8,128)(2,1)S(1)} %get-tuple-element.72), channel_id=1, source_target_pairs={{3,5},{4,8},{5,3},{6,10},{7,9},{8,4},{9,7},{10,6},{11,13},{13,11},... | collective-permute-start | bytes 196616 | tf_op jit(solution)/shard_map/ppermute | solution.py:45
  60.3 8.1 %collective-permute-start.28 = (bf16[256,128]{1,0:T(8,128)(2,1)S(1)}, bf16[256,128]{1,0:T(8,128)(2,1)S(1)}, u32[]{:S(2)}, u32[]{:S(2)}) collective-permute-start(bf16[256,128]{1,0:T(8,128)(2,1)S(1)} %get-tuple-element.71), channel_id=1, source_target_pairs={{1,7},{2,8},{5,11},{6,12},{7,1},{8,2},{9,15},{11,5},{12,6},{15,9},... | collective-permute-start | bytes 196616 | tf_op jit(solution)/shard_map/ppermute | solution.py:45
  (10 other events, 66.7 us)

commit v6 on v5

--- a/solution.py
+++ b/solution.py
@@ -31,7 +31,7 @@
 def partner(step, me):
     turn = 1 - 2 * (me % 2)
     row = 2 - 4 * ((me // 2) % 2)
-    return ((row, turn), (-row, -turn), (-3 * turn, 3 * turn))[step]
+    return ((row, turn), (-3 * turn, -turn), (-row, 3 * turn))[step]
 
 
 def offset(step, core):

time: 71.7 us -> 69.8 us (0.974); the launches traced: 70.4 us -> 69.7 us
  starting transfers between devices: 47.3 us -> 51.5 us
  waiting for transfers between devices: 12.2 us -> 8.01 us
  Pallas kernels: 7.47 us -> 6.67 us
    ppermute x14, waiting for transfers between devices: 9.42 us -> 5.27 us  [dp_swap(): return lax.ppermute(value, 'dp', [(i, i ^ mask) for i in range(count)])]
    ppermute x14, starting transfers between devices: 30.1 us -> 33.7 us  [dp_swap(): return lax.ppermute(value, 'dp', [(i, i ^ mask) for i in range(count)])]
    ppermute x14, starting transfers between devices: 8.45 us -> 11.6 us  [core_swap(): return lax.ppermute(value, 'fsdp', [(0, 1), (1, 0)])]
    ppermute x9, starting transfers between devices: 8.72 us -> 6.17 us  [fan_out(): lax.ppermute(value, BOTH, [(i, j) for i, j in pairs if 0 <= j < 2 * count])]
    pallas_call x7, Pallas kernels: 7.47 us -> 6.67 us  [call(): pl.pallas_call(kernel, in_specs=[SMEM] * smem + [VMEM] * (len(args) - sme...]
  transfers between devices with their start and end apart: 37 -> 37, of which waited for: 8 -> 6; matrix products, arithmetic and copies ran while one was open for 3% -> 3% of each run, Pallas kernels for 10% -> 9%
where the time goes in v6:
time: 69.8 us; the launch traced here: 69.7 us
  starting transfers between devices  51.5 us (74%)
  waiting for transfers between devices  8.01 us (11%)
  Pallas kernels  6.67 us (10%)
  other arithmetic  2.34 us (3%)
  between operations  0.94 us (1%)
    ppermute x14, starting transfers between devices, dp_swap(): return lax.ppermute(value, 'dp', [(i, i ^ mask) for i in range(count)])  33.7 us
    ppermute x14, starting transfers between devices, core_swap(): return lax.ppermute(value, 'fsdp', [(0, 1), (1, 0)])  11.6 us
    pallas_call x7, Pallas kernels, call(): pl.pallas_call(kernel, in_specs=[SMEM] * smem + [VMEM] * (len(args) - sme...  6.67 us
    ppermute x9, starting transfers between devices, fan_out(): lax.ppermute(value, BOTH, [(i, j) for i, j in pairs if 0 <= j < 2 * count])  6.17 us
    ppermute x14, waiting for transfers between devices, dp_swap(): return lax.ppermute(value, 'dp', [(i, i ^ mask) for i in range(count)])  5.27 us
    ppermute x14, waiting for transfers between devices, core_swap(): return lax.ppermute(value, 'fsdp', [(0, 1), (1, 0)])  2.71 us
  transfers between devices with their start and end apart: 37, of which 6 were waited for; matrix products, arithmetic and copies ran while one was open for 3% of the time, Pallas kernels for 9%

profile of v6, /device:TPU:0, one launch (start us, length us, event | category | flops | bytes accessed | tf_op | source)
XLA Modules:
  0.0 69.7 jit_solution(980672241779237392)
XLA Ops:
  0.7 3.0 %collective-permute-start = (bf16[16,4096]{1,0:T(8,128)(2,1)}, bf16[16,4096]{1,0:T(8,128)(2,1)S(1)}, u32[]{:S(2)}, u32[]{:S(2)}) collective-permute-start(bf16[16,4096]{1,0:T(8,128)(2,1)} %bitcast.19), channel_id=1, source_target_pairs={{0,2},{2,0},{4,6},{6,4},{8,10},{10,8},{12,14},{14,12},{1,3},{3,1},... | collective-permute-start | bytes 393224 | tf_op jit(solution)/shard_map/ppermute | solution.py:28
  3.7 1.6 %collective-permute-start.1 = (bf16[16,4096]{1,0:T(8,128)(2,1)}, bf16[16,4096]{1,0:T(8,128)(2,1)S(1)}, u32[]{:S(2)}, u32[]{:S(2)}) collective-permute-start(bf16[16,4096]{1,0:T(8,128)(2,1)} %bitcast.20), channel_id=1, source_target_pairs={{0,4},{2,6},{4,0},{6,2},{8,12},{10,14},{12,8},{14,10},{1,5},{3,7},... | collective-permute-start | bytes 393224 | tf_op jit(solution)/shard_map/ppermute | solution.py:28
  5.2 2.6 %collective-permute-start.3 = (bf16[16,4096]{1,0:T(8,128)(2,1)}, bf16[16,4096]{1,0:T(8,128)(2,1)S(1)}, u32[]{:S(2)}, u32[]{:S(2)}) collective-permute-start(bf16[16,4096]{1,0:T(8,128)(2,1)} %bitcast.21), channel_id=1, source_target_pairs={{0,8},{2,10},{4,12},{6,14},{8,0},{10,2},{12,4},{14,6},{1,9},{3,11}... | collective-permute-start | bytes 393224 | tf_op jit(solution)/shard_map/ppermute | solution.py:28
  7.8 0.7 %pad_add_fusion.docs_ref = s32[8]{0:T(128)S(1)} fusion(s32[4]{0:T(128)} %param.13, s32[4]{0:T(128)} %param.12), kind=kLoop, calls=%fused_computation.11 | loop fusion | flops 8 | bytes 64 | tf_op jit(solution)/shard_map/concatenate | solution.py:330
  9.2 0.7 collective-permute-start.7
  9.9 2.7 %collective-permute-start.12 = (bf16[16,4096]{1,0:T(8,128)(2,1)S(1)}, bf16[16,4096]{1,0:T(8,128)(2,1)S(1)}, u32[]{:S(2)}, u32[]{:S(2)}) collective-permute-start(bf16[16,4096]{1,0:T(8,128)(2,1)S(1)} %bitcast.22), channel_id=1, source_target_pairs={{0,12},{2,14},{4,8},{6,10},{8,4},{10,6},{12,0},{14,2},{1,13},{3,15... | collective-permute-start | bytes 393224 | tf_op jit(solution)/shard_map/ppermute | solution.py:28
  12.6 1.5 %collective-permute-start.2 = (bf16[16,4096]{1,0:T(8,128)(2,1)S(1)}, bf16[16,4096]{1,0:T(8,128)(2,1)S(1)}, u32[]{:S(2)}, u32[]{:S(2)}) collective-permute-start(bf16[16,4096]{1,0:T(8,128)(2,1)S(1)} %collective-permute-done.1.z1), channel_id=1, source_target_pairs={{0,2},{2,0},{4,6},{6,4},{8,10},{10,8},{12,14},{14,12},{1,3},{3,1},... | collective-permute-start | bytes 393224 | tf_op jit(solution)/shard_map/ppermute | solution.py:28
  14.1 1.2 %collective-permute-start.5 = (bf16[256,128]{1,0:T(8,128)(2,1)S(1)}, bf16[256,128]{1,0:T(8,128)(2,1)S(1)}, u32[]{:S(2)}, u32[]{:S(2)}) collective-permute-start(bf16[256,128]{1,0:T(8,128)(2,1)S(1)} %copy-done.2), channel_id=1, source_target_pairs={{0,4},{1,3},{2,6},{3,1},{4,0},{5,7},{6,2},{7,5},{8,12},{9,11},{10,... | collective-permute-start | bytes 196616 | tf_op jit(solution)/shard_map/ppermute | solution.py:45
  16.0 3.8 %collective-permute-start.4 = (bf16[16,4096]{1,0:T(8,128)(2,1)S(1)}, bf16[16,4096]{1,0:T(8,128)(2,1)S(1)}, u32[]{:S(2)}, u32[]{:S(2)}) collective-permute-start(bf16[16,4096]{1,0:T(8,128)(2,1)S(1)} %collective-permute-done.3.z2), channel_id=1, source_target_pairs={{0,2},{2,0},{4,6},{6,4},{8,10},{10,8},{12,14},{14,12},{1,3},{3,1},... | collective-permute-start | bytes 393224 | tf_op jit(solution)/shard_map/ppermute | solution.py:28
  20.4 4.8 %collective-permute-start.13 = (bf16[16,4096]{1,0:T(8,128)(2,1)S(1)}, bf16[16,4096]{1,0:T(8,128)(2,1)S(1)}, u32[]{:S(2)}, u32[]{:S(2)}) collective-permute-start(bf16[16,4096]{1,0:T(8,128)(2,1)S(1)} %collective-permute-done.12.z3), channel_id=1, source_target_pairs={{0,2},{2,0},{4,6},{6,4},{8,10},{10,8},{12,14},{14,12},{1,3},{3,1},... | collective-permute-start | bytes 393224 | tf_op jit(solution)/shard_map/ppermute | solution.py:28
  25.5 1.5 %shard_map.103 = (bf16[2,7,256,512]{3,2,1,0:T(8,128)(2,1)S(1)}, bf16[1792,128]{1,0:T(8,128)(2,1)S(1)}, f32[256,128]{1,0:T(8,128)S(1)}, f32[3,256,128]{2,1,0:T(8,128)S(1)}, bf16[3,256,128]{2,1,0:T(8,128)(2,1)S(1)}) custom-call(s32[2,8,128]{2,1,0:T(8,128)S(1)} %shard_map.102.info_ref, bf16[2,512,128]{2,1,0:T(8,128)(2,1)S(1)} %bitcast.15, ...), custom_call_target="tpu_custom_call" | custom-call | flops 1073741824 | bytes 4194304 | tf_op jit(solution)/shard_map/pallas_call | solution.py:305
  27.1 1.8 %collective-permute-done.13.c3 = bf16[16,4096]{1,0:T(8,128)(2,1)S(1)} collective-permute-done((bf16[16,4096]{1,0:T(8,128)(2,1)S(1)}, bf16[16,4096]{1,0:T(8,128)(2,1)S(1)}, u32[]{:S(2)}, u32[]{:S(2)}) %collective-permute-start.13) | collective-permute-done | bytes 131104 | tf_op jit(solution)/shard_map/ppermute | solution.py:28
  28.9 0.8 %shard_map.104 = (f32[256,128]{1,0:T(8,128)S(1)}, bf16[128,4096]{1,0:T(8,128)(2,1)S(1)}) custom-call(bf16[256,4096]{1,0:T(8,128)(2,1)S(1)} %copy-done, bf16[16,4096]{1,0:T(8,128)(2,1)S(1)} %bitcast.23, bf16[16,4096]{1,0:T(8,128)(2,1)S(1)} %collective-permute-done.1.z1, bf16[16,4096]{1,0:T(8,128)(2,1)S(1)} %collective-permute-done.3.z2, ...), custom_call_target="tpu_custom_call" | custom-call | flops 1073741824 | bytes 4194304 | tf_op jit(solution)/shard_map/pallas_call | solution.py:305
  29.8 1.3 %collective-permute-done.14.other_ref = f32[256,128]{1,0:T(8,128)S(1)} collective-permute-done((f32[256,128]{1,0:T(8,128)S(1)}, f32[256,128]{1,0:T(8,128)S(1)}, u32[]{:S(2)}, u32[]{:S(2)}) %collective-permute-start.14) | collective-permute-done | bytes 131104 | tf_op jit(solution)/shard_map/ppermute | solution.py:23
  31.3 0.7 collective-permute-start.17
  32.0 0.9 %collective-permute-start.18 = (bf16[2,256,128]{2,1,0:T(8,128)(2,1)S(1)}, bf16[2,256,128]{2,1,0:T(8,128)(2,1)S(1)}, u32[]{:S(2)}, u32[]{:S(2)}) collective-permute-start(bf16[2,256,128]{2,1,0:T(8,128)(2,1)S(1)} %get-tuple-element.49), channel_id=1, source_target_pairs={{1,7},{4,8},{5,11},{6,10},{7,1},{8,4},{9,15},{10,6},{11,5},{15,9},... | collective-permute-start | bytes 393224 | tf_op jit(solution)/shard_map/ppermute | solution.py:45
  32.9 5.0 %collective-permute-start.11 = (f32[256,128]{1,0:T(8,128)S(1)}, f32[256,128]{1,0:T(8,128)S(1)}, u32[]{:S(2)}, u32[]{:S(2)}) collective-permute-start(f32[256,128]{1,0:T(8,128)S(1)} %get-tuple-element.43.a_ref), channel_id=1, source_target_pairs={{0,1},{1,0},{2,3},{3,2},{4,5},{5,4},{6,7},{7,6},{8,9},{9,8},{10,11... | collective-permute-start | bytes 393224 | tf_op jit(solution)/shard_map/ppermute | solution.py:23
  38.4 1.8 %collective-permute-start.21 = (bf16[2,256,128]{2,1,0:T(8,128)(2,1)S(1)}, bf16[2,256,128]{2,1,0:T(8,128)(2,1)S(1)}, u32[]{:S(2)}, u32[]{:S(2)}) collective-permute-start(bf16[2,256,128]{2,1,0:T(8,128)(2,1)S(1)} %collective-permute-done.18.r3), channel_id=1, source_target_pairs={{0,1},{1,0},{2,3},{3,2},{4,5},{5,4},{6,7},{7,6},{8,9},{9,8},{10,11... | collective-permute-start | bytes 393224 | tf_op jit(solution)/shard_map/ppermute | solution.py:23
  40.2 1.0 %collective-permute-done.21.s3 = bf16[2,256,128]{2,1,0:T(8,128)(2,1)S(1)} collective-permute-done((bf16[2,256,128]{2,1,0:T(8,128)(2,1)S(1)}, bf16[2,256,128]{2,1,0:T(8,128)(2,1)S(1)}, u32[]{:S(2)}, u32[]{:S(2)}) %collective-permute-start.21) | collective-permute-done | bytes 131104 | tf_op jit(solution)/shard_map/ppermute | solution.py:23
  41.8 2.2 %collective-permute-start.30 = (bf16[16,4096]{1,0:T(8,128)(2,1)S(1)}, bf16[16,4096]{1,0:T(8,128)(2,1)S(1)}, u32[]{:S(2)}, u32[]{:S(2)}) collective-permute-start(bf16[16,4096]{1,0:T(8,128)(2,1)S(1)} %get-tuple-element.64), channel_id=1, source_target_pairs={{0,2},{2,0},{4,6},{6,4},{8,10},{10,8},{12,14},{14,12},{1,3},{3,1},... | collective-permute-start | bytes 393224 | tf_op jit(solution)/shard_map/ppermute | solution.py:28
  44.0 1.9 %collective-permute-start.34 = (bf16[16,4096]{1,0:T(8,128)(2,1)S(1)}, bf16[16,4096]{1,0:T(8,128)(2,1)S(1)}, u32[]{:S(2)}, u32[]{:S(2)}) collective-permute-start(bf16[16,4096]{1,0:T(8,128)(2,1)S(1)} %get-tuple-element.68), channel_id=1, source_target_pairs={{0,2},{2,0},{4,6},{6,4},{8,10},{10,8},{12,14},{14,12},{1,3},{3,1},... | collective-permute-start | bytes 393224 | tf_op jit(solution)/shard_map/ppermute | solution.py:28
  46.1 1.4 %shard_map.107 = (f32[2,128,512]{2,1,0:T(8,128)S(1)}, f32[256,128]{1,0:T(8,128)S(1)}, f32[3,256,128]{2,1,0:T(8,128)S(1)}, bf16[3,256,128]{2,1,0:T(8,128)(2,1)S(1)}) custom-call(s32[2,8,128]{2,1,0:T(8,128)S(1)} %shard_map.102.info_ref, bf16[2,512,128]{2,1,0:T(8,128)(2,1)S(1)} %bitcast.16, bf16[2,512,128]{2,1,0:T(8,128)(2,1)S(1)} %bitcast.18, ...), custom_call_target="tpu_custom_call" | custom-call | flops 1073741824 | bytes 4194304 | tf_op jit(solution)/shard_map/pallas_call | solution.py:305
  47.5 0.7 collective-permute-done.30
  48.2 3.4 %collective-permute-start.31 = (bf16[16,4096]{1,0:T(8,128)(2,1)S(1)}, bf16[16,4096]{1,0:T(8,128)(2,1)S(1)}, u32[]{:S(2)}, u32[]{:S(2)}) collective-permute-start(bf16[16,4096]{1,0:T(8,128)(2,1)S(1)} %add_convert_fusion.2), channel_id=1, source_target_pairs={{0,12},{2,14},{4,8},{6,10},{8,4},{10,6},{12,0},{14,2},{1,13},{3,15... | collective-permute-start | bytes 393224 | tf_op jit(solution)/shard_map/ppermute | solution.py:28
  51.7 4.5 %collective-permute-start.33 = (bf16[16,4096]{1,0:T(8,128)(2,1)S(1)}, bf16[16,4096]{1,0:T(8,128)(2,1)S(1)}, u32[]{:S(2)}, u32[]{:S(2)}) collective-permute-start(bf16[16,4096]{1,0:T(8,128)(2,1)S(1)} %add_convert_fusion.1), channel_id=1, source_target_pairs={{0,8},{2,10},{4,12},{6,14},{8,0},{10,2},{12,4},{14,6},{1,9},{3,11}... | collective-permute-start | bytes 393224 | tf_op jit(solution)/shard_map/ppermute | solution.py:28
  56.2 1.5 %collective-permute-start.35 = (bf16[16,4096]{1,0:T(8,128)(2,1)S(1)}, bf16[16,4096]{1,0:T(8,128)(2,1)S(1)}, u32[]{:S(2)}, u32[]{:S(2)}) collective-permute-start(bf16[16,4096]{1,0:T(8,128)(2,1)S(1)} %add_convert_fusion), channel_id=1, source_target_pairs={{0,4},{2,6},{4,0},{6,2},{8,12},{10,14},{12,8},{14,10},{1,5},{3,7},... | collective-permute-start | bytes 393224 | tf_op jit(solution)/shard_map/ppermute | solution.py:28
  59.1 0.7 collective-permute-start.28
  59.8 1.7 %shard_map.108 = (bf16[256,4096]{1,0:T(8,128)(2,1)}, bf16[256,512]{1,0:T(8,128)(2,1)}) custom-call(bf16[256,128]{1,0:T(8,128)(2,1)S(1)} %get-tuple-element.50.grad_ref, bf16[128,4096]{1,0:T(8,128)(2,1)S(1)} %get-tuple-element.51.weight_ref, f32[2,128,512]{2,1,0:T(8,128)S(1)} %get-tuple-element.56.query_ref), custom_call_target="tpu_custom_call" | custom-call | flops 1073741824 | bytes 4194304 | tf_op jit(solution)/shard_map/pallas_call | solution.py:305
  61.5 2.8 %collective-permute-done.33 = bf16[16,4096]{1,0:T(8,128)(2,1)S(1)} collective-permute-done((bf16[16,4096]{1,0:T(8,128)(2,1)S(1)}, bf16[16,4096]{1,0:T(8,128)(2,1)S(1)}, u32[]{:S(2)}, u32[]{:S(2)}) %collective-permute-start.33) | collective-permute-done | bytes 131104 | tf_op jit(solution)/shard_map/ppermute | solution.py:28
  64.2 3.0 %collective-permute-start.22 = (f32[256,128]{1,0:T(8,128)S(1)}, f32[256,128]{1,0:T(8,128)S(1)}, u32[]{:S(2)}, u32[]{:S(2)}) collective-permute-start(f32[256,128]{1,0:T(8,128)S(1)} %get-tuple-element.59), channel_id=1, source_target_pairs={{0,1},{1,0},{2,3},{3,2},{4,5},{5,4},{6,7},{7,6},{8,9},{9,8},{10,11... | collective-permute-start | bytes 393224 | tf_op jit(solution)/shard_map/ppermute | solution.py:23
  67.8 0.8 %add_bitcast_fusion = f32[4096,16]{0,1:T(8,128)} fusion(bf16[16,4096]{1,0:T(8,128)(2,1)S(1)} %collective-permute-done.36, bf16[16,4096]{1,0:T(8,128)(2,1)S(1)} %collective-permute-done.35, bf16[16,4096]{1,0:T(8,128)(2,1)S(1)} %collective-permute-done.33, f32[16,4096]{1,0:T(8,128)S(1)} %get-tuple-element.62, bf16[16,4096]{1,0:T(8,128)(2,1)S(1)} %collective-permute-done.31), kind=kLoop, calls=%fused_computation | loop fusion | flops 524288 | bytes 1048576 | tf_op jit(solution)/shard_map/transpose | solution.py:401
  69.0 0.7 add_convert_fusion.3
  (70 shorter events, 6.2 us)
Async XLA Ops:
  0.7 7.9 %collective-permute-start = (bf16[16,4096]{1,0:T(8,128)(2,1)}, bf16[16,4096]{1,0:T(8,128)(2,1)S(1)}, u32[]{:S(2)}, u32[]{:S(2)}) collective-permute-start(bf16[16,4096]{1,0:T(8,128)(2,1)} %bitcast.19), channel_id=1, source_target_pairs={{0,2},{2,0},{4,6},{6,4},{8,10},{10,8},{12,14},{14,12},{1,3},{3,1},... | collective-permute-start | bytes 393224 | tf_op jit(solution)/shard_map/ppermute | solution.py:28
  3.7 8.9 %collective-permute-start.1 = (bf16[16,4096]{1,0:T(8,128)(2,1)}, bf16[16,4096]{1,0:T(8,128)(2,1)S(1)}, u32[]{:S(2)}, u32[]{:S(2)}) collective-permute-start(bf16[16,4096]{1,0:T(8,128)(2,1)} %bitcast.20), channel_id=1, source_target_pairs={{0,4},{2,6},{4,0},{6,2},{8,12},{10,14},{12,8},{14,10},{1,5},{3,7},... | collective-permute-start | bytes 393224 | tf_op jit(solution)/shard_map/ppermute | solution.py:28
  5.2 10.1 %collective-permute-start.3 = (bf16[16,4096]{1,0:T(8,128)(2,1)}, bf16[16,4096]{1,0:T(8,128)(2,1)S(1)}, u32[]{:S(2)}, u32[]{:S(2)}) collective-permute-start(bf16[16,4096]{1,0:T(8,128)(2,1)} %bitcast.21), channel_id=1, source_target_pairs={{0,8},{2,10},{4,12},{6,14},{8,0},{10,2},{12,4},{14,6},{1,9},{3,11}... | collective-permute-start | bytes 393224 | tf_op jit(solution)/shard_map/ppermute | solution.py:28
  9.2 6.8 %collective-permute-start.7 = (bf16[256,128]{1,0:T(8,128)(2,1)S(1)}, bf16[256,128]{1,0:T(8,128)(2,1)S(1)}, u32[]{:S(2)}, u32[]{:S(2)}) collective-permute-start(bf16[256,128]{1,0:T(8,128)(2,1)S(1)} %copy-done.2), channel_id=1, source_target_pairs={{1,7},{4,8},{5,11},{6,10},{7,1},{8,4},{9,15},{10,6},{11,5},{15,9},... | collective-permute-start | bytes 196616 | tf_op jit(solution)/shard_map/ppermute | solution.py:45
  9.9 10.4 %collective-permute-start.12 = (bf16[16,4096]{1,0:T(8,128)(2,1)S(1)}, bf16[16,4096]{1,0:T(8,128)(2,1)S(1)}, u32[]{:S(2)}, u32[]{:S(2)}) collective-permute-start(bf16[16,4096]{1,0:T(8,128)(2,1)S(1)} %bitcast.22), channel_id=1, source_target_pairs={{0,12},{2,14},{4,8},{6,10},{8,4},{10,6},{12,0},{14,2},{1,13},{3,15... | collective-permute-start | bytes 393224 | tf_op jit(solution)/shard_map/ppermute | solution.py:28
  12.6 7.8 %collective-permute-start.2 = (bf16[16,4096]{1,0:T(8,128)(2,1)S(1)}, bf16[16,4096]{1,0:T(8,128)(2,1)S(1)}, u32[]{:S(2)}, u32[]{:S(2)}) collective-permute-start(bf16[16,4096]{1,0:T(8,128)(2,1)S(1)} %collective-permute-done.1.z1), channel_id=1, source_target_pairs={{0,2},{2,0},{4,6},{6,4},{8,10},{10,8},{12,14},{14,12},{1,3},{3,1},... | collective-permute-start | bytes 393224 | tf_op jit(solution)/shard_map/ppermute | solution.py:28
  14.1 5.7 %collective-permute-start.5 = (bf16[256,128]{1,0:T(8,128)(2,1)S(1)}, bf16[256,128]{1,0:T(8,128)(2,1)S(1)}, u32[]{:S(2)}, u32[]{:S(2)}) collective-permute-start(bf16[256,128]{1,0:T(8,128)(2,1)S(1)} %copy-done.2), channel_id=1, source_target_pairs={{0,4},{1,3},{2,6},{3,1},{4,0},{5,7},{6,2},{7,5},{8,12},{9,11},{10,... | collective-permute-start | bytes 196616 | tf_op jit(solution)/shard_map/ppermute | solution.py:45
  15.3 4.5 %collective-permute-start.6 = (bf16[256,128]{1,0:T(8,128)(2,1)S(1)}, bf16[256,128]{1,0:T(8,128)(2,1)S(1)}, u32[]{:S(2)}, u32[]{:S(2)}) collective-permute-start(bf16[256,128]{1,0:T(8,128)(2,1)S(1)} %copy-done.2), channel_id=1, source_target_pairs={{2,8},{3,5},{5,3},{6,12},{7,9},{8,2},{9,7},{11,13},{12,6},{13,11},... | collective-permute-start | bytes 196616 | tf_op jit(solution)/shard_map/ppermute | solution.py:45
  16.0 9.5 %collective-permute-start.4 = (bf16[16,4096]{1,0:T(8,128)(2,1)S(1)}, bf16[16,4096]{1,0:T(8,128)(2,1)S(1)}, u32[]{:S(2)}, u32[]{:S(2)}) collective-permute-start(bf16[16,4096]{1,0:T(8,128)(2,1)S(1)} %collective-permute-done.3.z2), channel_id=1, source_target_pairs={{0,2},{2,0},{4,6},{6,4},{8,10},{10,8},{12,14},{14,12},{1,3},{3,1},... | collective-permute-start | bytes 393224 | tf_op jit(solution)/shard_map/ppermute | solution.py:28
  19.8 5.7 %collective-permute-start.10 = (bf16[256,128]{1,0:T(8,128)(2,1)S(1)}, bf16[256,128]{1,0:T(8,128)(2,1)S(1)}, u32[]{:S(2)}, u32[]{:S(2)}) collective-permute-start(bf16[256,128]{1,0:T(8,128)(2,1)S(1)} %collective-permute-done.7.r3), channel_id=1, source_target_pairs={{0,1},{1,0},{2,3},{3,2},{4,5},{5,4},{6,7},{7,6},{8,9},{9,8},{10,11... | collective-permute-start | bytes 196616 | tf_op jit(solution)/shard_map/ppermute | solution.py:23
  19.8 5.7 %collective-permute-start.8 = (bf16[256,128]{1,0:T(8,128)(2,1)S(1)}, bf16[256,128]{1,0:T(8,128)(2,1)S(1)}, u32[]{:S(2)}, u32[]{:S(2)}) collective-permute-start(bf16[256,128]{1,0:T(8,128)(2,1)S(1)} %collective-permute-done.5.r1), channel_id=1, source_target_pairs={{0,1},{1,0},{2,3},{3,2},{4,5},{5,4},{6,7},{7,6},{8,9},{9,8},{10,11... | collective-permute-start | bytes 196616 | tf_op jit(solution)/shard_map/ppermute | solution.py:23
  20.3 5.2 %collective-permute-start.9 = (bf16[256,128]{1,0:T(8,128)(2,1)S(1)}, bf16[256,128]{1,0:T(8,128)(2,1)S(1)}, u32[]{:S(2)}, u32[]{:S(2)}) collective-permute-start(bf16[256,128]{1,0:T(8,128)(2,1)S(1)} %collective-permute-done.6.r2), channel_id=1, source_target_pairs={{0,1},{1,0},{2,3},{3,2},{4,5},{5,4},{6,7},{7,6},{8,9},{9,8},{10,11... | collective-permute-start | bytes 196616 | tf_op jit(solution)/shard_map/ppermute | solution.py:23
  20.4 8.6 %collective-permute-start.13 = (bf16[16,4096]{1,0:T(8,128)(2,1)S(1)}, bf16[16,4096]{1,0:T(8,128)(2,1)S(1)}, u32[]{:S(2)}, u32[]{:S(2)}) collective-permute-start(bf16[16,4096]{1,0:T(8,128)(2,1)S(1)} %collective-permute-done.12.z3), channel_id=1, source_target_pairs={{0,2},{2,0},{4,6},{6,4},{8,10},{10,8},{12,14},{14,12},{1,3},{3,1},... | collective-permute-start | bytes 393224 | tf_op jit(solution)/shard_map/ppermute | solution.py:28
  27.1 4.1 %collective-permute-start.15 = (bf16[3,256,128]{2,1,0:T(8,128)(2,1)S(1)}, bf16[3,256,128]{2,1,0:T(8,128)(2,1)S(1)}, u32[]{:S(2)}, u32[]{:S(2)}) collective-permute-start(bf16[3,256,128]{2,1,0:T(8,128)(2,1)S(1)} %get-tuple-element.46), channel_id=1, source_target_pairs={{0,1},{1,0},{2,3},{3,2},{4,5},{5,4},{6,7},{7,6},{8,9},{9,8},{10,11... | collective-permute-start | bytes 589832 | tf_op jit(solution)/shard_map/ppermute | solution.py:23
  31.2 6.6 %collective-permute-start.16 = (bf16[2,256,128]{2,1,0:T(8,128)(2,1)S(1)}, bf16[2,256,128]{2,1,0:T(8,128)(2,1)S(1)}, u32[]{:S(2)}, u32[]{:S(2)}) collective-permute-start(bf16[2,256,128]{2,1,0:T(8,128)(2,1)S(1)} %get-tuple-element.47), channel_id=1, source_target_pairs={{0,4},{1,3},{2,6},{3,1},{4,0},{5,7},{6,2},{7,5},{8,12},{9,11},{10,... | collective-permute-start | bytes 393224 | tf_op jit(solution)/shard_map/ppermute | solution.py:45
  31.3 6.6 %collective-permute-start.17 = (bf16[2,256,128]{2,1,0:T(8,128)(2,1)S(1)}, bf16[2,256,128]{2,1,0:T(8,128)(2,1)S(1)}, u32[]{:S(2)}, u32[]{:S(2)}) collective-permute-start(bf16[2,256,128]{2,1,0:T(8,128)(2,1)S(1)} %get-tuple-element.48), channel_id=1, source_target_pairs={{2,8},{3,5},{5,3},{6,12},{7,9},{8,2},{9,7},{11,13},{12,6},{13,11},... | collective-permute-start | bytes 393224 | tf_op jit(solution)/shard_map/ppermute | solution.py:45
  32.0 6.4 %collective-permute-start.18 = (bf16[2,256,128]{2,1,0:T(8,128)(2,1)S(1)}, bf16[2,256,128]{2,1,0:T(8,128)(2,1)S(1)}, u32[]{:S(2)}, u32[]{:S(2)}) collective-permute-start(bf16[2,256,128]{2,1,0:T(8,128)(2,1)S(1)} %get-tuple-element.49), channel_id=1, source_target_pairs={{1,7},{4,8},{5,11},{6,10},{7,1},{8,4},{9,15},{10,6},{11,5},{15,9},... | collective-permute-start | bytes 393224 | tf_op jit(solution)/shard_map/ppermute | solution.py:45
  32.9 7.3 %collective-permute-start.11 = (f32[256,128]{1,0:T(8,128)S(1)}, f32[256,128]{1,0:T(8,128)S(1)}, u32[]{:S(2)}, u32[]{:S(2)}) collective-permute-start(f32[256,128]{1,0:T(8,128)S(1)} %get-tuple-element.43.a_ref), channel_id=1, source_target_pairs={{0,1},{1,0},{2,3},{3,2},{4,5},{5,4},{6,7},{7,6},{8,9},{9,8},{10,11... | collective-permute-start | bytes 393224 | tf_op jit(solution)/shard_map/ppermute | solution.py:23
  37.8 2.3 %collective-permute-start.19 = (bf16[2,256,128]{2,1,0:T(8,128)(2,1)S(1)}, bf16[2,256,128]{2,1,0:T(8,128)(2,1)S(1)}, u32[]{:S(2)}, u32[]{:S(2)}) collective-permute-start(bf16[2,256,128]{2,1,0:T(8,128)(2,1)S(1)} %collective-permute-done.16.r1), channel_id=1, source_target_pairs={{0,1},{1,0},{2,3},{3,2},{4,5},{5,4},{6,7},{7,6},{8,9},{9,8},{10,11... | collective-permute-start | bytes 393224 | tf_op jit(solution)/shard_map/ppermute | solution.py:23
  38.4 2.8 %collective-permute-start.21 = (bf16[2,256,128]{2,1,0:T(8,128)(2,1)S(1)}, bf16[2,256,128]{2,1,0:T(8,128)(2,1)S(1)}, u32[]{:S(2)}, u32[]{:S(2)}) collective-permute-start(bf16[2,256,128]{2,1,0:T(8,128)(2,1)S(1)} %collective-permute-done.18.r3), channel_id=1, source_target_pairs={{0,1},{1,0},{2,3},{3,2},{4,5},{5,4},{6,7},{7,6},{8,9},{9,8},{10,11... | collective-permute-start | bytes 393224 | tf_op jit(solution)/shard_map/ppermute | solution.py:23
  41.8 6.4 %collective-permute-start.30 = (bf16[16,4096]{1,0:T(8,128)(2,1)S(1)}, bf16[16,4096]{1,0:T(8,128)(2,1)S(1)}, u32[]{:S(2)}, u32[]{:S(2)}) collective-permute-start(bf16[16,4096]{1,0:T(8,128)(2,1)S(1)} %get-tuple-element.64), channel_id=1, source_target_pairs={{0,2},{2,0},{4,6},{6,4},{8,10},{10,8},{12,14},{14,12},{1,3},{3,1},... | collective-permute-start | bytes 393224 | tf_op jit(solution)/shard_map/ppermute | solution.py:28
  44.0 7.7 %collective-permute-start.32 = (bf16[16,4096]{1,0:T(8,128)(2,1)S(1)}, bf16[16,4096]{1,0:T(8,128)(2,1)S(1)}, u32[]{:S(2)}, u32[]{:S(2)}) collective-permute-start(bf16[16,4096]{1,0:T(8,128)(2,1)S(1)} %get-tuple-element.66), channel_id=1, source_target_pairs={{0,2},{2,0},{4,6},{6,4},{8,10},{10,8},{12,14},{14,12},{1,3},{3,1},... | collective-permute-start | bytes 393224 | tf_op jit(solution)/shard_map/ppermute | solution.py:28
  44.0 12.1 %collective-permute-start.34 = (bf16[16,4096]{1,0:T(8,128)(2,1)S(1)}, bf16[16,4096]{1,0:T(8,128)(2,1)S(1)}, u32[]{:S(2)}, u32[]{:S(2)}) collective-permute-start(bf16[16,4096]{1,0:T(8,128)(2,1)S(1)} %get-tuple-element.68), channel_id=1, source_target_pairs={{0,2},{2,0},{4,6},{6,4},{8,10},{10,8},{12,14},{14,12},{1,3},{3,1},... | collective-permute-start | bytes 393224 | tf_op jit(solution)/shard_map/ppermute | solution.py:28
  46.0 12.4 %collective-permute-start.36 = (bf16[16,4096]{1,0:T(8,128)(2,1)S(1)}, bf16[16,4096]{1,0:T(8,128)(2,1)S(1)}, u32[]{:S(2)}, u32[]{:S(2)}) collective-permute-start(bf16[16,4096]{1,0:T(8,128)(2,1)S(1)} %get-tuple-element.69), channel_id=1, source_target_pairs={{0,2},{2,0},{4,6},{6,4},{8,10},{10,8},{12,14},{14,12},{1,3},{3,1},... | collective-permute-start | bytes 393224 | tf_op jit(solution)/shard_map/ppermute | solution.py:28
  47.5 10.3 %collective-permute-start.23 = (bf16[3,256,128]{2,1,0:T(8,128)(2,1)S(1)}, bf16[3,256,128]{2,1,0:T(8,128)(2,1)S(1)}, u32[]{:S(2)}, u32[]{:S(2)}) collective-permute-start(bf16[3,256,128]{2,1,0:T(8,128)(2,1)S(1)} %get-tuple-element.61), channel_id=1, source_target_pairs={{0,1},{1,0},{2,3},{3,2},{4,5},{5,4},{6,7},{7,6},{8,9},{9,8},{10,11... | collective-permute-start | bytes 589832 | tf_op jit(solution)/shard_map/ppermute | solution.py:23
  48.2 10.8 %collective-permute-start.31 = (bf16[16,4096]{1,0:T(8,128)(2,1)S(1)}, bf16[16,4096]{1,0:T(8,128)(2,1)S(1)}, u32[]{:S(2)}, u32[]{:S(2)}) collective-permute-start(bf16[16,4096]{1,0:T(8,128)(2,1)S(1)} %add_convert_fusion.2), channel_id=1, source_target_pairs={{0,12},{2,14},{4,8},{6,10},{8,4},{10,6},{12,0},{14,2},{1,13},{3,15... | collective-permute-start | bytes 393224 | tf_op jit(solution)/shard_map/ppermute | solution.py:28
  51.7 12.6 %collective-permute-start.33 = (bf16[16,4096]{1,0:T(8,128)(2,1)S(1)}, bf16[16,4096]{1,0:T(8,128)(2,1)S(1)}, u32[]{:S(2)}, u32[]{:S(2)}) collective-permute-start(bf16[16,4096]{1,0:T(8,128)(2,1)S(1)} %add_convert_fusion.1), channel_id=1, source_target_pairs={{0,8},{2,10},{4,12},{6,14},{8,0},{10,2},{12,4},{14,6},{1,9},{3,11}... | collective-permute-start | bytes 393224 | tf_op jit(solution)/shard_map/ppermute | solution.py:28
  56.2 11.6 %collective-permute-start.35 = (bf16[16,4096]{1,0:T(8,128)(2,1)S(1)}, bf16[16,4096]{1,0:T(8,128)(2,1)S(1)}, u32[]{:S(2)}, u32[]{:S(2)}) collective-permute-start(bf16[16,4096]{1,0:T(8,128)(2,1)S(1)} %add_convert_fusion), channel_id=1, source_target_pairs={{0,4},{2,6},{4,0},{6,2},{8,12},{10,14},{12,8},{14,10},{1,5},{3,7},... | collective-permute-start | bytes 393224 | tf_op jit(solution)/shard_map/ppermute | solution.py:28
  57.8 9.4 %collective-permute-start.24 = (bf16[256,128]{1,0:T(8,128)(2,1)S(1)}, bf16[256,128]{1,0:T(8,128)(2,1)S(1)}, u32[]{:S(2)}, u32[]{:S(2)}) collective-permute-start(bf16[256,128]{1,0:T(8,128)(2,1)S(1)} %get-tuple-element.70), channel_id=1, source_target_pairs={{0,4},{1,3},{2,6},{3,1},{4,0},{5,7},{6,2},{7,5},{8,12},{9,11},{10,... | collective-permute-start | bytes 196616 | tf_op jit(solution)/shard_map/ppermute | solution.py:45
  58.4 8.9 %collective-permute-start.26 = (bf16[256,128]{1,0:T(8,128)(2,1)S(1)}, bf16[256,128]{1,0:T(8,128)(2,1)S(1)}, u32[]{:S(2)}, u32[]{:S(2)}) collective-permute-start(bf16[256,128]{1,0:T(8,128)(2,1)S(1)} %get-tuple-element.72), channel_id=1, source_target_pairs={{2,8},{3,5},{5,3},{6,12},{7,9},{8,2},{9,7},{11,13},{12,6},{13,11},... | collective-permute-start | bytes 196616 | tf_op jit(solution)/shard_map/ppermute | solution.py:45
  59.1 8.6 %collective-permute-start.28 = (bf16[256,128]{1,0:T(8,128)(2,1)S(1)}, bf16[256,128]{1,0:T(8,128)(2,1)S(1)}, u32[]{:S(2)}, u32[]{:S(2)}) collective-permute-start(bf16[256,128]{1,0:T(8,128)(2,1)S(1)} %get-tuple-element.71), channel_id=1, source_target_pairs={{1,7},{4,8},{5,11},{6,10},{7,1},{8,4},{9,15},{10,6},{11,5},{15,9},... | collective-permute-start | bytes 196616 | tf_op jit(solution)/shard_map/ppermute | solution.py:45
  64.2 4.4 %collective-permute-start.22 = (f32[256,128]{1,0:T(8,128)S(1)}, f32[256,128]{1,0:T(8,128)S(1)}, u32[]{:S(2)}, u32[]{:S(2)}) collective-permute-start(f32[256,128]{1,0:T(8,128)S(1)} %get-tuple-element.59), channel_id=1, source_target_pairs={{0,1},{1,0},{2,3},{3,2},{4,5},{5,4},{6,7},{7,6},{8,9},{9,8},{10,11... | collective-permute-start | bytes 393224 | tf_op jit(solution)/shard_map/ppermute | solution.py:23
  (10 other events, 70.2 us)
